TPU v7x, 32 devices: a whole 2x2x4 slice. The times are simulated.
32 devices in a mesh: pair: 4 (over y, x), slab: 8 (over z, core).
Axes of the slice: x: 2, y: 2, z: 4, core: 2. Of those that a mesh axis runs over, the one named last changes fastest.
Arguments:
- pair_density: bfloat16 [12288, 49152], P('pair', 'slab'), may hold values from -6 to 6
- subspace: bfloat16 [49152, 512], P('slab'), may hold values from -0.02734375 to 0.02734375
- band_valence: int32 [12288], P('pair'), may hold values from 0 to 510, as said below
- band_conduction: int32 [12288], P('pair'), may hold values from 1 to 511, as said below
- occupied: int32 [512], replicated, may hold values from 0 to 1, as said below
- energies: float32 [512], replicated, may hold values from -1 to 1
Outputs:
- chi_panel: float32 [512, 49152], P('pair', 'slab')
- subspace_chi: float32 [512, 512], P('slab', 'pair')
Inputs may be any that keep to these rules, and one draw needn't show every extreme that they name: Exactly half of the 512 bands are occupied. `band_valence`: every entry names a band that occupied marks as occupied. `band_conduction`: every entry names a band that occupied marks as unoccupied.
All inputs are finite; a program needn't handle non-finite values.
Results may differ from a plain program's by a relative error of at most 0.0024.
Values sent between devices are 32-bit elements; how exact they have to be, the bound alone decides.
No kernel may reach another device: no remote copies, remote signals or barrier semaphores. Data moves between devices by JAX's collectives and lax.ppermute only.
A program may use at most 128 MiB of HBM per device.

v0:
```python
import math

import jax
import jax.numpy as jnp
from jax import lax
from jax.sharding import PartitionSpec as P


def lookup(indices, table):
    levels = jnp.arange(table.shape[0], dtype=jnp.int32)
    one_hot = (indices[:, None] == levels[None, :]).astype(jnp.float32)
    return jnp.dot(one_hot, table, precision=lax.Precision.HIGHEST)


def body(pair_density, subspace, band_valence, band_conduction, occupied, energies):
    partial_value = jnp.dot(pair_density, subspace, preferred_element_type=jnp.float32)
    coefficient = lax.psum(partial_value, "slab")
    total_pairs = pair_density.shape[0] * lax.axis_size("pair")
    band_table = jnp.stack([energies, occupied.astype(jnp.float32)], axis=1)
    valence_rows = lookup(band_valence, band_table)
    conduction_rows = lookup(band_conduction, band_table)
    scale = 1.0 / math.sqrt(total_pairs)
    pair_weight = (
        -2.0
        * valence_rows[:, 1]
        * (1.0 - conduction_rows[:, 1])
        / (jnp.abs(conduction_rows[:, 0] - valence_rows[:, 0]) + 0.5)
        * scale
    )
    weighted = (coefficient * pair_weight[:, None]).astype(jnp.bfloat16)
    chi_panel = lax.psum_scatter(
        lax.dot_general(
            weighted, pair_density, (((0,), (0,)), ((), ())), preferred_element_type=jnp.float32
        ),
        "pair",
        scatter_dimension=0,
        tiled=True,
    )
    slab_rows = coefficient.shape[1] // lax.axis_size("slab")
    own_block = lax.dynamic_slice_in_dim(
        coefficient, lax.axis_index("slab") * slab_rows, slab_rows, 1
    )
    local_sum = lax.dot_general(
        own_block,
        weighted.astype(jnp.float32),
        (((0,), (0,)), ((), ())),
        precision=lax.Precision.HIGHEST,
    )
    subspace_chi = lax.psum_scatter(local_sum, "pair", scatter_dimension=1, tiled=True)
    return (chi_panel, subspace_chi)


def solution(mesh):
    return jax.shard_map(
        body,
        mesh=mesh,
        in_specs=(P("pair", "slab"), P("slab", None), P("pair"), P("pair"), P(), P()),
        out_specs=(P("pair", "slab"), P("slab", "pair")),
        check_vma=False,
    )
```

profile of v0, /device:TPU:0, one launch (start us, length us, event | category | flops | bytes accessed | tf_op | source)
XLA Modules:
  0.0 336.4 jit_solution(6650642593318806425)
XLA Ops:
  7.2 0.0 all-reduce.2.cloned.1.call-start
  7.2 26.8 %fusion.14 = f32[3072,512]{1,0:T(8,128)} fusion(bf16[3072,6144]{1,0:T(8,128)(2,1)} %param.6, bf16[6144,512]{1,0:T(8,128)(2,1)} %param.7), kind=kOutput, calls=%fused_computation.21 | convolution fusion | flops 19327352832 | bytes 50331648 | tf_op jit(solution)/shard_map/dot_general | solution.py:16
  34.0 0.0 copy-start
  34.0 0.0 copy-start.1
  34.0 0.0 copy-start.3
  34.0 0.0 copy-start.2
  34.0 0.0 all-reduce.2.cloned.1.call-update
  34.0 0.0 reduce-scatter.5.cloned.1.call-start
  34.1 0.6 copy-done
  34.6 0.0 copy-done.1
  34.7 0.0 copy-done.3
  34.7 3.3 fusion.1
  37.9 0.0 copy-done.2
  37.9 3.3 fusion
  41.2 0.1 fusion.9
  41.3 131.7 %all-reduce.2.cloned.1.call-done = f32[3072,512]{1,0:T(8,128)} async-done(((f32[3072,512]{1,0:T(8,128)}), f32[3072,512]{1,0:T(8,128)}) %all-reduce.2.cloned.1.call-update) | async-done | bytes 6291472 | tf_op jit(solution)/shard_map/psum | solution.py:17
  173.0 6.2 %fusion.4 = f32[64,512]{1,0:T(8,128)} fusion(f32[3072,512]{1,0:T(8,128)} %all-reduce.2.cloned.1.call-done, s32[]{:T(128)S(6)} %select_n.3, f32[3072]{0:T(1024)S(1)} %bitcast.6), kind=kOutput, calls=%fused_computation.7 | convolution fusion | flops 1211105280 | bytes 8007684 | tf_op jit(solution)/shard_map/dot_general | solution.py:43
  179.2 0.0 reduce-scatter.5.cloned.1.call-update
  179.3 0.2 reduce-scatter.3.cloned.1.call-start
  179.5 29.4 %fusion.13 = f32[512,6144]{1,0:T(8,128)} fusion(bf16[3072,6144]{1,0:T(8,128)(2,1)} %param.6, f32[3072,512]{1,0:T(8,128)} %all-reduce.2.cloned.1.call-done, f32[3072]{0:T(1024)S(1)} %bitcast.7), kind=kOutput, calls=%fused_computation.20 | convolution fusion | flops 19330498560 | bytes 56635392 | tf_op jit(solution)/shard_map/dot_general | solution.py:32
  208.9 0.0 reduce-scatter.3.cloned.1.call-update
  208.9 0.0 reduce-scatter.5.cloned.1.call-done
  208.9 120.9 %reduce-scatter.3.cloned.1.call-done = f32[128,6144]{1,0:T(8,128)} async-done(((f32[512,6144]{1,0:T(8,128)}), f32[128,6144]{1,0:T(8,128)}) %reduce-scatter.3.cloned.1.call-update) | async-done | bytes 3145744 | tf_op jit(solution)/shard_map/reduce_scatter | solution.py:31
  (1 shorter events, 0.0 us)
Async XLA Ops:
  7.2 165.8 %all-reduce.2.cloned.1.call-start = ((), (), s32[]{:S(2)}) async-start(), calls=%async_computation.2 | async-start | bytes 12582912 | tf_op jit(solution)/shard_map/psum | solution.py:17
  34.0 0.7 copy-start
  34.0 0.7 copy-start.1
  34.0 0.7 copy-start.3
  34.0 4.0 %copy-start.2 = (s32[3072]{0:T(1024)S(1)}, s32[3072]{0:T(1024)}, u32[]{:S(2)}) copy-start(s32[3072]{0:T(1024)} %param.8) | copy-start | bytes 36868
  34.0 174.9 %reduce-scatter.5.cloned.1.call-start = ((), (), s32[]{:S(2)}) async-start(), calls=%async_computation.4 | async-start | bytes 163840 | tf_op jit(solution)/shard_map/reduce_scatter | solution.py:49
  179.3 150.6 %reduce-scatter.3.cloned.1.call-start = ((), (), s32[]{:S(2)}) async-start(), calls=%async_computation.3 | async-start | bytes 15728640 | tf_op jit(solution)/shard_map/reduce_scatter | solution.py:31
Sparse Core Ops, SparseCore 0:
  34.1 138.8 all-reduce.1
  179.4 23.9 reduce-scatter.4
  209.0 120.7 reduce-scatter.2
where the time goes:
time: 337 us; the launch traced here: 336 us
  waiting for transfers between devices  253 us (75%)
  matrix products  68.9 us (20%)
  between operations  13.8 us (4%)
    psum x1, waiting for transfers between devices, body(): coefficient = lax.psum(partial_value, 'slab')  132 us
    reduce_scatter x1, waiting for transfers between devices, body(): lax.psum_scatter(lax.dot_general(weighted, pair_density, (((0,), (0,)), (...  121 us
    dot_general x1, matrix products, body(): lax.dot_general(weighted, pair_density, (((0,), (0,)), ((), ())), preferr...  29.4 us
    dot_general x1, matrix products, body(): jnp.dot(pair_density, subspace, preferred_element_type=jnp.float32)  26.8 us
  transfers between devices with their start and end apart: 3, of which 2 were waited for; matrix products, arithmetic and copies ran while one was open for 11% of the time, Pallas kernels for 0%

commit v1 on v0

v1 whole, which is shorter than its diff:
```python
import math

import jax
import jax.numpy as jnp
from jax import lax
from jax.experimental import pallas as pl
from jax.experimental.pallas import tpu as pltpu
from jax.sharding import PartitionSpec as P

VMEM = 18 << 20
COST = pl.CostEstimate(flops=1000, bytes_accessed=1000, transcendentals=0)


BLOCK = 384
WIDE = 768
CUTS = (1, 1, 1, 1)
TURNS = (2, 2, 2)
STEPS = 2


def split(extent, most):
    most = min(extent, most)
    return [(a, a + most) for a in range(0, extent, most)]


def split_bf16(value, pieces):
    out = []
    for _ in range(pieces):
        top = lax.reduce_precision(value, 8, 7)
        out.append(top.astype(jnp.bfloat16))
        value = value - top
    return out


def pair_weights(band_valence, band_conduction, occupied, energies, total_pairs):
    table = jnp.stack(split_bf16(energies, 3) + [occupied.astype(jnp.bfloat16)])
    levels = jnp.arange(energies.shape[0], dtype=jnp.int32)

    def lookup(indices):
        one_hot = (levels[:, None] == indices[None, :]).astype(jnp.bfloat16)
        rows = jnp.dot(table, one_hot, preferred_element_type=jnp.float32)
        return rows[0] + rows[1] + rows[2], rows[3]

    energy_low, filled_low = lookup(band_valence)
    energy_high, filled_high = lookup(band_conduction)
    scale = 1.0 / math.sqrt(total_pairs)
    return -2.0 * filled_low * (1.0 - filled_high) / (jnp.abs(energy_high - energy_low) + 0.5) * scale


def fitting(extent, most):
    for unit in (128, 1):
        for size in range(most // unit * unit, 0, -unit):
            if extent % size == 0:
                return size


def project(where, subspace, rho, start, stop, groups):
    depth, vectors = subspace.shape
    block = fitting(math.gcd(start, stop) if start else stop, BLOCK)

    def kernel(where_ref, s_ref, rho_ref, *refs):
        outs, found = refs[:-1], refs[-1]
        found[...] = jnp.dot(rho_ref[...], s_ref[...], preferred_element_type=jnp.float32).T
        first = where_ref[0] == 0

        def rows(part):
            got = [found[pl.ds(pl.multiple_of(where_ref[1 + n] + a, 8), b - a), :] for n, a, b in part]
            return jnp.concatenate(got) if len(got) > 1 else got[0]

        for at, (upper, lower) in enumerate(groups):
            upper, lower = rows(upper), rows(lower)
            outs[2 * at][...] = jnp.where(first, upper, lower)
            outs[2 * at + 1][...] = jnp.where(first, lower, upper)

    halves = [sum(b - a for _, a, b in group[0]) for group in groups for _ in (0, 1)]
    return pl.pallas_call(
        kernel,
        out_shape=[jax.ShapeDtypeStruct((h, stop - start), jnp.float32) for h in halves],
        grid_spec=pltpu.PrefetchScalarGridSpec(
            num_scalar_prefetch=1,
            grid=((stop - start) // block,),
            in_specs=[
                pl.BlockSpec(memory_space=pltpu.VMEM),
                pl.BlockSpec((block, depth), lambda i, at: (start // block + i, 0)),
            ],
            out_specs=[pl.BlockSpec((h, block), lambda i, at: (0, i)) for h in halves],
            scratch_shapes=[pltpu.VMEM((vectors, block), jnp.float32)],
        ),
        compiler_params=pltpu.CompilerParams(vmem_limit_bytes=VMEM),
        cost_estimate=COST,
    )(where, subspace, rho)


def panel(weighted, rho, step, steps, outputs, adds):
    rows, pairs = weighted.shape
    piece = rho.shape[1] // 2 // steps
    block = fitting(piece, WIDE)
    turns = piece // block

    def kernel(w_ref, rho_ref, *refs):
        more, outs = refs[: len(adds)], refs[len(adds) :]
        side, turn = pl.program_id(0), pl.program_id(1)
        found = jnp.dot(w_ref[...], rho_ref[...], preferred_element_type=jnp.float32)
        for s in (0, 1):

            @pl.when(side == s)
            def _():
                for at, ((a, b), sides) in enumerate(outputs):
                    if s not in sides:
                        continue
                    value = found[a:b]
                    for (output, its_side, _, _), ref in zip(adds, more):
                        if output == at and its_side == s:
                            value = value + ref[...]
                    outs[at][...] = value

    def of_output(sides):
        if len(sides) == 2:
            return lambda s, t: (0, s * turns + t)
        return (lambda s, t: (0, t + s * (turns - 1 - t))) if sides[0] == 0 else (lambda s, t: (0, s * t))

    def of_add(side, r):
        return (lambda s, t: (r, t + s * (turns - 1 - t))) if side == 0 else (lambda s, t: (r, s * t))

    return pl.pallas_call(
        kernel,
        out_shape=[
            jax.ShapeDtypeStruct((b - a, piece * len(sides)), jnp.float32) for (a, b), sides in outputs
        ],
        grid=(2, turns),
        in_specs=[
            pl.BlockSpec((rows, pairs), lambda s, t: (0, 0)),
            pl.BlockSpec((pairs, block), lambda s, t: (0, (step + s * steps) * turns + t)),
        ]
        + [
            pl.BlockSpec((outputs[at][0][1] - outputs[at][0][0], block), of_add(side, r))
            for at, side, _, r in adds
        ],
        out_specs=[pl.BlockSpec((b - a, block), of_output(sides)) for (a, b), sides in outputs],
        compiler_params=pltpu.CompilerParams(vmem_limit_bytes=VMEM),
        cost_estimate=COST,
    )(weighted, rho, *[a for _, _, a, _ in adds])


def assemble(chi, own, step, steps, low, high):
    rows, width = own.shape[0], own.shape[1] // 2 * 2 * steps
    piece = width // 2 // steps
    half = rows // 2
    arrived = low + high

    def kernel(*refs):
        own_ref, more, out_ref = refs[-2 - len(arrived)], refs[-1 - len(arrived) : -1], refs[-1]
        for part, got in ((slice(0, half), more[: len(low)]), (slice(half, rows), more[len(low) :])):
            value = own_ref[part, :]
            for ref in got:
                value = value + ref[...]
            out_ref[part, :] = value

    before = [] if chi is None else [chi]
    return pl.pallas_call(
        kernel,
        out_shape=jax.ShapeDtypeStruct((rows, width), own.dtype),
        grid=(2,),
        in_specs=[pl.BlockSpec(memory_space=pl.ANY)] * len(before)
        + [pl.BlockSpec((rows, piece), lambda s: (0, s))]
        + [pl.BlockSpec((half, piece), lambda s: (0, s))] * len(arrived),
        out_specs=pl.BlockSpec((rows, piece), lambda s: (0, step + s * steps)),
        input_output_aliases={0: 0} if before else {},
        compiler_params=pltpu.CompilerParams(vmem_limit_bytes=VMEM),
        cost_estimate=COST,
    )(*before, own, *arrived)


def body(rho, subspace, band_valence, band_conduction, occupied, energies):
    q, slabs = lax.axis_size("pair"), lax.axis_size("slab")
    pairs, width = rho.shape
    vectors = subspace.shape[1]
    rows = vectors // q
    inner = 2 if q % 2 == 0 else 1
    outer = q // inner
    chips = slabs // 2
    me, slab = lax.axis_index("pair"), lax.axis_index("slab")
    my_outer, my_inner = me // inner, me % inner
    core, chip = slab % 2, slab // 2
    last = []

    def run(work, *operands):
        n = len(operands)
        out = work(*lax.optimization_barrier((*operands, *last))[:n])
        last[:] = jax.tree.leaves(out)[:1]
        return out

    def target(offset):
        return (my_outer + offset[0]) % outer * inner + (my_inner + offset[1]) % inner

    def send_pair(x, offset):
        perm = [
            (s, (s // inner + offset[0]) % outer * inner + (s % inner + offset[1]) % inner)
            for s in range(q)
        ]
        return lax.ppermute(x, "pair", perm)

    def send_core(x):
        return lax.ppermute(x, "slab", [(s, s ^ 1) for s in range(slabs)])

    middle = chips // 2

    class Piece:
        def __init__(self, keep, send):
            self.total, self.hop, self.value = keep, -1, None
            self.got = send

        def receive(self):
            total, got, hop = self.total, self.got, self.hop
            if hop < 0:
                self.got = send_core(got)
            elif hop == 0:
                self.total = run(jnp.add, total, got)
            elif hop <= middle:
                here = (chip == hop) | (chip == chips - 1 - hop)
                if hop == middle:
                    here = (chip == middle - 1) | (chip == middle)
                self.total = run(lambda a, b: jnp.where(here, a + b, a), total, got)
            elif hop < 2 * middle:
                out = 2 * middle - hop
                here = (chip == out - 1) | (chip == chips - out)
                self.total = run(lambda a, b: jnp.where(here, b, a), total, got)
            else:
                self.value = (total, got)
            self.hop += 1

    def exchange(x, pairs, both=True):
        moves = pairs + [(b, a) for a, b in pairs] if both else pairs
        perm = [(2 * a + c, 2 * b + c) for a, b in moves for c in (0, 1)]
        if both:
            busy = {c for pair in pairs for c in pair}
            perm += [(2 * a + c, 2 * a + 1 - c) for a in range(chips) if a not in busy for c in (0, 1)]
        return lax.ppermute(x, "slab", perm)

    def advance(*groups):
        moving = [piece for group in groups for piece in group if piece.value is None]
        for piece in moving:
            piece.receive()
        for piece in moving:
            if piece.hop == 2 * middle and piece.value is None:
                piece.got = send_core(piece.total)
        for t in range(middle - 1, 0, -1):
            ins = [p for p in moving if p.hop == t]
            outs = [p for p in moving if p.hop == 2 * middle - t]
            pairs = [(t - 1, t), (chips - t, chips - 1 - t)]
            for back in outs:
                mate = next((p for p in ins if p.total.shape == back.total.shape), None)
                if mate is not None:
                    ins.remove(mate)
                    sender = (chip == t - 1) | (chip == chips - t)
                    both = run(lambda a, b: jnp.where(sender, a, b), mate.total, back.total)
                    back.got = mate.got = exchange(both, pairs)
                elif ins or any(p.hop < t for p in moving):
                    back.got = exchange(back.total, [(b, a) for a, b in pairs], False)
                else:
                    back.got = exchange(back.total, pairs)
            for piece in ins:
                piece.got = exchange(piece.total, pairs)
        for piece in moving:
            if piece.hop == middle:
                piece.got = exchange(piece.total, [(middle - 1, middle)])

    def finish(group, *others):
        while any(piece.value is None for piece in group):
            advance(group, *others)

    def cuts(sizes):
        unit, at, out = pairs // sum(sizes), 0, []
        for size in sizes:
            out.append((at, at + size * unit))
            at += size * unit
        return out

    mixed = [(y, x) for y in range(1, outer) for x in range(1, inner)]
    straight_x = [(0, x) for x in range(1, inner)]
    straight_y = [(y, 0) for y in range(1, outer)]
    straight = straight_x + straight_y
    own = [(0, 0)]
    n_mixed, half = len(mixed) * rows, rows // 2
    blocks = mixed + straight + own
    where = jnp.stack([core] + [target(o) * rows for o in blocks])

    def halves(group):
        left = sum(b - a for _, a, b in group) // 2
        upper, lower = [], []
        for offset, a, b in group:
            n, cut = blocks.index(offset), min(b, a + left)
            upper += [(n, a, cut)] if cut > a else []
            lower += [(n, cut, b)] if b > cut else []
            left -= cut - a
        return upper, lower

    groups = [
        halves([(o, 0, rows) for o in mixed]),
        halves([(o, 0, half) for o in straight]),
        halves([(o, half, rows) for o in straight]),
        halves([((0, 0), 0, rows)]),
    ]
    groups = [g for g in groups if g[0]]

    mixed_parts, found = [], []
    for cut in cuts(CUTS):
        out = run(lambda s: project(where, s, rho, *cut, groups), subspace)
        advance(mixed_parts)
        mixed_parts.append(Piece(*out[:2]))
        mixed_parts[-1].receive()
        found.append(out)

    def joined(at, turns):
        n = len(found) // turns
        return [
            [jnp.concatenate([f[2 * at + side] for f in found[k * n : (k + 1) * n]], 1) for side in (0, 1)]
            for k in range(turns)
        ]

    low_parts, high_parts, own_parts = [], [], []
    for at, group in enumerate((low_parts, high_parts, own_parts), 1):
        group += [Piece(*halves) for halves in joined(at, TURNS[at - 1])]

    weight = run(
        lambda *a: pair_weights(*a, pairs * q)[None, :], band_valence, band_conduction, occupied, energies
    )

    def gather(group):
        flat = [x for part in group for x in part.value]

        def work(*flat):
            halves = list(zip(flat[::2], flat[1::2]))
            upper = jnp.concatenate([jnp.where(core == 0, mine, other) for mine, other in halves], 1)
            lower = jnp.concatenate([jnp.where(core == 0, other, mine) for mine, other in halves], 1)
            sums = jnp.concatenate([upper, lower])
            return (sums * weight).astype(jnp.bfloat16), sums

        return run(work, *flat)

    steps = STEPS
    advance(mixed_parts)
    advance(mixed_parts, low_parts[:1])
    advance(mixed_parts, low_parts)
    advance(mixed_parts)
    advance(mixed_parts, low_parts)
    finish(mixed_parts)
    w_mixed, sum_mixed = gather(mixed_parts)

    def send_all(values, before):
        flat = run(lambda *v: v, *[v for v, _ in values], *before)
        return [send_pair(v, offset) for v, (_, offset) in zip(flat, values)]

    left, right = {}, {}
    before = []
    for k in range(steps):
        a, b = run(
            lambda w: panel(w, rho, k, steps, [((0, n_mixed), (0,)), ((0, n_mixed), (1,))], []), w_mixed
        )
        if k:
            advance(low_parts, high_parts)
        blocks = [slice(at * rows, (at + 1) * rows) for at in range(len(mixed))]
        got = send_all(
            [(a[block], (0, dx)) for block, (dy, dx) in zip(blocks, mixed)]
            + [(b[block], (dy, 0)) for block, (dy, dx) in zip(blocks, mixed)],
            before,
        )
        before = got
        for x, y, (dy, dx) in zip(got[: len(mixed)], got[len(mixed) :], mixed):
            left.setdefault((k, dy), []).append(x)
            right.setdefault((k, dx), []).append(y)
        if k == 0:
            advance(low_parts, high_parts[:1])
        else:
            advance(low_parts, high_parts, own_parts[:1])

    def straight_panel(w, k, part):
        adds = []
        for at, (dy, dx) in enumerate(straight):
            side, got = (0, left.get((k, dy))) if dy else (1, right.get((k, dx)))
            adds += [(at, side, x) for x in got or []]
        ends = [(at * half, (at + 1) * half) for at in range(len(straight))]

        def work(w, *extra):
            return panel(
                w, rho, k, steps, [(e, (0, 1)) for e in ends], [(o, s, x, part) for (o, s, _), x in zip(adds, extra)]
            )

        return run(work, w, *[x for _, _, x in adds])

    finish(low_parts)
    w_low, sum_low = gather(low_parts)
    low_arrived, high_arrived = [], []
    for k in range(steps):
        out = straight_panel(w_low, k, 0)
        if k:
            advance(high_parts, own_parts)
        before = send_all(list(zip(out, straight)), before)
        low_arrived.append(before)
        advance(high_parts, own_parts)

    finish(high_parts)
    w_high, sum_high = gather(high_parts)
    for k in range(steps):
        out = straight_panel(w_high, k, 1)
        if k:
            advance(own_parts)
        before = send_all(list(zip(out, straight)), before)
        high_arrived.append(before)
        advance(own_parts)

    finish(own_parts)
    w_own, sum_own = gather(own_parts)

    def by_block(mixed_rows, low_rows, high_rows, own_rows):
        blocks = {(0, 0): own_rows}
        for at, o in enumerate(mixed):
            blocks[o] = mixed_rows[at * rows : (at + 1) * rows]
        for at, o in enumerate(straight):
            block = slice(at * half, (at + 1) * half)
            blocks[o] = jnp.concatenate([low_rows[block], high_rows[block]])
        return jnp.concatenate([blocks[y, x] for y in range(outer) for x in range(inner)])

    def place(block):
        return (block // inner - my_outer) % outer * inner + (block % inner - my_inner) % inner

    slab_rows = vectors // slabs
    first_row = slab * slab_rows

    def local_sums(*parts):
        sums, weighted = by_block(*parts[:4]), by_block(*parts[4:])
        mine = lax.dynamic_slice_in_dim(
            sums, place(first_row // rows) * rows + first_row % rows, slab_rows
        )
        pieces = jnp.concatenate(split_bf16(mine, 2))
        local = lax.dot_general(
            pieces, weighted, (((1,), (1,)), ((), ())), preferred_element_type=jnp.float32
        )
        local = local[:slab_rows] + local[slab_rows:]
        return jnp.concatenate(
            [lax.dynamic_slice_in_dim(local, place(d) * rows, rows, 1) for d in range(q)], 1
        )

    local = run(local_sums, sum_mixed, sum_low, sum_high, sum_own, w_mixed, w_low, w_high, w_own)
    subspace_chi = lax.psum_scatter(local, "pair", scatter_dimension=1, tiled=True)

    own_sums = []
    for k in range(steps):
        own_sums += run(lambda w: panel(w, rho, k, steps, [((0, rows), (0, 1))], []), w_own)
    chi = None
    for k in range(steps):
        def work(own, *got, chi=chi):
            n = len(low_arrived[k])
            return assemble(chi, own, k, steps, list(got[:n]), list(got[n:]))

        chi = run(work, own_sums[k], *low_arrived[k], *high_arrived[k])
    return chi, subspace_chi


def solution(mesh):
    return jax.shard_map(
        body,
        mesh=mesh,
        in_specs=(P("pair", "slab"), P("slab", None), P("pair"), P("pair"), P(), P()),
        out_specs=(P("pair", "slab"), P("slab", "pair")),
        check_vma=False,
    )
```

time: 337 us -> 261 us (0.77)
  waiting for transfers between devices: 253 us -> 69.9 us
  Pallas kernels: 0 us -> 106 us
  matrix products: 68.9 us -> 3.43 us
  starting transfers between devices: 0.3 us -> 41.6 us
  other arithmetic: 0.06 us -> 12.7 us
  local copies, waits for them, and re-layouts: 0.63 us -> 11.2 us
    psum x1 -> x0, waiting for transfers between devices: 132 us -> none  [body(): coefficient = lax.psum(partial_value, 'slab')]
    reduce_scatter x2 -> x1, waiting for transfers between devices: 121 us -> 0.35 us  [body(): lax.psum_scatter(local, 'pair', scatter_dimension=1, tiled=True)]
    pallas_call x0 -> x14, Pallas kernels: none -> 106 us  [the longest x8 66 us: panel(): pl.pallas_call(kernel, out_shape=[jax.ShapeDtypeStruct((b - a, piece * le...]
    ppermute x0 -> x57, waiting for transfers between devices: none -> 69.6 us  [the longest x25 35.5 us: exchange(): return lax.ppermute(x, 'slab', perm)]
    dot_general x5 -> x3, matrix products: 68.9 us -> 3.43 us  [the longest x2 2.26 us: lookup(): rows = jnp.dot(table, one_hot, preferred_element_type=jnp.float32)]
    ppermute x0 -> x57, starting transfers between devices: none -> 41.6 us  [the longest x25 25.5 us: exchange(): return lax.ppermute(x, 'slab', perm)]
    unnamed x8 -> x52, local copies, waits for them, and re-layouts: 0.63 us -> 10.9 us
    select_n x0 -> x45, other arithmetic: none -> 4.75 us  [the longest x10 2.6 us: work(): jnp.where(core == 0, mine, other)]
  transfers between devices with their start and end apart: 3 -> 58, of which waited for: 2 -> 20; matrix products, arithmetic and copies ran while one was open for 11% -> 6% of each run, Pallas kernels for 0% -> 37%
where the time goes in v1:
time: 261 us; the launch traced here: 260 us
  Pallas kernels  106 us (41%)
  waiting for transfers between devices  69.9 us (27%)
  starting transfers between devices  41.6 us (16%)
  between operations  15.2 us (6%)
  other arithmetic  12.7 us (5%)
  local copies, waits for them, and re-layouts  11.2 us (4%)
  matrix products  3.43 us (1%)
    pallas_call x8, Pallas kernels, panel(): pl.pallas_call(kernel, out_shape=[jax.ShapeDtypeStruct((b - a, piece * le...  66 us
    ppermute x25, waiting for transfers between devices, exchange(): return lax.ppermute(x, 'slab', perm)  35.5 us
    pallas_call x4, Pallas kernels, project(): pl.pallas_call(kernel, out_shape=[jax.ShapeDtypeStruct((h, stop - start),...  34.8 us
    ppermute x12, waiting for transfers between devices, send_pair(): return lax.ppermute(x, 'pair', perm)  32.8 us
    ppermute x25, starting transfers between devices, exchange(): return lax.ppermute(x, 'slab', perm)  25.5 us
    ppermute x12, starting transfers between devices, send_pair(): return lax.ppermute(x, 'pair', perm)  11.4 us
    unnamed x52, local copies, waits for them, and re-layouts  10.9 us
    pallas_call x2, Pallas kernels, assemble(): pl.pallas_call(kernel, out_shape=jax.ShapeDtypeStruct((rows, width), own....  5.23 us
  transfers between devices with their start and end apart: 58, of which 20 were waited for; matrix products, arithmetic and copies ran while one was open for 6% of the time, Pallas kernels for 37%

profile of v1, /device:TPU:0, one launch (start us, length us, event | category | flops | bytes accessed | tf_op | source)
XLA Modules:
  0.0 260.2 jit_solution(17750101175129796084)
XLA Ops:
  7.4 2.8 %copy-done = bf16[6144,512]{1,0:T(8,128)(2,1)S(1)} copy-done((bf16[6144,512]{1,0:T(8,128)(2,1)S(1)}, bf16[6144,512]{1,0:T(8,128)(2,1)}, u32[]{:S(2)}) %copy-start) | copy-done | bytes 6291480
  10.2 8.7 %shard_map.77 = (f32[64,768]{1,0:T(8,128)S(1)}, f32[64,768]{1,0:T(8,128)S(1)}, f32[64,768]{1,0:T(8,128)S(1)}, f32[64,768]{1,0:T(8,128)S(1)}, f32[64,768]{1,0:T(8...) custom-call(s32[5]{0:T(128)S(1)} %stack.38.where_ref, ...), custom_call_target="tpu_custom_call" | custom-call | flops 1000 | bytes 1000 | tf_op jit(solution)/shard_map/pallas_call | solution.py:76
  19.4 8.7 %shard_map.78 = (f32[64,768]{1,0:T(8,128)S(1)}, f32[64,768]{1,0:T(8,128)S(1)}, f32[64,768]{1,0:T(8,128)S(1)}, f32[64,768]{1,0:T(8,128)S(1)}, f32[64,768]{1,0:T(8...) custom-call(s32[5]{0:T(128)S(1)} %stack.38.where_ref, ...), custom_call_target="tpu_custom_call" | custom-call | flops 1000 | bytes 1000 | tf_op jit(solution)/shard_map/pallas_call | solution.py:76
  29.8 2.7 %collective-permute-start.3 = (f32[64,768]{1,0:T(8,128)S(1)}, f32[64,768]{1,0:T(8,128)S(1)}, u32[]{:S(2)}, u32[]{:S(2)}) collective-permute-start(f32[64,768]{1,0:T(8,128)S(1)} %add.238), channel_id=1, source_target_pairs={{0,2},{1,3},{6,4},{7,5},{2,0},{3,1},{4,6},{5,7},{8,10},{9,11},{14,... | collective-permute-start | bytes 589832 | tf_op jit(solution)/shard_map/ppermute | solution.py:238
  32.5 2.8 %copy-done.1 = bf16[6144,512]{1,0:T(8,128)(2,1)S(1)} copy-done((bf16[6144,512]{1,0:T(8,128)(2,1)S(1)}, bf16[6144,512]{1,0:T(8,128)(2,1)}, u32[]{:S(2)}) %copy-start.1) | copy-done | bytes 6291480
  35.3 8.7 %shard_map.79 = (f32[64,768]{1,0:T(8,128)S(1)}, f32[64,768]{1,0:T(8,128)S(1)}, f32[64,768]{1,0:T(8,128)S(1)}, f32[64,768]{1,0:T(8,128)S(1)}, f32[64,768]{1,0:T(8...) custom-call(s32[5]{0:T(128)S(1)} %stack.38.where_ref, ...), custom_call_target="tpu_custom_call" | custom-call | flops 1000 | bytes 1000 | tf_op jit(solution)/shard_map/pallas_call | solution.py:76
  45.7 2.7 %collective-permute-start.10 = (f32[64,768]{1,0:T(8,128)S(1)}, f32[64,768]{1,0:T(8,128)S(1)}, u32[]{:S(2)}, u32[]{:S(2)}) collective-permute-start(f32[64,768]{1,0:T(8,128)S(1)} %add.240), channel_id=1, source_target_pairs={{0,2},{1,3},{6,4},{7,5},{2,0},{3,1},{4,6},{5,7},{8,10},{9,11},{14,... | collective-permute-start | bytes 589832 | tf_op jit(solution)/shard_map/ppermute | solution.py:238
  48.4 8.7 %shard_map.80 = (f32[64,768]{1,0:T(8,128)S(1)}, f32[64,768]{1,0:T(8,128)S(1)}, f32[64,768]{1,0:T(8,128)S(1)}, f32[64,768]{1,0:T(8,128)S(1)}, f32[64,768]{1,0:T(8...) custom-call(s32[5]{0:T(128)S(1)} %stack.38.where_ref, ...), custom_call_target="tpu_custom_call" | custom-call | flops 1000 | bytes 1000 | tf_op jit(solution)/shard_map/pallas_call | solution.py:76
  60.9 4.1 %collective-permute-done.12 = f32[64,768]{1,0:T(8,128)S(1)} collective-permute-done((f32[64,768]{1,0:T(8,128)S(1)}, f32[64,768]{1,0:T(8,128)S(1)}, u32[]{:S(2)}, u32[]{:S(2)}) %collective-permute-start.12) | collective-permute-done | bytes 196640 | tf_op jit(solution)/shard_map/ppermute | solution.py:238
  66.3 5.1 %collective-permute-done.14 = f32[64,768]{1,0:T(8,128)S(1)} collective-permute-done((f32[64,768]{1,0:T(8,128)S(1)}, f32[64,768]{1,0:T(8,128)S(1)}, u32[]{:S(2)}, u32[]{:S(2)}) %collective-permute-start.14) | collective-permute-done | bytes 196640 | tf_op jit(solution)/shard_map/ppermute | solution.py:238
  71.5 1.3 collective-permute-start.17
  72.9 7.8 %collective-permute-done.17 = f32[64,768]{1,0:T(8,128)S(1)} collective-permute-done((f32[64,768]{1,0:T(8,128)S(1)}, f32[64,768]{1,0:T(8,128)S(1)}, u32[]{:S(2)}, u32[]{:S(2)}) %collective-permute-start.17) | collective-permute-done | bytes 196640 | tf_op jit(solution)/shard_map/ppermute | solution.py:238
  80.8 1.3 collective-permute-start.19
  82.2 2.7 %collective-permute-start.18 = (f32[64,1536]{1,0:T(8,128)S(1)}, f32[64,1536]{1,0:T(8,128)S(1)}, u32[]{:S(2)}, u32[]{:S(2)}) collective-permute-start(f32[64,1536]{1,0:T(8,128)S(1)} %add.256), channel_id=1, source_target_pairs={{0,2},{1,3},{6,4},{7,5},{2,0},{3,1},{4,6},{5,7},{8,10},{9,11},{14,... | collective-permute-start | bytes 1179656 | tf_op jit(solution)/shard_map/ppermute | solution.py:238
  85.6 5.0 %collective-permute-done.19 = f32[64,768]{1,0:T(8,128)S(1)} collective-permute-done((f32[64,768]{1,0:T(8,128)S(1)}, f32[64,768]{1,0:T(8,128)S(1)}, u32[]{:S(2)}, u32[]{:S(2)}) %collective-permute-start.19) | collective-permute-done | bytes 196640 | tf_op jit(solution)/shard_map/ppermute | solution.py:238
  90.6 6.4 %collective-permute-done.18 = f32[64,1536]{1,0:T(8,128)S(1)} collective-permute-done((f32[64,1536]{1,0:T(8,128)S(1)}, f32[64,1536]{1,0:T(8,128)S(1)}, u32[]{:S(2)}, u32[]{:S(2)}) %collective-permute-start.18) | collective-permute-done | bytes 393248 | tf_op jit(solution)/shard_map/ppermute | solution.py:238
  98.6 1.4 multiply_convert_fusion.3
  100.0 8.1 %shard_map.81 = (f32[128,1536]{1,0:T(8,128)S(1)}, f32[128,1536]{1,0:T(8,128)S(1)}) custom-call(bf16[128,3072]{1,0:T(8,128)(2,1)S(1)} %get-tuple-element.398.w_ref, bf16[3072,6144]{1,0:T(8,128)(2,1)} %rho_ref.23), custom_call_target="tpu_custom_call" | custom-call | flops 1000 | bytes 1000 | tf_op jit(solution)/shard_map/pallas_call | solution.py:125
  108.1 1.6 collective-permute-start.29
  109.7 1.5 collective-permute-start.30
  111.2 1.5 collective-permute-start.27
  112.9 8.1 %shard_map.82 = (f32[128,1536]{1,0:T(8,128)S(1)}, f32[128,1536]{1,0:T(8,128)S(1)}) custom-call(bf16[128,3072]{1,0:T(8,128)(2,1)S(1)} %get-tuple-element.398.w_ref, bf16[3072,6144]{1,0:T(8,128)(2,1)} %rho_ref.23), custom_call_target="tpu_custom_call" | custom-call | flops 1000 | bytes 1000 | tf_op jit(solution)/shard_map/pallas_call | solution.py:125
  121.0 2.7 %collective-permute-done.27 = f32[64,1536]{1,0:T(8,128)S(1)} collective-permute-done((f32[64,1536]{1,0:T(8,128)S(1)}, f32[64,1536]{1,0:T(8,128)S(1)}, u32[]{:S(2)}, u32[]{:S(2)}) %collective-permute-start.27) | collective-permute-done | bytes 393248 | tf_op jit(solution)/shard_map/ppermute | solution.py:238
  124.0 2.1 collective-permute-start.28
  129.5 4.2 %collective-permute-done.28 = f32[64,1536]{1,0:T(8,128)S(1)} collective-permute-done((f32[64,1536]{1,0:T(8,128)S(1)}, f32[64,1536]{1,0:T(8,128)S(1)}, u32[]{:S(2)}, u32[]{:S(2)}) %collective-permute-start.28) | collective-permute-done | bytes 393248 | tf_op jit(solution)/shard_map/ppermute | solution.py:238
  135.6 1.7 collective-permute-start.31
  137.4 1.4 maximum_maximum_fusion.1
  138.8 8.1 %shard_map.83 = (f32[64,3072]{1,0:T(8,128)S(1)}, f32[64,3072]{1,0:T(8,128)S(1)}) custom-call(bf16[128,3072]{1,0:T(8,128)(2,1)S(1)} %get-tuple-element.396.w_ref, bf16[3072,6144]{1,0:T(8,128)(2,1)} %rho_ref.23, f32[128,1536]{1,0:T(8,128)S(1)} %collective-permute-done.30.refs_0_, f32[128,1536]{1,0:T(8,128)S(1)} %collective-permute-done.29.refs_1_), custom_call_target="tpu_custom_call" | custom-call | flops 1000 | bytes 1000 | tf_op jit(solution)/shard_map/pallas_call | solution.py:125
  147.7 6.2 %collective-permute-done.36.refs_0_ = f32[128,1536]{1,0:T(8,128)S(1)} collective-permute-done((f32[128,1536]{1,0:T(8,128)S(1)}, f32[128,1536]{1,0:T(8,128)S(1)}, u32[]{:S(2)}, u32[]{:S(2)}) %collective-permute-start.36) | collective-permute-done | bytes 786464 | tf_op jit(solution)/shard_map/ppermute | solution.py:201
  154.1 1.8 collective-permute-start.37
  157.7 8.1 %shard_map.84 = (f32[64,3072]{1,0:T(8,128)S(1)}, f32[64,3072]{1,0:T(8,128)S(1)}) custom-call(bf16[128,3072]{1,0:T(8,128)(2,1)S(1)} %get-tuple-element.396.w_ref, bf16[3072,6144]{1,0:T(8,128)(2,1)} %rho_ref.23, f32[128,1536]{1,0:T(8,128)S(1)} %collective-permute-done.36.refs_0_, f32[128,1536]{1,0:T(8,128)S(1)} %collective-permute-done.35.refs_1_), custom_call_target="tpu_custom_call" | custom-call | flops 1000 | bytes 1000 | tf_op jit(solution)/shard_map/pallas_call | solution.py:125
  166.1 2.1 collective-permute-start.41
  168.8 7.4 %collective-permute-done.42.refs_1_ = f32[64,3072]{1,0:T(8,128)S(1)} collective-permute-done((f32[64,3072]{1,0:T(8,128)S(1)}, f32[64,3072]{1,0:T(8,128)S(1)}, u32[]{:S(2)}, u32[]{:S(2)}) %collective-permute-start.42) | collective-permute-done | bytes 786464 | tf_op jit(solution)/shard_map/ppermute | solution.py:201
  176.4 1.5 collective-permute-start.47
  180.5 1.4 maximum_maximum_fusion.2
  181.8 9.0 %shard_map.85 = (f32[64,3072]{1,0:T(8,128)}, f32[64,3072]{1,0:T(8,128)}) custom-call(bf16[128,3072]{1,0:T(8,128)(2,1)S(1)} %get-tuple-element.397.w_ref, bf16[3072,6144]{1,0:T(8,128)(2,1)} %rho_ref.23, f32[128,1536]{1,0:T(8,128)S(1)} %collective-permute-done.30.refs_0_, f32[128,1536]{1,0:T(8,128)S(1)} %collective-permute-done.29.refs_1_), custom_call_target="tpu_custom_call" | custom-call | flops 1000 | bytes 1000 | tf_op jit(solution)/shard_map/pallas_call | solution.py:125
  190.8 4.1 %collective-permute-done.47.refs_2_ = f32[64,3072]{1,0:T(8,128)S(1)} collective-permute-done((f32[64,3072]{1,0:T(8,128)S(1)}, f32[64,3072]{1,0:T(8,128)S(1)}, u32[]{:S(2)}, u32[]{:S(2)}) %collective-permute-start.47) | collective-permute-done | bytes 786464 | tf_op jit(solution)/shard_map/ppermute | solution.py:201
  194.9 4.0 %collective-permute-done.48.refs_3_ = f32[64,3072]{1,0:T(8,128)S(1)} collective-permute-done((f32[64,3072]{1,0:T(8,128)S(1)}, f32[64,3072]{1,0:T(8,128)S(1)}, u32[]{:S(2)}, u32[]{:S(2)}) %collective-permute-start.48) | collective-permute-done | bytes 786464 | tf_op jit(solution)/shard_map/ppermute | solution.py:201
  200.6 1.3 collective-permute-start.54
  201.9 8.1 %shard_map.86 = (f32[64,3072]{1,0:T(8,128)S(1)}, f32[64,3072]{1,0:T(8,128)S(1)}) custom-call(bf16[128,3072]{1,0:T(8,128)(2,1)S(1)} %get-tuple-element.397.w_ref, bf16[3072,6144]{1,0:T(8,128)(2,1)} %rho_ref.23, f32[128,1536]{1,0:T(8,128)S(1)} %collective-permute-done.36.refs_0_, f32[128,1536]{1,0:T(8,128)S(1)} %collective-permute-done.35.refs_1_), custom_call_target="tpu_custom_call" | custom-call | flops 1000 | bytes 1000 | tf_op jit(solution)/shard_map/pallas_call | solution.py:125
  213.0 5.8 %collective-permute-done.53.refs_3_ = f32[64,3072]{1,0:T(8,128)S(1)} collective-permute-done((f32[64,3072]{1,0:T(8,128)}, f32[64,3072]{1,0:T(8,128)S(1)}, u32[]{:S(2)}, u32[]{:S(2)}) %collective-permute-start.53) | collective-permute-done | bytes 786464 | tf_op jit(solution)/shard_map/ppermute | solution.py:201
  218.9 2.0 collective-permute-done.54.refs_4_
  220.9 1.5 collective-permute-start.55
  227.7 1.3 copy-done.14
  231.2 8.1 %shard_map.87.refs_0_ = f32[128,3072]{1,0:T(8,128)S(1)} custom-call(bf16[128,3072]{1,0:T(8,128)(2,1)S(1)} %get-tuple-element.400.w_ref, bf16[3072,6144]{1,0:T(8,128)(2,1)} %rho_ref.23), custom_call_target="tpu_custom_call" | custom-call | flops 1000 | bytes 1000 | tf_op jit(solution)/shard_map/pallas_call | solution.py:125
  239.3 8.3 %shard_map.88.refs_1_ = f32[128,3072]{1,0:T(8,128)S(1)} custom-call(bf16[128,3072]{1,0:T(8,128)(2,1)S(1)} %get-tuple-element.400.w_ref, bf16[3072,6144]{1,0:T(8,128)(2,1)} %rho_ref.23), custom_call_target="tpu_custom_call" | custom-call | flops 1000 | bytes 1000 | tf_op jit(solution)/shard_map/pallas_call | solution.py:125
  247.7 2.7 %shard_map.89.refs_0_ = f32[128,6144]{1,0:T(8,128)} custom-call(f32[128,3072]{1,0:T(8,128)S(1)} %shard_map.87.refs_0_, f32[64,3072]{1,0:T(8,128)S(1)} %copy-done.3, f32[64,3072]{1,0:T(8,128)S(1)} %copy-done.5, f32[64,3072]{1,0:T(8,128)S(1)} %copy-done.11, f32[64,3072]{1,0:T(8,128)} %collective-permute-done.54.refs_4_), custom_call_target="tpu_custom_call" | custom-call | flops 1000 | bytes 1000 | tf_op jit(solution)/shard_map/pallas_call | solution.py:160
  250.5 2.5 shard_map.90
  (221 shorter events, 35.6 us)
Async XLA Ops:
  7.2 246.2 %reduce-scatter.2.cloned.1.call-start = ((), (), s32[]{:S(2)}) async-start(), calls=%async_computation.1 | async-start | bytes 163840 | tf_op jit(solution)/shard_map/reduce_scatter | solution.py:445
  18.9 10.0 %collective-permute-start.1 = (f32[64,768]{1,0:T(8,128)S(1)}, f32[64,768]{1,0:T(8,128)}, u32[]{:S(2)}, u32[]{:S(2)}) collective-permute-start(f32[64,768]{1,0:T(8,128)S(1)} %get-tuple-element.213), channel_id=1, source_target_pairs={{0,1},{1,0},{2,3},{3,2},{4,5},{5,4},{6,7},{7,6},{8,9},{9,8},{10,11... | collective-permute-start | bytes 589832 | tf_op jit(solution)/shard_map/ppermute | solution.py:204
  28.1 16.6 %collective-permute-start.2 = (f32[64,768]{1,0:T(8,128)S(1)}, f32[64,768]{1,0:T(8,128)}, u32[]{:S(2)}, u32[]{:S(2)}) collective-permute-start(f32[64,768]{1,0:T(8,128)S(1)} %get-tuple-element.219), channel_id=1, source_target_pairs={{0,1},{1,0},{2,3},{3,2},{4,5},{5,4},{6,7},{7,6},{8,9},{9,8},{10,11... | collective-permute-start | bytes 589832 | tf_op jit(solution)/shard_map/ppermute | solution.py:204
  28.2 53.9 %collective-permute-start.7 = (f32[64,1536]{1,0:T(8,128)S(1)}, f32[64,1536]{1,0:T(8,128)S(1)}, u32[]{:S(2)}, u32[]{:S(2)}) collective-permute-start(f32[64,1536]{1,0:T(8,128)S(1)} %pad_maximum_fusion.9), channel_id=1, source_target_pairs={{0,1},{1,0},{2,3},{3,2},{4,5},{5,4},{6,7},{7,6},{8,9},{9,8},{10,11... | collective-permute-start | bytes 1179656 | tf_op jit(solution)/shard_map/ppermute | solution.py:204
  29.8 14.2 %collective-permute-start.3 = (f32[64,768]{1,0:T(8,128)S(1)}, f32[64,768]{1,0:T(8,128)S(1)}, u32[]{:S(2)}, u32[]{:S(2)}) collective-permute-start(f32[64,768]{1,0:T(8,128)S(1)} %add.238), channel_id=1, source_target_pairs={{0,2},{1,3},{6,4},{7,5},{2,0},{3,1},{4,6},{5,7},{8,10},{9,11},{14,... | collective-permute-start | bytes 589832 | tf_op jit(solution)/shard_map/ppermute | solution.py:238
  44.1 13.4 %collective-permute-start.11 = (f32[64,768]{1,0:T(8,128)S(1)}, f32[64,768]{1,0:T(8,128)S(1)}, u32[]{:S(2)}, u32[]{:S(2)}) collective-permute-start(f32[64,768]{1,0:T(8,128)S(1)} %add_select_fusion.19), channel_id=1, source_target_pairs={{2,4},{3,5},{4,2},{5,3},{0,1},{1,0},{6,7},{7,6},{10,12},{11,13},{1... | collective-permute-start | bytes 589832 | tf_op jit(solution)/shard_map/ppermute | solution.py:238
  44.3 13.6 %collective-permute-start.9 = (f32[64,768]{1,0:T(8,128)S(1)}, f32[64,768]{1,0:T(8,128)S(1)}, u32[]{:S(2)}, u32[]{:S(2)}) collective-permute-start(f32[64,768]{1,0:T(8,128)S(1)} %get-tuple-element.243), channel_id=1, source_target_pairs={{0,1},{1,0},{2,3},{3,2},{4,5},{5,4},{6,7},{7,6},{8,9},{9,8},{10,11... | collective-permute-start | bytes 589832 | tf_op jit(solution)/shard_map/ppermute | solution.py:204
  45.7 11.8 %collective-permute-start.10 = (f32[64,768]{1,0:T(8,128)S(1)}, f32[64,768]{1,0:T(8,128)S(1)}, u32[]{:S(2)}, u32[]{:S(2)}) collective-permute-start(f32[64,768]{1,0:T(8,128)S(1)} %add.240), channel_id=1, source_target_pairs={{0,2},{1,3},{6,4},{7,5},{2,0},{3,1},{4,6},{5,7},{8,10},{9,11},{14,... | collective-permute-start | bytes 589832 | tf_op jit(solution)/shard_map/ppermute | solution.py:238
  57.2 8.0 %collective-permute-start.8 = (f32[64,768]{1,0:T(8,128)S(1)}, f32[64,768]{1,0:T(8,128)S(1)}, u32[]{:S(2)}, u32[]{:S(2)}) collective-permute-start(f32[64,768]{1,0:T(8,128)S(1)} %get-tuple-element.242), channel_id=1, source_target_pairs={{0,1},{1,0},{2,3},{3,2},{4,5},{5,4},{6,7},{7,6},{8,9},{9,8},{10,11... | collective-permute-start | bytes 589832 | tf_op jit(solution)/shard_map/ppermute | solution.py:204
  65.8 31.3 %collective-permute-start.6 = (f32[64,1536]{1,0:T(8,128)S(1)}, f32[64,1536]{1,0:T(8,128)S(1)}, u32[]{:S(2)}, u32[]{:S(2)}) collective-permute-start(f32[64,1536]{1,0:T(8,128)S(1)} %pad_maximum_fusion.7), channel_id=1, source_target_pairs={{0,1},{1,0},{2,3},{3,2},{4,5},{5,4},{6,7},{7,6},{8,9},{9,8},{10,11... | collective-permute-start | bytes 1179656 | tf_op jit(solution)/shard_map/ppermute | solution.py:204
  71.5 9.2 %collective-permute-start.17 = (f32[64,768]{1,0:T(8,128)S(1)}, f32[64,768]{1,0:T(8,128)S(1)}, u32[]{:S(2)}, u32[]{:S(2)}) collective-permute-start(f32[64,768]{1,0:T(8,128)S(1)} %add_select_fusion.14), channel_id=1, source_target_pairs={{2,0},{3,1},{4,6},{5,7},{10,8},{11,9},{12,14},{13,15},{18,16},{19,... | collective-permute-start | bytes 589832 | tf_op jit(solution)/shard_map/ppermute | solution.py:238
  72.9 7.9 %collective-permute-start.16 = (f32[64,768]{1,0:T(8,128)S(1)}, f32[64,768]{1,0:T(8,128)S(1)}, u32[]{:S(2)}, u32[]{:S(2)}) collective-permute-start(f32[64,768]{1,0:T(8,128)S(1)} %add_select_fusion.13), channel_id=1, source_target_pairs={{2,4},{3,5},{4,2},{5,3},{0,1},{1,0},{6,7},{7,6},{10,12},{11,13},{1... | collective-permute-start | bytes 589832 | tf_op jit(solution)/shard_map/ppermute | solution.py:238
  80.8 9.7 %collective-permute-start.19 = (f32[64,768]{1,0:T(8,128)S(1)}, f32[64,768]{1,0:T(8,128)S(1)}, u32[]{:S(2)}, u32[]{:S(2)}) collective-permute-start(f32[64,768]{1,0:T(8,128)S(1)} %add_select_fusion.12), channel_id=1, source_target_pairs={{2,0},{3,1},{4,6},{5,7},{10,8},{11,9},{12,14},{13,15},{18,16},{19,... | collective-permute-start | bytes 589832 | tf_op jit(solution)/shard_map/ppermute | solution.py:238
  82.2 14.8 %collective-permute-start.18 = (f32[64,1536]{1,0:T(8,128)S(1)}, f32[64,1536]{1,0:T(8,128)S(1)}, u32[]{:S(2)}, u32[]{:S(2)}) collective-permute-start(f32[64,1536]{1,0:T(8,128)S(1)} %add.256), channel_id=1, source_target_pairs={{0,2},{1,3},{6,4},{7,5},{2,0},{3,1},{4,6},{5,7},{8,10},{9,11},{14,... | collective-permute-start | bytes 1179656 | tf_op jit(solution)/shard_map/ppermute | solution.py:238
  85.0 12.7 %collective-permute-start.22 = (f32[64,768]{1,0:T(8,128)S(1)}, f32[64,768]{1,0:T(8,128)S(1)}, u32[]{:S(2)}, u32[]{:S(2)}) collective-permute-start(f32[64,768]{1,0:T(8,128)S(1)} %broadcast_select_fusion.33), channel_id=1, source_target_pairs={{0,1},{1,0},{2,3},{3,2},{4,5},{5,4},{6,7},{7,6},{8,9},{9,8},{10,11... | collective-permute-start | bytes 589832 | tf_op jit(solution)/shard_map/ppermute | solution.py:204
  85.1 12.8 %collective-permute-start.23 = (f32[64,768]{1,0:T(8,128)S(1)}, f32[64,768]{1,0:T(8,128)S(1)}, u32[]{:S(2)}, u32[]{:S(2)}) collective-permute-start(f32[64,768]{1,0:T(8,128)S(1)} %broadcast_select_fusion.31), channel_id=1, source_target_pairs={{0,1},{1,0},{2,3},{3,2},{4,5},{5,4},{6,7},{7,6},{8,9},{9,8},{10,11... | collective-permute-start | bytes 589832 | tf_op jit(solution)/shard_map/ppermute | solution.py:204
  97.1 26.7 %collective-permute-start.5 = (f32[64,1536]{1,0:T(8,128)S(1)}, f32[64,1536]{1,0:T(8,128)S(1)}, u32[]{:S(2)}, u32[]{:S(2)}) collective-permute-start(f32[64,1536]{1,0:T(8,128)S(1)} %pad_maximum_fusion.5), channel_id=1, source_target_pairs={{0,1},{1,0},{2,3},{3,2},{4,5},{5,4},{6,7},{7,6},{8,9},{9,8},{10,11... | collective-permute-start | bytes 1179656 | tf_op jit(solution)/shard_map/ppermute | solution.py:204
  97.7 13.4 %collective-permute-start.21 = (f32[64,1536]{1,0:T(8,128)S(1)}, f32[64,1536]{1,0:T(8,128)S(1)}, u32[]{:S(2)}, u32[]{:S(2)}) collective-permute-start(f32[64,1536]{1,0:T(8,128)S(1)} %add_select_fusion.11), channel_id=1, source_target_pairs={{2,4},{3,5},{4,2},{5,3},{0,1},{1,0},{6,7},{7,6},{10,12},{11,13},{1... | collective-permute-start | bytes 1179656 | tf_op jit(solution)/shard_map/ppermute | solution.py:238
  97.8 14.9 %collective-permute-start.20 = (f32[64,1536]{1,0:T(8,128)S(1)}, f32[64,1536]{1,0:T(8,128)S(1)}, u32[]{:S(2)}, u32[]{:S(2)}) collective-permute-start(f32[64,1536]{1,0:T(8,128)S(1)} %add.258), channel_id=1, source_target_pairs={{0,2},{1,3},{6,4},{7,5},{2,0},{3,1},{4,6},{5,7},{8,10},{9,11},{14,... | collective-permute-start | bytes 1179656 | tf_op jit(solution)/shard_map/ppermute | solution.py:238
  108.1 19.6 %collective-permute-start.29 = (f32[128,1536]{1,0:T(8,128)S(1)}, f32[128,1536]{1,0:T(8,128)S(1)}, u32[]{:S(2)}, u32[]{:S(2)}) collective-permute-start(f32[128,1536]{1,0:T(8,128)S(1)} %get-tuple-element.293), channel_id=1, source_target_pairs={{0,8},{8,0},{16,24},{24,16},{1,9},{9,1},{17,25},{25,17},{2,10},{10... | collective-permute-start | bytes 2359304 | tf_op jit(solution)/shard_map/ppermute | solution.py:201
  109.7 19.3 %collective-permute-start.30 = (f32[128,1536]{1,0:T(8,128)S(1)}, f32[128,1536]{1,0:T(8,128)S(1)}, u32[]{:S(2)}, u32[]{:S(2)}) collective-permute-start(f32[128,1536]{1,0:T(8,128)S(1)} %get-tuple-element.309), channel_id=1, source_target_pairs={{0,16},{8,24},{16,0},{24,8},{1,17},{9,25},{17,1},{25,9},{2,18},{10... | collective-permute-start | bytes 2359304 | tf_op jit(solution)/shard_map/ppermute | solution.py:201
  111.2 12.5 %collective-permute-start.27 = (f32[64,1536]{1,0:T(8,128)S(1)}, f32[64,1536]{1,0:T(8,128)S(1)}, u32[]{:S(2)}, u32[]{:S(2)}) collective-permute-start(f32[64,1536]{1,0:T(8,128)S(1)} %add_select_fusion.10), channel_id=1, source_target_pairs={{2,0},{3,1},{4,6},{5,7},{10,8},{11,9},{12,14},{13,15},{18,16},{19,... | collective-permute-start | bytes 1179656 | tf_op jit(solution)/shard_map/ppermute | solution.py:238
  112.8 11.0 %collective-permute-start.26 = (f32[64,1536]{1,0:T(8,128)S(1)}, f32[64,1536]{1,0:T(8,128)S(1)}, u32[]{:S(2)}, u32[]{:S(2)}) collective-permute-start(f32[64,1536]{1,0:T(8,128)S(1)} %add_select_fusion.9), channel_id=1, source_target_pairs={{2,4},{3,5},{4,2},{5,3},{0,1},{1,0},{6,7},{7,6},{10,12},{11,13},{1... | collective-permute-start | bytes 1179656 | tf_op jit(solution)/shard_map/ppermute | solution.py:238
  124.0 9.8 %collective-permute-start.28 = (f32[64,1536]{1,0:T(8,128)S(1)}, f32[64,1536]{1,0:T(8,128)S(1)}, u32[]{:S(2)}, u32[]{:S(2)}) collective-permute-start(f32[64,1536]{1,0:T(8,128)S(1)} %broadcast_select_fusion.7), channel_id=1, source_target_pairs={{0,2},{1,3},{6,4},{7,5},{2,0},{3,1},{4,6},{5,7},{8,10},{9,11},{14,... | collective-permute-start | bytes 1179656 | tf_op jit(solution)/shard_map/ppermute | solution.py:238
  126.1 27.9 %collective-permute-start = (f32[64,1536]{1,0:T(8,128)S(1)}, f32[64,1536]{1,0:T(8,128)S(1)}, u32[]{:S(2)}, u32[]{:S(2)}) collective-permute-start(f32[64,1536]{1,0:T(8,128)S(1)} %pad_maximum_fusion.1), channel_id=1, source_target_pairs={{0,1},{1,0},{2,3},{3,2},{4,5},{5,4},{6,7},{7,6},{8,9},{9,8},{10,11... | collective-permute-start | bytes 1179656 | tf_op jit(solution)/shard_map/ppermute | solution.py:204
  129.0 18.7 %collective-permute-start.35 = (f32[128,1536]{1,0:T(8,128)S(1)}, f32[128,1536]{1,0:T(8,128)S(1)}, u32[]{:S(2)}, u32[]{:S(2)}) collective-permute-start(f32[128,1536]{1,0:T(8,128)S(1)} %get-tuple-element.310), channel_id=1, source_target_pairs={{0,8},{8,0},{16,24},{24,16},{1,9},{9,1},{17,25},{25,17},{2,10},{10... | collective-permute-start | bytes 2359304 | tf_op jit(solution)/shard_map/ppermute | solution.py:201
  133.9 20.0 %collective-permute-start.36 = (f32[128,1536]{1,0:T(8,128)S(1)}, f32[128,1536]{1,0:T(8,128)S(1)}, u32[]{:S(2)}, u32[]{:S(2)}) collective-permute-start(f32[128,1536]{1,0:T(8,128)S(1)} %get-tuple-element.326), channel_id=1, source_target_pairs={{0,16},{8,24},{16,0},{24,8},{1,17},{9,25},{17,1},{25,9},{2,18},{10... | collective-permute-start | bytes 2359304 | tf_op jit(solution)/shard_map/ppermute | solution.py:201
  134.5 19.4 %collective-permute-start.32 = (f32[64,1536]{1,0:T(8,128)S(1)}, f32[64,1536]{1,0:T(8,128)S(1)}, u32[]{:S(2)}, u32[]{:S(2)}) collective-permute-start(f32[64,1536]{1,0:T(8,128)S(1)} %add_select_fusion.7), channel_id=1, source_target_pairs={{2,4},{3,5},{4,2},{5,3},{0,1},{1,0},{6,7},{7,6},{10,12},{11,13},{1... | collective-permute-start | bytes 1179656 | tf_op jit(solution)/shard_map/ppermute | solution.py:238
  135.6 18.4 %collective-permute-start.31 = (f32[64,1536]{1,0:T(8,128)S(1)}, f32[64,1536]{1,0:T(8,128)S(1)}, u32[]{:S(2)}, u32[]{:S(2)}) collective-permute-start(f32[64,1536]{1,0:T(8,128)S(1)} %add.264), channel_id=1, source_target_pairs={{0,2},{1,3},{6,4},{7,5},{2,0},{3,1},{4,6},{5,7},{8,10},{9,11},{14,... | collective-permute-start | bytes 1179656 | tf_op jit(solution)/shard_map/ppermute | solution.py:238
  154.1 11.7 %collective-permute-start.37 = (f32[64,1536]{1,0:T(8,128)S(1)}, f32[64,1536]{1,0:T(8,128)S(1)}, u32[]{:S(2)}, u32[]{:S(2)}) collective-permute-start(f32[64,1536]{1,0:T(8,128)S(1)} %broadcast_select_fusion.5), channel_id=1, source_target_pairs={{0,2},{1,3},{6,4},{7,5},{2,0},{3,1},{4,6},{5,7},{8,10},{9,11},{14,... | collective-permute-start | bytes 1179656 | tf_op jit(solution)/shard_map/ppermute | solution.py:238
  156.0 10.0 %collective-permute-start.40 = (f32[64,1536]{1,0:T(8,128)S(1)}, f32[64,1536]{1,0:T(8,128)S(1)}, u32[]{:S(2)}, u32[]{:S(2)}) collective-permute-start(f32[64,1536]{1,0:T(8,128)S(1)} %pad_maximum_fusion.11), channel_id=1, source_target_pairs={{0,1},{1,0},{2,3},{3,2},{4,5},{5,4},{6,7},{7,6},{8,9},{9,8},{10,11... | collective-permute-start | bytes 1179656 | tf_op jit(solution)/shard_map/ppermute | solution.py:204
  156.1 9.8 %collective-permute-start.38 = (f32[64,1536]{1,0:T(8,128)S(1)}, f32[64,1536]{1,0:T(8,128)S(1)}, u32[]{:S(2)}, u32[]{:S(2)}) collective-permute-start(f32[64,1536]{1,0:T(8,128)S(1)} %add_select_fusion.5), channel_id=1, source_target_pairs={{2,4},{3,5},{4,2},{5,3},{0,1},{1,0},{6,7},{7,6},{10,12},{11,13},{1... | collective-permute-start | bytes 1179656 | tf_op jit(solution)/shard_map/ppermute | solution.py:238
  156.7 19.5 %collective-permute-start.42 = (f32[64,3072]{1,0:T(8,128)S(1)}, f32[64,3072]{1,0:T(8,128)S(1)}, u32[]{:S(2)}, u32[]{:S(2)}) collective-permute-start(f32[64,3072]{1,0:T(8,128)S(1)} %get-tuple-element.327), channel_id=1, source_target_pairs={{0,8},{8,0},{16,24},{24,16},{1,9},{9,1},{17,25},{25,17},{2,10},{10... | collective-permute-start | bytes 2359304 | tf_op jit(solution)/shard_map/ppermute | solution.py:201
  157.2 19.2 %collective-permute-start.43 = (f32[64,3072]{1,0:T(8,128)S(1)}, f32[64,3072]{1,0:T(8,128)S(1)}, u32[]{:S(2)}, u32[]{:S(2)}) collective-permute-start(f32[64,3072]{1,0:T(8,128)S(1)} %get-tuple-element.355), channel_id=1, source_target_pairs={{0,16},{8,24},{16,0},{24,8},{1,17},{9,25},{17,1},{25,9},{2,18},{10... | collective-permute-start | bytes 2359304 | tf_op jit(solution)/shard_map/ppermute | solution.py:201
  166.1 11.8 %collective-permute-start.41 = (f32[64,1536]{1,0:T(8,128)S(1)}, f32[64,1536]{1,0:T(8,128)S(1)}, u32[]{:S(2)}, u32[]{:S(2)}) collective-permute-start(f32[64,1536]{1,0:T(8,128)S(1)} %broadcast_select_fusion.3), channel_id=1, source_target_pairs={{0,2},{1,3},{6,4},{7,5},{2,0},{3,1},{4,6},{5,7},{8,10},{9,11},{14,... | collective-permute-start | bytes 1179656 | tf_op jit(solution)/shard_map/ppermute | solution.py:238
  168.3 9.8 %collective-permute-start.39 = (f32[64,1536]{1,0:T(8,128)S(1)}, f32[64,1536]{1,0:T(8,128)S(1)}, u32[]{:S(2)}, u32[]{:S(2)}) collective-permute-start(f32[64,1536]{1,0:T(8,128)S(1)} %add_select_fusion.3), channel_id=1, source_target_pairs={{2,4},{3,5},{4,2},{5,3},{0,1},{1,0},{6,7},{7,6},{10,12},{11,13},{1... | collective-permute-start | bytes 1179656 | tf_op jit(solution)/shard_map/ppermute | solution.py:238
  168.3 12.0 %collective-permute-start.45 = (f32[64,1536]{1,0:T(8,128)S(1)}, f32[64,1536]{1,0:T(8,128)S(1)}, u32[]{:S(2)}, u32[]{:S(2)}) collective-permute-start(f32[64,1536]{1,0:T(8,128)S(1)} %broadcast_select_fusion.4), channel_id=1, source_target_pairs={{0,1},{1,0},{2,3},{3,2},{4,5},{5,4},{6,7},{7,6},{8,9},{9,8},{10,11... | collective-permute-start | bytes 1179656 | tf_op jit(solution)/shard_map/ppermute | solution.py:204
  176.4 18.5 %collective-permute-start.47 = (f32[64,3072]{1,0:T(8,128)S(1)}, f32[64,3072]{1,0:T(8,128)S(1)}, u32[]{:S(2)}, u32[]{:S(2)}) collective-permute-start(f32[64,3072]{1,0:T(8,128)S(1)} %get-tuple-element.356), channel_id=1, source_target_pairs={{0,8},{8,0},{16,24},{24,16},{1,9},{9,1},{17,25},{25,17},{2,10},{10... | collective-permute-start | bytes 2359304 | tf_op jit(solution)/shard_map/ppermute | solution.py:201
  178.1 20.8 %collective-permute-start.44 = (f32[64,1536]{1,0:T(8,128)S(1)}, f32[64,1536]{1,0:T(8,128)S(1)}, u32[]{:S(2)}, u32[]{:S(2)}) collective-permute-start(f32[64,1536]{1,0:T(8,128)S(1)} %add_select_fusion.2), channel_id=1, source_target_pairs={{0,2},{1,3},{6,4},{7,5},{2,0},{3,1},{4,6},{5,7},{8,10},{9,11},{14,... | collective-permute-start | bytes 1179656 | tf_op jit(solution)/shard_map/ppermute | solution.py:238
  179.3 19.7 %collective-permute-start.48 = (f32[64,3072]{1,0:T(8,128)S(1)}, f32[64,3072]{1,0:T(8,128)S(1)}, u32[]{:S(2)}, u32[]{:S(2)}) collective-permute-start(f32[64,3072]{1,0:T(8,128)S(1)} %get-tuple-element.372), channel_id=1, source_target_pairs={{0,16},{8,24},{16,0},{24,8},{1,17},{9,25},{17,1},{25,9},{2,18},{10... | collective-permute-start | bytes 2359304 | tf_op jit(solution)/shard_map/ppermute | solution.py:201
  180.2 18.7 %collective-permute-start.50 = (f32[64,1536]{1,0:T(8,128)S(1)}, f32[64,1536]{1,0:T(8,128)S(1)}, u32[]{:S(2)}, u32[]{:S(2)}) collective-permute-start(f32[64,1536]{1,0:T(8,128)S(1)} %add_select_fusion.1), channel_id=1, source_target_pairs={{2,4},{3,5},{4,2},{5,3},{0,1},{1,0},{6,7},{7,6},{10,12},{11,13},{1... | collective-permute-start | bytes 1179656 | tf_op jit(solution)/shard_map/ppermute | solution.py:238
  199.1 12.9 %collective-permute-start.51 = (f32[64,1536]{1,0:T(8,128)S(1)}, f32[64,1536]{1,0:T(8,128)S(1)}, u32[]{:S(2)}, u32[]{:S(2)}) collective-permute-start(f32[64,1536]{1,0:T(8,128)S(1)} %add_select_fusion), channel_id=1, source_target_pairs={{0,2},{1,3},{6,4},{7,5},{2,0},{3,1},{4,6},{5,7},{8,10},{9,11},{14,... | collective-permute-start | bytes 1179656 | tf_op jit(solution)/shard_map/ppermute | solution.py:238
  200.1 18.8 %collective-permute-start.53 = (f32[64,3072]{1,0:T(8,128)}, f32[64,3072]{1,0:T(8,128)S(1)}, u32[]{:S(2)}, u32[]{:S(2)}) collective-permute-start(f32[64,3072]{1,0:T(8,128)} %get-tuple-element.373), channel_id=1, source_target_pairs={{0,8},{8,0},{16,24},{24,16},{1,9},{9,1},{17,25},{25,17},{2,10},{10... | collective-permute-start | bytes 2359304 | tf_op jit(solution)/shard_map/ppermute | solution.py:201
  200.6 22.3 %collective-permute-start.49 = (f32[64,1536]{1,0:T(8,128)S(1)}, f32[64,1536]{1,0:T(8,128)}, u32[]{:S(2)}, u32[]{:S(2)}) collective-permute-start(f32[64,1536]{1,0:T(8,128)S(1)} %broadcast_select_fusion.1), channel_id=1, source_target_pairs={{0,1},{1,0},{2,3},{3,2},{4,5},{5,4},{6,7},{7,6},{8,9},{9,8},{10,11... | collective-permute-start | bytes 1179656 | tf_op jit(solution)/shard_map/ppermute | solution.py:204
  200.6 20.3 %collective-permute-start.54 = (f32[64,3072]{1,0:T(8,128)}, f32[64,3072]{1,0:T(8,128)}, u32[]{:S(2)}, u32[]{:S(2)}) collective-permute-start(f32[64,3072]{1,0:T(8,128)} %get-tuple-element.385), channel_id=1, source_target_pairs={{0,16},{8,24},{16,0},{24,8},{1,17},{9,25},{17,1},{25,9},{2,18},{10... | collective-permute-start | bytes 2359304 | tf_op jit(solution)/shard_map/ppermute | solution.py:201
  212.8 10.1 %collective-permute-start.52 = (f32[64,1536]{1,0:T(8,128)}, f32[64,1536]{1,0:T(8,128)}, u32[]{:S(2)}, u32[]{:S(2)}) collective-permute-start(f32[64,1536]{1,0:T(8,128)} %broadcast_select_fusion), channel_id=1, source_target_pairs={{0,1},{1,0},{2,3},{3,2},{4,5},{5,4},{6,7},{7,6},{8,9},{9,8},{10,11... | collective-permute-start | bytes 1179656 | tf_op jit(solution)/shard_map/ppermute | solution.py:204
  220.9 29.6 %collective-permute-start.55 = (f32[64,3072]{1,0:T(8,128)}, f32[64,3072]{1,0:T(8,128)}, u32[]{:S(2)}, u32[]{:S(2)}) collective-permute-start(f32[64,3072]{1,0:T(8,128)} %copy-done.13), channel_id=1, source_target_pairs={{0,8},{8,0},{16,24},{24,16},{1,9},{9,1},{17,25},{25,17},{2,10},{10... | collective-permute-start | bytes 2359304 | tf_op jit(solution)/shard_map/ppermute | solution.py:201
  222.4 28.1 %collective-permute-start.56 = (f32[64,3072]{1,0:T(8,128)}, f32[64,3072]{1,0:T(8,128)}, u32[]{:S(2)}, u32[]{:S(2)}) collective-permute-start(f32[64,3072]{1,0:T(8,128)} %copy-done.12), channel_id=1, source_target_pairs={{0,16},{8,24},{16,0},{24,8},{1,17},{9,25},{17,1},{25,9},{2,18},{10... | collective-permute-start | bytes 2359304 | tf_op jit(solution)/shard_map/ppermute | solution.py:201
  (31 other events, 143.5 us)
Sparse Core Ops, SparseCore 0:
  231.3 21.9 reduce-scatter.1

commit v2 on v1

--- a/solution.py
+++ b/solution.py
@@ -11,10 +11,9 @@
 COST = pl.CostEstimate(flops=1000, bytes_accessed=1000, transcendentals=0)
 
 
-BLOCK = 384
+BLOCK = 512
 WIDE = 768
-CUTS = (1, 1, 1, 1)
-TURNS = (2, 2, 2)
+CUTS = (1, 1)
 STEPS = 2
 
 
@@ -52,6 +51,33 @@
         for size in range(most // unit * unit, 0, -unit):
             if extent % size == 0:
                 return size
+
+
+def small(work, out_shapes, flags, *operands):
+    def kernel(flags_ref, *refs):
+        results = work(flags_ref, *[ref[...] for ref in refs[: len(operands)]])
+        for ref, result in zip(refs[len(operands) :], results):
+            ref[...] = result
+
+    def whole(x):
+        return pl.BlockSpec(x.shape, lambda i, flags: (0,) * len(x.shape))
+
+    return pl.pallas_call(
+        kernel,
+        out_shape=out_shapes,
+        grid_spec=pltpu.PrefetchScalarGridSpec(
+            num_scalar_prefetch=1,
+            grid=(1,),
+            in_specs=[whole(x) for x in operands],
+            out_specs=[whole(x) for x in out_shapes],
+        ),
+        compiler_params=pltpu.CompilerParams(vmem_limit_bytes=VMEM),
+        cost_estimate=COST,
+    )(flags, *operands)
+
+
+def like(x):
+    return jax.ShapeDtypeStruct(x.shape, x.dtype)
 
 
 def project(where, subspace, rho, start, stop, groups):
@@ -171,6 +197,49 @@
     )(*before, own, *arrived)
 
 
+def small_product(first, count, sums, weighted, stands):
+    pairs = sums[0].shape[1]
+    total = sum(x.shape[0] for x in sums)
+    block = fitting(pairs, 512)
+    n = len(sums)
+
+    def kernel(first_ref, *refs):
+        out, rows, others = refs[2 * n :]
+        for group, to in ((refs[:n], rows), (refs[n : 2 * n], others)):
+            for ref, at in zip(group, stands):
+                size = ref.shape[0] // len(at)
+                for k, start in enumerate(at):
+                    to[pl.ds(start, size), :] = ref[pl.ds(k * size, size), :]
+        mine = rows[pl.ds(pl.multiple_of(first_ref[0], 8), count), :]
+        top = mine.astype(jnp.bfloat16)
+        rest = (mine - top.astype(jnp.float32)).astype(jnp.bfloat16)
+        dims = (((1,), (1,)), ((), ()))
+        found = lax.dot_general(top, others[...], dims, preferred_element_type=jnp.float32)
+        found = found + lax.dot_general(rest, others[...], dims, preferred_element_type=jnp.float32)
+
+        @pl.when(pl.program_id(0) == 0)
+        def _():
+            out[...] = found
+
+        @pl.when(pl.program_id(0) > 0)
+        def _():
+            out[...] += found
+
+    return pl.pallas_call(
+        kernel,
+        out_shape=jax.ShapeDtypeStruct((count, total), jnp.float32),
+        grid_spec=pltpu.PrefetchScalarGridSpec(
+            num_scalar_prefetch=1,
+            grid=(pairs // block,),
+            in_specs=[pl.BlockSpec((x.shape[0], block), lambda i, at: (0, i)) for x in (*sums, *weighted)],
+            out_specs=pl.BlockSpec((count, total), lambda i, at: (0, 0)),
+            scratch_shapes=[pltpu.VMEM((total, block), jnp.float32), pltpu.VMEM((total, block), jnp.bfloat16)],
+        ),
+        compiler_params=pltpu.CompilerParams(vmem_limit_bytes=VMEM),
+        cost_estimate=COST,
+    )(first, *sums, *weighted)
+
+
 def body(rho, subspace, band_valence, band_conduction, occupied, energies):
     q, slabs = lax.axis_size("pair"), lax.axis_size("slab")
     pairs, width = rho.shape
@@ -187,7 +256,7 @@
     def run(work, *operands):
         n = len(operands)
         out = work(*lax.optimization_barrier((*operands, *last))[:n])
-        last[:] = jax.tree.leaves(out)[:1]
+        last[:] = jax.tree.leaves(out)
         return out
 
     def target(offset):
@@ -207,27 +276,26 @@
 
     class Piece:
         def __init__(self, keep, send):
-            self.total, self.hop, self.value = keep, -1, None
-            self.got = send
+            self.total, self.hop, self.value, self.moving = keep, 0, None, True
+            self.got = send_core(send)
 
         def receive(self):
+            if not self.moving:
+                return
             total, got, hop = self.total, self.got, self.hop
-            if hop < 0:
-                self.got = send_core(got)
-            elif hop == 0:
+            if hop == 0:
                 self.total = run(jnp.add, total, got)
             elif hop <= middle:
                 here = (chip == hop) | (chip == chips - 1 - hop)
                 if hop == middle:
                     here = (chip == middle - 1) | (chip == middle)
                 self.total = run(lambda a, b: jnp.where(here, a + b, a), total, got)
-            elif hop < 2 * middle:
+            else:
                 out = 2 * middle - hop
                 here = (chip == out - 1) | (chip == chips - out)
                 self.total = run(lambda a, b: jnp.where(here, b, a), total, got)
-            else:
-                self.value = (total, got)
             self.hop += 1
+            self.moving = False
 
     def exchange(x, pairs, both=True):
         moves = pairs + [(b, a) for a, b in pairs] if both else pairs
@@ -241,9 +309,7 @@
         moving = [piece for group in groups for piece in group if piece.value is None]
         for piece in moving:
             piece.receive()
-        for piece in moving:
-            if piece.hop == 2 * middle and piece.value is None:
-                piece.got = send_core(piece.total)
+            piece.moving = piece.value is None
         for t in range(middle - 1, 0, -1):
             ins = [p for p in moving if p.hop == t]
             outs = [p for p in moving if p.hop == 2 * middle - t]
@@ -264,6 +330,10 @@
         for piece in moving:
             if piece.hop == middle:
                 piece.got = exchange(piece.total, [(middle - 1, middle)])
+        for piece in moving:
+            if piece.hop == 2 * middle:
+                piece.value = (piece.total, run(lambda x: x, send_core(piece.total)))
+                piece.moving = False
 
     def finish(group, *others):
         while any(piece.value is None for piece in group):
@@ -303,24 +373,21 @@
     ]
     groups = [g for g in groups if g[0]]
 
-    mixed_parts, found = [], []
+    mixed_parts, low_parts, high_parts, own_parts = parts = [[] for _ in groups]
+
+    def receive(*groups):
+        for group in groups:
+            for piece in group:
+                piece.receive()
+
     for cut in cuts(CUTS):
         out = run(lambda s: project(where, s, rho, *cut, groups), subspace)
-        advance(mixed_parts)
-        mixed_parts.append(Piece(*out[:2]))
-        mixed_parts[-1].receive()
-        found.append(out)
-
-    def joined(at, turns):
-        n = len(found) // turns
-        return [
-            [jnp.concatenate([f[2 * at + side] for f in found[k * n : (k + 1) * n]], 1) for side in (0, 1)]
-            for k in range(turns)
-        ]
-
-    low_parts, high_parts, own_parts = [], [], []
-    for at, group in enumerate((low_parts, high_parts, own_parts), 1):
-        group += [Piece(*halves) for halves in joined(at, TURNS[at - 1])]
+        halves_of = [out[2 * at : 2 * at + 2] for at in range(len(groups))]
+        mixed_parts.append(Piece(*halves_of[0]))
+        advance(mixed_parts[:-1])
+        advance(mixed_parts[-1:])
+        for group, both in zip(parts[1:], halves_of[1:]):
+            group.append(Piece(*both))
 
     weight = run(
         lambda *a: pair_weights(*a, pairs * q)[None, :], band_valence, band_conduction, occupied, energies
@@ -329,21 +396,28 @@
     def gather(group):
         flat = [x for part in group for x in part.value]
 
+        half = flat[0].shape[0]
+
+        def kernel(flags, weight, *flat):
+            upper, lower = [], []
+            for mine, other in zip(flat[::2], flat[1::2]):
+                upper.append(jnp.where(flags[0] == 0, mine, other))
+                lower.append(jnp.where(flags[0] == 0, other, mine))
+            sums = jnp.concatenate([jnp.concatenate(upper, 1), jnp.concatenate(lower, 1)])
+            return (sums * weight).astype(jnp.bfloat16), sums
+
         def work(*flat):
-            halves = list(zip(flat[::2], flat[1::2]))
-            upper = jnp.concatenate([jnp.where(core == 0, mine, other) for mine, other in halves], 1)
-            lower = jnp.concatenate([jnp.where(core == 0, other, mine) for mine, other in halves], 1)
-            sums = jnp.concatenate([upper, lower])
-            return (sums * weight).astype(jnp.bfloat16), sums
+            shape = (2 * half, pairs)
+            out = [jax.ShapeDtypeStruct(shape, jnp.bfloat16), jax.ShapeDtypeStruct(shape, jnp.float32)]
+            return small(kernel, out, core[None], weight, *flat)
 
         return run(work, *flat)
 
     steps = STEPS
-    advance(mixed_parts)
+    receive(low_parts, high_parts, own_parts)
     advance(mixed_parts, low_parts[:1])
     advance(mixed_parts, low_parts)
-    advance(mixed_parts)
-    advance(mixed_parts, low_parts)
+    advance(mixed_parts, low_parts, high_parts[:1])
     finish(mixed_parts)
     w_mixed, sum_mixed = gather(mixed_parts)
 
@@ -358,7 +432,7 @@
             lambda w: panel(w, rho, k, steps, [((0, n_mixed), (0,)), ((0, n_mixed), (1,))], []), w_mixed
         )
         if k:
-            advance(low_parts, high_parts)
+            advance(low_parts, high_parts, own_parts[:1])
         blocks = [slice(at * rows, (at + 1) * rows) for at in range(len(mixed))]
         got = send_all(
             [(a[block], (0, dx)) for block, (dy, dx) in zip(blocks, mixed)]
@@ -370,9 +444,7 @@
             left.setdefault((k, dy), []).append(x)
             right.setdefault((k, dx), []).append(y)
         if k == 0:
-            advance(low_parts, high_parts[:1])
-        else:
-            advance(low_parts, high_parts, own_parts[:1])
+            advance(low_parts, high_parts)
 
     def straight_panel(w, k, part):
         adds = []
@@ -395,57 +467,48 @@
         out = straight_panel(w_low, k, 0)
         if k:
             advance(high_parts, own_parts)
+        else:
+            advance(high_parts, own_parts)
         before = send_all(list(zip(out, straight)), before)
         low_arrived.append(before)
-        advance(high_parts, own_parts)
+
+    def rank(offset):
+        return offset[0] * inner + offset[1]
+
+    def place(block):
+        return (block // inner - my_outer) % outer * inner + (block % inner - my_inner) % inner
+
+    stands = [
+        [rank(o) * rows for o in mixed],
+        [rank(o) * rows for o in straight],
+        [rank(o) * rows + half for o in straight],
+        [0],
+    ]
+    slab_rows = vectors // slabs
+    first_row = slab * slab_rows
+
+    def local_sums(*groups):
+        mine = place(first_row // rows) * rows + first_row % rows
+        local = small_product(mine[None], slab_rows, groups[:4], groups[4:], stands)
+        return [local[:, n * rows : (n + 1) * rows] for n in range(q)]
 
     finish(high_parts)
     w_high, sum_high = gather(high_parts)
+    own_sums = []
     for k in range(steps):
         out = straight_panel(w_high, k, 1)
-        if k:
+        if k == 0:
             advance(own_parts)
+        else:
+            finish(own_parts)
+            w_own, sum_own = gather(own_parts)
+            local = run(local_sums, sum_mixed, sum_low, sum_high, sum_own, w_mixed, w_low, w_high, w_own)
+            arrivals = [send_pair(local[n], (n // inner, n % inner)) for n in range(1, q)]
+            own_sums += run(lambda w: panel(w, rho, 0, steps, [((0, rows), (0, 1))], []), w_own)
         before = send_all(list(zip(out, straight)), before)
         high_arrived.append(before)
-        advance(own_parts)
-
-    finish(own_parts)
-    w_own, sum_own = gather(own_parts)
-
-    def by_block(mixed_rows, low_rows, high_rows, own_rows):
-        blocks = {(0, 0): own_rows}
-        for at, o in enumerate(mixed):
-            blocks[o] = mixed_rows[at * rows : (at + 1) * rows]
-        for at, o in enumerate(straight):
-            block = slice(at * half, (at + 1) * half)
-            blocks[o] = jnp.concatenate([low_rows[block], high_rows[block]])
-        return jnp.concatenate([blocks[y, x] for y in range(outer) for x in range(inner)])
-
-    def place(block):
-        return (block // inner - my_outer) % outer * inner + (block % inner - my_inner) % inner
-
-    slab_rows = vectors // slabs
-    first_row = slab * slab_rows
-
-    def local_sums(*parts):
-        sums, weighted = by_block(*parts[:4]), by_block(*parts[4:])
-        mine = lax.dynamic_slice_in_dim(
-            sums, place(first_row // rows) * rows + first_row % rows, slab_rows
-        )
-        pieces = jnp.concatenate(split_bf16(mine, 2))
-        local = lax.dot_general(
-            pieces, weighted, (((1,), (1,)), ((), ())), preferred_element_type=jnp.float32
-        )
-        local = local[:slab_rows] + local[slab_rows:]
-        return jnp.concatenate(
-            [lax.dynamic_slice_in_dim(local, place(d) * rows, rows, 1) for d in range(q)], 1
-        )
-
-    local = run(local_sums, sum_mixed, sum_low, sum_high, sum_own, w_mixed, w_low, w_high, w_own)
-    subspace_chi = lax.psum_scatter(local, "pair", scatter_dimension=1, tiled=True)
-
-    own_sums = []
-    for k in range(steps):
+
+    for k in range(1, steps):
         own_sums += run(lambda w: panel(w, rho, k, steps, [((0, rows), (0, 1))], []), w_own)
     chi = None
     for k in range(steps):
@@ -454,6 +517,8 @@
             return assemble(chi, own, k, steps, list(got[:n]), list(got[n:]))
 
         chi = run(work, own_sums[k], *low_arrived[k], *high_arrived[k])
+        if k == steps - 2:
+            subspace_chi = run(lambda *x: sum(x[1:], x[0]), local[0], *arrivals)
     return chi, subspace_chi
 
 

time: 261 us -> 228 us (0.87)
  between operations: 15.2 us -> 1.62 us
  waiting for transfers between devices: 69.9 us -> 61.4 us
  other arithmetic: 12.7 us -> 4.6 us
  starting transfers between devices: 41.6 us -> 36.7 us
  local copies, waits for them, and re-layouts: 11.2 us -> 15.5 us
    ppermute x25 -> x18, starting transfers between devices: 25.5 us -> 15.5 us  [exchange(): return lax.ppermute(x, 'slab', perm)]
    ppermute x25 -> x18, waiting for transfers between devices: 35.5 us -> 26.2 us  [exchange(): return lax.ppermute(x, 'slab', perm)]
    ppermute x12 -> x15, starting transfers between devices: 11.4 us -> 18.3 us  [send_pair(): return lax.ppermute(x, 'pair', perm)]
    ppermute x20 -> x16, waiting for transfers between devices: 1.25 us -> 8.1 us  [send_core(): return lax.ppermute(x, 'slab', [(s, s ^ 1) for s in range(slabs)])]
    ppermute x12 -> x15, waiting for transfers between devices: 32.8 us -> 27.1 us  [send_pair(): return lax.ppermute(x, 'pair', perm)]
    pallas_call x4 -> x2, Pallas kernels: 34.8 us -> 29.3 us  [project(): pl.pallas_call(kernel, out_shape=[jax.ShapeDtypeStruct((h, stop - start),...]
    pallas_call x0 -> x5, Pallas kernels: none -> 5.47 us  [the longest x1 3.54 us: small_product(): pl.pallas_call(kernel, out_shape=jax.ShapeDtypeStruct((count, total), jnp...]
    unnamed x52 -> x48, local copies, waits for them, and re-layouts: 10.9 us -> 15.4 us
  transfers between devices with their start and end apart: 58 -> 49, of which waited for: 20 -> 21; matrix products, arithmetic and copies ran while one was open for 6% -> 3% of each run, Pallas kernels for 37% -> 39%
where the time goes in v2:
time: 228 us; the launch traced here: 227 us
  Pallas kernels  105 us (46%)
  waiting for transfers between devices  61.4 us (27%)
  starting transfers between devices  36.7 us (16%)
  local copies, waits for them, and re-layouts  15.5 us (7%)
  other arithmetic  4.6 us (2%)
    pallas_call x8, Pallas kernels, panel(): pl.pallas_call(kernel, out_shape=[jax.ShapeDtypeStruct((b - a, piece * le...  66.1 us
    pallas_call x2, Pallas kernels, project(): pl.pallas_call(kernel, out_shape=[jax.ShapeDtypeStruct((h, stop - start),...  29.3 us
    ppermute x15, waiting for transfers between devices, send_pair(): return lax.ppermute(x, 'pair', perm)  27.1 us
    ppermute x18, waiting for transfers between devices, exchange(): return lax.ppermute(x, 'slab', perm)  26.2 us
    ppermute x15, starting transfers between devices, send_pair(): return lax.ppermute(x, 'pair', perm)  18.3 us
    ppermute x18, starting transfers between devices, exchange(): return lax.ppermute(x, 'slab', perm)  15.5 us
    unnamed x48, local copies, waits for them, and re-layouts  15.4 us
    ppermute x16, waiting for transfers between devices, send_core(): return lax.ppermute(x, 'slab', [(s, s ^ 1) for s in range(slabs)])  8.1 us
  transfers between devices with their start and end apart: 49, of which 21 were waited for; matrix products, arithmetic and copies ran while one was open for 3% of the time, Pallas kernels for 39%

profile of v2, /device:TPU:0, one launch (start us, length us, event | category | flops | bytes accessed | tf_op | source)
XLA Modules:
  0.0 227.4 jit_solution(4311491095257585670)
XLA Ops:
  0.8 2.8 %copy-done = bf16[6144,512]{1,0:T(8,128)(2,1)S(1)} copy-done((bf16[6144,512]{1,0:T(8,128)(2,1)S(1)}, bf16[6144,512]{1,0:T(8,128)(2,1)}, u32[]{:S(2)}) %copy-start) | copy-done | bytes 6291480
  3.6 14.6 %shard_map.77 = (f32[64,1536]{1,0:T(8,128)S(1)}, f32[64,1536]{1,0:T(8,128)S(1)}, f32[64,1536]{1,0:T(8,128)S(1)}, f32[64,1536]{1,0:T(8,128)S(1)}, f32[64,1536]{1,...) custom-call(s32[5]{0:T(128)S(1)} %stack.35.where_ref, ...), custom_call_target="tpu_custom_call" | custom-call | flops 1000 | bytes 1000 | tf_op jit(solution)/shard_map/pallas_call | solution.py:102
  18.8 1.3 collective-permute-done
  20.2 3.0 %collective-permute-start.2 = (f32[64,1536]{1,0:T(8,128)S(1)}, f32[64,1536]{1,0:T(8,128)S(1)}, u32[]{:S(2)}, u32[]{:S(2)}) collective-permute-start(f32[64,1536]{1,0:T(8,128)S(1)} %add.181), channel_id=1, source_target_pairs={{0,2},{1,3},{6,4},{7,5},{2,0},{3,1},{4,6},{5,7},{8,10},{9,11},{14,... | collective-permute-start | bytes 1179656 | tf_op jit(solution)/shard_map/ppermute | solution.py:306
  23.7 2.8 %copy-done.1 = bf16[6144,512]{1,0:T(8,128)(2,1)S(1)} copy-done((bf16[6144,512]{1,0:T(8,128)(2,1)S(1)}, bf16[6144,512]{1,0:T(8,128)(2,1)}, u32[]{:S(2)}) %copy-start.1) | copy-done | bytes 6291480
  26.5 14.7 %shard_map.78 = (f32[64,1536]{1,0:T(8,128)S(1)}, f32[64,1536]{1,0:T(8,128)S(1)}, f32[64,1536]{1,0:T(8,128)S(1)}, f32[64,1536]{1,0:T(8,128)S(1)}, f32[64,1536]{1,...) custom-call(s32[5]{0:T(128)S(1)} %stack.35.where_ref, ...), custom_call_target="tpu_custom_call" | custom-call | flops 1000 | bytes 1000 | tf_op jit(solution)/shard_map/pallas_call | solution.py:102
  41.9 1.2 collective-permute-done.1
  46.6 2.9 %collective-permute-start.10 = (f32[64,1536]{1,0:T(8,128)S(1)}, f32[64,1536]{1,0:T(8,128)S(1)}, u32[]{:S(2)}, u32[]{:S(2)}) collective-permute-start(f32[64,1536]{1,0:T(8,128)S(1)} %add.183), channel_id=1, source_target_pairs={{0,2},{1,3},{6,4},{7,5},{2,0},{3,1},{4,6},{5,7},{8,10},{9,11},{14,... | collective-permute-start | bytes 1179656 | tf_op jit(solution)/shard_map/ppermute | solution.py:306
  51.8 7.0 %collective-permute-done.10 = f32[64,1536]{1,0:T(8,128)S(1)} collective-permute-done((f32[64,1536]{1,0:T(8,128)S(1)}, f32[64,1536]{1,0:T(8,128)S(1)}, u32[]{:S(2)}, u32[]{:S(2)}) %collective-permute-start.10) | collective-permute-done | bytes 393248 | tf_op jit(solution)/shard_map/ppermute | solution.py:306
  59.0 1.8 collective-permute-start.11
  60.8 8.8 %collective-permute-done.11 = f32[64,1536]{1,0:T(8,128)S(1)} collective-permute-done((f32[64,1536]{1,0:T(8,128)S(1)}, f32[64,1536]{1,0:T(8,128)S(1)}, u32[]{:S(2)}, u32[]{:S(2)}) %collective-permute-start.11) | collective-permute-done | bytes 393248 | tf_op jit(solution)/shard_map/ppermute | solution.py:306
  69.9 1.7 collective-permute-start.14
  71.6 9.9 %collective-permute-done.14 = f32[64,1536]{1,0:T(8,128)S(1)} collective-permute-done((f32[64,1536]{1,0:T(8,128)S(1)}, f32[64,1536]{1,0:T(8,128)S(1)}, u32[]{:S(2)}, u32[]{:S(2)}) %collective-permute-start.14) | collective-permute-done | bytes 393248 | tf_op jit(solution)/shard_map/ppermute | solution.py:306
  81.8 1.7 collective-permute-start.16
  84.9 8.1 %shard_map.80 = (f32[128,1536]{1,0:T(8,128)S(1)}, f32[128,1536]{1,0:T(8,128)S(1)}) custom-call(bf16[128,3072]{1,0:T(8,128)(2,1)S(1)} %get-tuple-element.358.w_ref.refs_4_, bf16[3072,6144]{1,0:T(8,128)(2,1)} %rho_ref.19), custom_call_target="tpu_custom_call" | custom-call | flops 1000 | bytes 1000 | tf_op jit(solution)/shard_map/pallas_call | solution.py:151
  93.8 1.6 collective-permute-start.20
  95.4 1.5 collective-permute-start.25
  96.9 1.5 collective-permute-start.26
  98.4 8.3 %shard_map.81 = (f32[128,1536]{1,0:T(8,128)S(1)}, f32[128,1536]{1,0:T(8,128)S(1)}) custom-call(bf16[128,3072]{1,0:T(8,128)(2,1)S(1)} %get-tuple-element.358.w_ref.refs_4_, bf16[3072,6144]{1,0:T(8,128)(2,1)} %rho_ref.19), custom_call_target="tpu_custom_call" | custom-call | flops 1000 | bytes 1000 | tf_op jit(solution)/shard_map/pallas_call | solution.py:151
  108.5 6.8 %collective-permute-done.25.refs_1_ = f32[128,1536]{1,0:T(8,128)S(1)} collective-permute-done((f32[128,1536]{1,0:T(8,128)S(1)}, f32[128,1536]{1,0:T(8,128)S(1)}, u32[]{:S(2)}, u32[]{:S(2)}) %collective-permute-start.25) | collective-permute-done | bytes 786464 | tf_op jit(solution)/shard_map/ppermute | solution.py:270
  115.3 1.2 collective-permute-done.26.refs_0_
  117.1 1.5 collective-permute-start.29
  119.9 8.1 %shard_map.83 = (f32[64,3072]{1,0:T(8,128)S(1)}, f32[64,3072]{1,0:T(8,128)S(1)}) custom-call(bf16[128,3072]{1,0:T(8,128)(2,1)S(1)} %get-tuple-element.359.w_ref.refs_5_, bf16[3072,6144]{1,0:T(8,128)(2,1)} %rho_ref.19, f32[128,1536]{1,0:T(8,128)S(1)} %collective-permute-done.26.refs_0_, f32[128,1536]{1,0:T(8,128)S(1)} %collective-permute-done.25.refs_1_), custom_call_target="tpu_custom_call" | custom-call | flops 1000 | bytes 1000 | tf_op jit(solution)/shard_map/pallas_call | solution.py:151
  129.9 5.4 %collective-permute-done.30.refs_1_ = f32[128,1536]{1,0:T(8,128)S(1)} collective-permute-done((f32[128,1536]{1,0:T(8,128)S(1)}, f32[128,1536]{1,0:T(8,128)S(1)}, u32[]{:S(2)}, u32[]{:S(2)}) %collective-permute-start.30) | collective-permute-done | bytes 786464 | tf_op jit(solution)/shard_map/ppermute | solution.py:270
  135.7 1.4 collective-permute-start.34
  137.1 1.5 collective-permute-start.35
  138.6 8.1 %shard_map.84 = (f32[64,3072]{1,0:T(8,128)S(1)}, f32[64,3072]{1,0:T(8,128)S(1)}) custom-call(bf16[128,3072]{1,0:T(8,128)(2,1)S(1)} %get-tuple-element.359.w_ref.refs_5_, bf16[3072,6144]{1,0:T(8,128)(2,1)} %rho_ref.19, f32[128,1536]{1,0:T(8,128)S(1)} %collective-permute-done.29.refs_0_, f32[128,1536]{1,0:T(8,128)S(1)} %collective-permute-done.30.refs_1_), custom_call_target="tpu_custom_call" | custom-call | flops 1000 | bytes 1000 | tf_op jit(solution)/shard_map/pallas_call | solution.py:151
  148.6 4.8 %collective-permute-done.34.refs_1_ = f32[64,3072]{1,0:T(8,128)S(1)} collective-permute-done((f32[64,3072]{1,0:T(8,128)S(1)}, f32[64,3072]{1,0:T(8,128)S(1)}, u32[]{:S(2)}, u32[]{:S(2)}) %collective-permute-start.34) | collective-permute-done | bytes 786464 | tf_op jit(solution)/shard_map/ppermute | solution.py:270
  156.5 1.5 collective-permute-start.40
  159.4 9.0 %shard_map.86 = (f32[64,3072]{1,0:T(8,128)}, f32[64,3072]{1,0:T(8,128)}) custom-call(bf16[128,3072]{1,0:T(8,128)(2,1)S(1)} %get-tuple-element.360.w_ref.refs_6_, bf16[3072,6144]{1,0:T(8,128)(2,1)} %rho_ref.19, f32[128,1536]{1,0:T(8,128)S(1)} %collective-permute-done.26.refs_0_, f32[128,1536]{1,0:T(8,128)S(1)} %collective-permute-done.25.refs_1_), custom_call_target="tpu_custom_call" | custom-call | flops 1000 | bytes 1000 | tf_op jit(solution)/shard_map/pallas_call | solution.py:151
  168.7 1.6 collective-permute-done.36.refs_2_
  170.3 1.7 collective-permute-done.39.refs_2_
  173.7 1.5 collective-permute-start.43
  175.2 8.2 %shard_map.87 = (f32[64,3072]{1,0:T(8,128)S(1)}, f32[64,3072]{1,0:T(8,128)S(1)}) custom-call(bf16[128,3072]{1,0:T(8,128)(2,1)S(1)} %get-tuple-element.360.w_ref.refs_6_, bf16[3072,6144]{1,0:T(8,128)(2,1)} %rho_ref.19, f32[128,1536]{1,0:T(8,128)S(1)} %collective-permute-done.29.refs_0_, f32[128,1536]{1,0:T(8,128)S(1)} %collective-permute-done.30.refs_1_), custom_call_target="tpu_custom_call" | custom-call | flops 1000 | bytes 1000 | tf_op jit(solution)/shard_map/pallas_call | solution.py:151
  185.4 1.7 collective-permute-done.41.refs_4_
  187.2 1.2 shard_map.88
  188.4 1.4 copy-done.5
  189.8 1.4 copy-done.7
  191.2 3.5 %shard_map.89 = f32[64,512]{1,0:T(8,128)S(1)} custom-call(s32[1]{0:T(128)} %bitcast.5.first_ref, f32[128,3072]{1,0:T(8,128)S(1)} %copy-done.3, f32[128,3072]{1,0:T(8,128)S(1)} %copy-done.5, f32[128,3072]{1,0:T(8,128)S(1)} %copy-done.7, f32[128,3072]{1,0:T(8,128)S(1)} %get-tuple-element.357.refs_3_, bf16[128,3072]{1,0:T(8,128)(2,1)S(1)} %get-tuple-element.358.w_ref.refs_4_, ...), custom_call_target="tpu_custom_call" | custom-call | flops 1000 | bytes 1000 | tf_op jit(solution)/shard_map/pallas_call | solution.py:228
  194.8 8.2 %shard_map.90.refs_0_ = f32[128,3072]{1,0:T(8,128)S(1)} custom-call(bf16[128,3072]{1,0:T(8,128)(2,1)S(1)} %get-tuple-element.365.refs_7_.w_ref, bf16[3072,6144]{1,0:T(8,128)(2,1)} %rho_ref.19), custom_call_target="tpu_custom_call" | custom-call | flops 1000 | bytes 1000 | tf_op jit(solution)/shard_map/pallas_call | solution.py:151
  203.1 1.3 collective-permute-start.44
  204.9 1.7 collective-permute-start.48
  207.1 1.3 collective-permute-start.46
  208.4 8.1 %shard_map.91.refs_1_ = f32[128,3072]{1,0:T(8,128)S(1)} custom-call(bf16[128,3072]{1,0:T(8,128)(2,1)S(1)} %get-tuple-element.365.refs_7_.w_ref, bf16[3072,6144]{1,0:T(8,128)(2,1)} %rho_ref.19), custom_call_target="tpu_custom_call" | custom-call | flops 1000 | bytes 1000 | tf_op jit(solution)/shard_map/pallas_call | solution.py:151
  216.5 2.8 %shard_map.92.refs_0_ = f32[128,6144]{1,0:T(8,128)} custom-call(f32[128,3072]{1,0:T(8,128)S(1)} %shard_map.90.refs_0_, f32[64,3072]{1,0:T(8,128)S(1)} %copy-done.9, f32[64,3072]{1,0:T(8,128)S(1)} %copy-done.11, f32[64,3072]{1,0:T(8,128)} %collective-permute-done.42.refs_3_, f32[64,3072]{1,0:T(8,128)} %collective-permute-done.43.refs_4_), custom_call_target="tpu_custom_call" | custom-call | flops 1000 | bytes 1000 | tf_op jit(solution)/shard_map/pallas_call | solution.py:186
  219.3 4.5 %collective-permute-done.48 = f32[64,128]{1,0:T(8,128)S(1)} collective-permute-done((f32[64,128]{1,0:T(8,128)S(1)}, f32[64,128]{1,0:T(8,128)S(1)}, u32[]{:S(2)}, u32[]{:S(2)}) %collective-permute-start.48) | collective-permute-done | bytes 32800 | tf_op jit(solution)/shard_map/ppermute | solution.py:270
  223.8 1.3 collective-permute-done.47
  225.7 1.6 shard_map.93
  (165 shorter events, 28.1 us)
Async XLA Ops:
  18.2 1.9 collective-permute-start
  20.2 21.6 %collective-permute-start.2 = (f32[64,1536]{1,0:T(8,128)S(1)}, f32[64,1536]{1,0:T(8,128)S(1)}, u32[]{:S(2)}, u32[]{:S(2)}) collective-permute-start(f32[64,1536]{1,0:T(8,128)S(1)} %add.181), channel_id=1, source_target_pairs={{0,2},{1,3},{6,4},{7,5},{2,0},{3,1},{4,6},{5,7},{8,10},{9,11},{14,... | collective-permute-start | bytes 1179656 | tf_op jit(solution)/shard_map/ppermute | solution.py:306
  23.2 22.7 %collective-permute-start.7 = (f32[64,1536]{1,0:T(8,128)S(1)}, f32[64,1536]{1,0:T(8,128)S(1)}, u32[]{:S(2)}, u32[]{:S(2)}) collective-permute-start(f32[64,1536]{1,0:T(8,128)S(1)} %get-tuple-element.194), channel_id=1, source_target_pairs={{0,1},{1,0},{2,3},{3,2},{4,5},{5,4},{6,7},{7,6},{8,9},{9,8},{10,11... | collective-permute-start | bytes 1179656 | tf_op jit(solution)/shard_map/ppermute | solution.py:273
  23.2 23.4 %collective-permute-start.5 = (f32[64,1536]{1,0:T(8,128)S(1)}, f32[64,1536]{1,0:T(8,128)}, u32[]{:S(2)}, u32[]{:S(2)}) collective-permute-start(f32[64,1536]{1,0:T(8,128)S(1)} %get-tuple-element.196), channel_id=1, source_target_pairs={{0,1},{1,0},{2,3},{3,2},{4,5},{5,4},{6,7},{7,6},{8,9},{9,8},{10,11... | collective-permute-start | bytes 1179656 | tf_op jit(solution)/shard_map/ppermute | solution.py:273
  23.7 26.9 %collective-permute-start.3 = (f32[64,1536]{1,0:T(8,128)S(1)}, f32[64,1536]{1,0:T(8,128)}, u32[]{:S(2)}, u32[]{:S(2)}) collective-permute-start(f32[64,1536]{1,0:T(8,128)S(1)} %get-tuple-element.198), channel_id=1, source_target_pairs={{0,1},{1,0},{2,3},{3,2},{4,5},{5,4},{6,7},{7,6},{8,9},{9,8},{10,11... | collective-permute-start | bytes 1179656 | tf_op jit(solution)/shard_map/ppermute | solution.py:273
  41.2 1.9 collective-permute-start.1
  41.8 4.3 %collective-permute-start.6 = (f32[64,1536]{1,0:T(8,128)S(1)}, f32[64,1536]{1,0:T(8,128)S(1)}, u32[]{:S(2)}, u32[]{:S(2)}) collective-permute-start(f32[64,1536]{1,0:T(8,128)S(1)} %get-tuple-element.205), channel_id=1, source_target_pairs={{0,1},{1,0},{2,3},{3,2},{4,5},{5,4},{6,7},{7,6},{8,9},{9,8},{10,11... | collective-permute-start | bytes 1179656 | tf_op jit(solution)/shard_map/ppermute | solution.py:273
  43.1 7.4 %collective-permute-start.4 = (f32[64,1536]{1,0:T(8,128)S(1)}, f32[64,1536]{1,0:T(8,128)S(1)}, u32[]{:S(2)}, u32[]{:S(2)}) collective-permute-start(f32[64,1536]{1,0:T(8,128)S(1)} %get-tuple-element.207), channel_id=1, source_target_pairs={{0,1},{1,0},{2,3},{3,2},{4,5},{5,4},{6,7},{7,6},{8,9},{9,8},{10,11... | collective-permute-start | bytes 1179656 | tf_op jit(solution)/shard_map/ppermute | solution.py:273
  45.9 5.8 %collective-permute-start.9 = (f32[64,1536]{1,0:T(8,128)S(1)}, f32[64,1536]{1,0:T(8,128)S(1)}, u32[]{:S(2)}, u32[]{:S(2)}) collective-permute-start(f32[64,1536]{1,0:T(8,128)S(1)} %get-tuple-element.209), channel_id=1, source_target_pairs={{0,1},{1,0},{2,3},{3,2},{4,5},{5,4},{6,7},{7,6},{8,9},{9,8},{10,11... | collective-permute-start | bytes 1179656 | tf_op jit(solution)/shard_map/ppermute | solution.py:273
  46.0 5.7 %collective-permute-start.8 = (f32[64,1536]{1,0:T(8,128)S(1)}, f32[64,1536]{1,0:T(8,128)S(1)}, u32[]{:S(2)}, u32[]{:S(2)}) collective-permute-start(f32[64,1536]{1,0:T(8,128)S(1)} %add_select_fusion.15), channel_id=1, source_target_pairs={{2,4},{3,5},{4,2},{5,3},{0,1},{1,0},{6,7},{7,6},{10,12},{11,13},{1... | collective-permute-start | bytes 1179656 | tf_op jit(solution)/shard_map/ppermute | solution.py:306
  46.6 12.2 %collective-permute-start.10 = (f32[64,1536]{1,0:T(8,128)S(1)}, f32[64,1536]{1,0:T(8,128)S(1)}, u32[]{:S(2)}, u32[]{:S(2)}) collective-permute-start(f32[64,1536]{1,0:T(8,128)S(1)} %add.183), channel_id=1, source_target_pairs={{0,2},{1,3},{6,4},{7,5},{2,0},{3,1},{4,6},{5,7},{8,10},{9,11},{14,... | collective-permute-start | bytes 1179656 | tf_op jit(solution)/shard_map/ppermute | solution.py:306
  59.0 10.6 %collective-permute-start.11 = (f32[64,1536]{1,0:T(8,128)S(1)}, f32[64,1536]{1,0:T(8,128)S(1)}, u32[]{:S(2)}, u32[]{:S(2)}) collective-permute-start(f32[64,1536]{1,0:T(8,128)S(1)} %broadcast_select_fusion.13), channel_id=1, source_target_pairs={{0,2},{1,3},{6,4},{7,5},{2,0},{3,1},{4,6},{5,7},{8,10},{9,11},{14,... | collective-permute-start | bytes 1179656 | tf_op jit(solution)/shard_map/ppermute | solution.py:306
  60.8 9.0 %collective-permute-start.12 = (f32[64,1536]{1,0:T(8,128)S(1)}, f32[64,1536]{1,0:T(8,128)S(1)}, u32[]{:S(2)}, u32[]{:S(2)}) collective-permute-start(f32[64,1536]{1,0:T(8,128)S(1)} %add_select_fusion.13), channel_id=1, source_target_pairs={{2,4},{3,5},{4,2},{5,3},{0,1},{1,0},{6,7},{7,6},{10,12},{11,13},{1... | collective-permute-start | bytes 1179656 | tf_op jit(solution)/shard_map/ppermute | solution.py:306
  69.6 2.0 collective-permute-start.15
  69.9 11.6 %collective-permute-start.14 = (f32[64,1536]{1,0:T(8,128)S(1)}, f32[64,1536]{1,0:T(8,128)S(1)}, u32[]{:S(2)}, u32[]{:S(2)}) collective-permute-start(f32[64,1536]{1,0:T(8,128)S(1)} %broadcast_select_fusion.11), channel_id=1, source_target_pairs={{0,2},{1,3},{6,4},{7,5},{2,0},{3,1},{4,6},{5,7},{8,10},{9,11},{14,... | collective-permute-start | bytes 1179656 | tf_op jit(solution)/shard_map/ppermute | solution.py:306
  71.6 10.0 %collective-permute-start.13 = (f32[64,1536]{1,0:T(8,128)S(1)}, f32[64,1536]{1,0:T(8,128)S(1)}, u32[]{:S(2)}, u32[]{:S(2)}) collective-permute-start(f32[64,1536]{1,0:T(8,128)S(1)} %add_select_fusion.11), channel_id=1, source_target_pairs={{2,4},{3,5},{4,2},{5,3},{0,1},{1,0},{6,7},{7,6},{10,12},{11,13},{1... | collective-permute-start | bytes 1179656 | tf_op jit(solution)/shard_map/ppermute | solution.py:306
  81.5 2.0 collective-permute-start.18
  81.8 11.6 %collective-permute-start.16 = (f32[64,1536]{1,0:T(8,128)S(1)}, f32[64,1536]{1,0:T(8,128)S(1)}, u32[]{:S(2)}, u32[]{:S(2)}) collective-permute-start(f32[64,1536]{1,0:T(8,128)S(1)} %broadcast_select_fusion.9), channel_id=1, source_target_pairs={{0,2},{1,3},{6,4},{7,5},{2,0},{3,1},{4,6},{5,7},{8,10},{9,11},{14,... | collective-permute-start | bytes 1179656 | tf_op jit(solution)/shard_map/ppermute | solution.py:306
  83.5 10.1 %collective-permute-start.17 = (f32[64,1536]{1,0:T(8,128)S(1)}, f32[64,1536]{1,0:T(8,128)S(1)}, u32[]{:S(2)}, u32[]{:S(2)}) collective-permute-start(f32[64,1536]{1,0:T(8,128)S(1)} %add_select_fusion.9), channel_id=1, source_target_pairs={{2,4},{3,5},{4,2},{5,3},{0,1},{1,0},{6,7},{7,6},{10,12},{11,13},{1... | collective-permute-start | bytes 1179656 | tf_op jit(solution)/shard_map/ppermute | solution.py:306
  93.4 5.0 %collective-permute-start.21 = (f32[64,1536]{1,0:T(8,128)S(1)}, f32[64,1536]{1,0:T(8,128)S(1)}, u32[]{:S(2)}, u32[]{:S(2)}) collective-permute-start(f32[64,1536]{1,0:T(8,128)S(1)} %broadcast_select_fusion.8.refs_1_), channel_id=1, source_target_pairs={{0,1},{1,0},{2,3},{3,2},{4,5},{5,4},{6,7},{7,6},{8,9},{9,8},{10,11... | collective-permute-start | bytes 1179656 | tf_op jit(solution)/shard_map/ppermute | solution.py:273
  93.8 12.9 %collective-permute-start.20 = (f32[64,1536]{1,0:T(8,128)S(1)}, f32[64,1536]{1,0:T(8,128)S(1)}, u32[]{:S(2)}, u32[]{:S(2)}) collective-permute-start(f32[64,1536]{1,0:T(8,128)S(1)} %broadcast_select_fusion.7), channel_id=1, source_target_pairs={{0,2},{1,3},{6,4},{7,5},{2,0},{3,1},{4,6},{5,7},{8,10},{9,11},{14,... | collective-permute-start | bytes 1179656 | tf_op jit(solution)/shard_map/ppermute | solution.py:306
  95.3 11.5 %collective-permute-start.19 = (f32[64,1536]{1,0:T(8,128)S(1)}, f32[64,1536]{1,0:T(8,128)S(1)}, u32[]{:S(2)}, u32[]{:S(2)}) collective-permute-start(f32[64,1536]{1,0:T(8,128)S(1)} %add_select_fusion.7), channel_id=1, source_target_pairs={{2,4},{3,5},{4,2},{5,3},{0,1},{1,0},{6,7},{7,6},{10,12},{11,13},{1... | collective-permute-start | bytes 1179656 | tf_op jit(solution)/shard_map/ppermute | solution.py:306
  95.4 19.9 %collective-permute-start.25 = (f32[128,1536]{1,0:T(8,128)S(1)}, f32[128,1536]{1,0:T(8,128)S(1)}, u32[]{:S(2)}, u32[]{:S(2)}) collective-permute-start(f32[128,1536]{1,0:T(8,128)S(1)} %get-tuple-element.261), channel_id=1, source_target_pairs={{0,8},{8,0},{16,24},{24,16},{1,9},{9,1},{17,25},{25,17},{2,10},{10... | collective-permute-start | bytes 2359304 | tf_op jit(solution)/shard_map/ppermute | solution.py:270
  96.9 19.7 %collective-permute-start.26 = (f32[128,1536]{1,0:T(8,128)S(1)}, f32[128,1536]{1,0:T(8,128)S(1)}, u32[]{:S(2)}, u32[]{:S(2)}) collective-permute-start(f32[128,1536]{1,0:T(8,128)S(1)} %get-tuple-element.262), channel_id=1, source_target_pairs={{0,16},{8,24},{16,0},{24,8},{1,17},{9,25},{17,1},{25,9},{2,18},{10... | collective-permute-start | bytes 2359304 | tf_op jit(solution)/shard_map/ppermute | solution.py:270
  106.7 1.8 collective-permute-start.24
  107.0 21.1 %collective-permute-start.22 = (f32[64,1536]{1,0:T(8,128)S(1)}, f32[64,1536]{1,0:T(8,128)S(1)}, u32[]{:S(2)}, u32[]{:S(2)}) collective-permute-start(f32[64,1536]{1,0:T(8,128)S(1)} %broadcast_select_fusion.5), channel_id=1, source_target_pairs={{0,2},{1,3},{6,4},{7,5},{2,0},{3,1},{4,6},{5,7},{8,10},{9,11},{14,... | collective-permute-start | bytes 1179656 | tf_op jit(solution)/shard_map/ppermute | solution.py:306
  108.0 20.3 %collective-permute-start.23 = (f32[64,1536]{1,0:T(8,128)S(1)}, f32[64,1536]{1,0:T(8,128)S(1)}, u32[]{:S(2)}, u32[]{:S(2)}) collective-permute-start(f32[64,1536]{1,0:T(8,128)S(1)} %add_select_fusion.5), channel_id=1, source_target_pairs={{2,4},{3,5},{4,2},{5,3},{0,1},{1,0},{6,7},{7,6},{10,12},{11,13},{1... | collective-permute-start | bytes 1179656 | tf_op jit(solution)/shard_map/ppermute | solution.py:306
  116.5 18.8 %collective-permute-start.30 = (f32[128,1536]{1,0:T(8,128)S(1)}, f32[128,1536]{1,0:T(8,128)S(1)}, u32[]{:S(2)}, u32[]{:S(2)}) collective-permute-start(f32[128,1536]{1,0:T(8,128)S(1)} %get-tuple-element.284), channel_id=1, source_target_pairs={{0,8},{8,0},{16,24},{24,16},{1,9},{9,1},{17,25},{25,17},{2,10},{10... | collective-permute-start | bytes 2359304 | tf_op jit(solution)/shard_map/ppermute | solution.py:270
  117.1 18.6 %collective-permute-start.29 = (f32[128,1536]{1,0:T(8,128)S(1)}, f32[128,1536]{1,0:T(8,128)S(1)}, u32[]{:S(2)}, u32[]{:S(2)}) collective-permute-start(f32[128,1536]{1,0:T(8,128)S(1)} %get-tuple-element.285), channel_id=1, source_target_pairs={{0,16},{8,24},{16,0},{24,8},{1,17},{9,25},{17,1},{25,9},{2,18},{10... | collective-permute-start | bytes 2359304 | tf_op jit(solution)/shard_map/ppermute | solution.py:270
  128.2 1.8 collective-permute-start.31
  128.4 18.4 %collective-permute-start.28 = (f32[64,1536]{1,0:T(8,128)S(1)}, f32[64,1536]{1,0:T(8,128)S(1)}, u32[]{:S(2)}, u32[]{:S(2)}) collective-permute-start(f32[64,1536]{1,0:T(8,128)S(1)} %broadcast_select_fusion.3), channel_id=1, source_target_pairs={{0,2},{1,3},{6,4},{7,5},{2,0},{3,1},{4,6},{5,7},{8,10},{9,11},{14,... | collective-permute-start | bytes 1179656 | tf_op jit(solution)/shard_map/ppermute | solution.py:306
  128.7 18.2 %collective-permute-start.27 = (f32[64,1536]{1,0:T(8,128)S(1)}, f32[64,1536]{1,0:T(8,128)S(1)}, u32[]{:S(2)}, u32[]{:S(2)}) collective-permute-start(f32[64,1536]{1,0:T(8,128)S(1)} %add_select_fusion.3), channel_id=1, source_target_pairs={{2,4},{3,5},{4,2},{5,3},{0,1},{1,0},{6,7},{7,6},{10,12},{11,13},{1... | collective-permute-start | bytes 1179656 | tf_op jit(solution)/shard_map/ppermute | solution.py:306
  135.7 17.7 %collective-permute-start.34 = (f32[64,3072]{1,0:T(8,128)S(1)}, f32[64,3072]{1,0:T(8,128)S(1)}, u32[]{:S(2)}, u32[]{:S(2)}) collective-permute-start(f32[64,3072]{1,0:T(8,128)S(1)} %get-tuple-element.306), channel_id=1, source_target_pairs={{0,8},{8,0},{16,24},{24,16},{1,9},{9,1},{17,25},{25,17},{2,10},{10... | collective-permute-start | bytes 2359304 | tf_op jit(solution)/shard_map/ppermute | solution.py:270
  137.1 17.3 %collective-permute-start.35 = (f32[64,3072]{1,0:T(8,128)S(1)}, f32[64,3072]{1,0:T(8,128)S(1)}, u32[]{:S(2)}, u32[]{:S(2)}) collective-permute-start(f32[64,3072]{1,0:T(8,128)S(1)} %get-tuple-element.307), channel_id=1, source_target_pairs={{0,16},{8,24},{16,0},{24,8},{1,17},{9,25},{17,1},{25,9},{2,18},{10... | collective-permute-start | bytes 2359304 | tf_op jit(solution)/shard_map/ppermute | solution.py:270
  146.8 1.8 collective-permute-start.33
  147.0 21.5 %collective-permute-start.32 = (f32[64,1536]{1,0:T(8,128)S(1)}, f32[64,1536]{1,0:T(8,128)S(1)}, u32[]{:S(2)}, u32[]{:S(2)}) collective-permute-start(f32[64,1536]{1,0:T(8,128)S(1)} %add_select_fusion.2), channel_id=1, source_target_pairs={{0,2},{1,3},{6,4},{7,5},{2,0},{3,1},{4,6},{5,7},{8,10},{9,11},{14,... | collective-permute-start | bytes 1179656 | tf_op jit(solution)/shard_map/ppermute | solution.py:306
  147.1 21.5 %collective-permute-start.37 = (f32[64,1536]{1,0:T(8,128)S(1)}, f32[64,1536]{1,0:T(8,128)S(1)}, u32[]{:S(2)}, u32[]{:S(2)}) collective-permute-start(f32[64,1536]{1,0:T(8,128)S(1)} %add_select_fusion.1), channel_id=1, source_target_pairs={{2,4},{3,5},{4,2},{5,3},{0,1},{1,0},{6,7},{7,6},{10,12},{11,13},{1... | collective-permute-start | bytes 1179656 | tf_op jit(solution)/shard_map/ppermute | solution.py:306
  155.3 16.6 %collective-permute-start.39 = (f32[64,3072]{1,0:T(8,128)S(1)}, f32[64,3072]{1,0:T(8,128)S(1)}, u32[]{:S(2)}, u32[]{:S(2)}) collective-permute-start(f32[64,3072]{1,0:T(8,128)S(1)} %get-tuple-element.320), channel_id=1, source_target_pairs={{0,8},{8,0},{16,24},{24,16},{1,9},{9,1},{17,25},{25,17},{2,10},{10... | collective-permute-start | bytes 2359304 | tf_op jit(solution)/shard_map/ppermute | solution.py:270
  156.5 16.4 %collective-permute-start.40 = (f32[64,3072]{1,0:T(8,128)S(1)}, f32[64,3072]{1,0:T(8,128)S(1)}, u32[]{:S(2)}, u32[]{:S(2)}) collective-permute-start(f32[64,3072]{1,0:T(8,128)S(1)} %get-tuple-element.321), channel_id=1, source_target_pairs={{0,16},{8,24},{16,0},{24,8},{1,17},{9,25},{17,1},{25,9},{2,18},{10... | collective-permute-start | bytes 2359304 | tf_op jit(solution)/shard_map/ppermute | solution.py:270
  168.6 16.6 %collective-permute-start.38 = (f32[64,1536]{1,0:T(8,128)S(1)}, f32[64,1536]{1,0:T(8,128)S(1)}, u32[]{:S(2)}, u32[]{:S(2)}) collective-permute-start(f32[64,1536]{1,0:T(8,128)S(1)} %add_select_fusion), channel_id=1, source_target_pairs={{0,2},{1,3},{6,4},{7,5},{2,0},{3,1},{4,6},{5,7},{8,10},{9,11},{14,... | collective-permute-start | bytes 1179656 | tf_op jit(solution)/shard_map/ppermute | solution.py:306
  172.9 30.1 %collective-permute-start.42 = (f32[64,3072]{1,0:T(8,128)}, f32[64,3072]{1,0:T(8,128)}, u32[]{:S(2)}, u32[]{:S(2)}) collective-permute-start(f32[64,3072]{1,0:T(8,128)} %get-tuple-element.338), channel_id=1, source_target_pairs={{0,8},{8,0},{16,24},{24,16},{1,9},{9,1},{17,25},{25,17},{2,10},{10... | collective-permute-start | bytes 2359304 | tf_op jit(solution)/shard_map/ppermute | solution.py:270
  173.7 29.3 %collective-permute-start.43 = (f32[64,3072]{1,0:T(8,128)}, f32[64,3072]{1,0:T(8,128)}, u32[]{:S(2)}, u32[]{:S(2)}) collective-permute-start(f32[64,3072]{1,0:T(8,128)} %get-tuple-element.339), channel_id=1, source_target_pairs={{0,16},{8,24},{16,0},{24,8},{1,17},{9,25},{17,1},{25,9},{2,18},{10... | collective-permute-start | bytes 2359304 | tf_op jit(solution)/shard_map/ppermute | solution.py:270
  185.2 1.9 collective-permute-start.41
  203.1 22.7 %collective-permute-start.44 = (f32[64,3072]{1,0:T(8,128)S(1)}, f32[64,3072]{1,0:T(8,128)S(1)}, u32[]{:S(2)}, u32[]{:S(2)}) collective-permute-start(f32[64,3072]{1,0:T(8,128)S(1)} %copy-done.19), channel_id=1, source_target_pairs={{0,8},{8,0},{16,24},{24,16},{1,9},{9,1},{17,25},{25,17},{2,10},{10... | collective-permute-start | bytes 2359304 | tf_op jit(solution)/shard_map/ppermute | solution.py:270
  204.4 21.3 %collective-permute-start.45 = (f32[64,3072]{1,0:T(8,128)S(1)}, f32[64,3072]{1,0:T(8,128)S(1)}, u32[]{:S(2)}, u32[]{:S(2)}) collective-permute-start(f32[64,3072]{1,0:T(8,128)S(1)} %copy-done.17), channel_id=1, source_target_pairs={{0,16},{8,24},{16,0},{24,8},{1,17},{9,25},{17,1},{25,9},{2,18},{10... | collective-permute-start | bytes 2359304 | tf_op jit(solution)/shard_map/ppermute | solution.py:270
  204.9 18.9 %collective-permute-start.48 = (f32[64,128]{1,0:T(8,128)S(1)}, f32[64,128]{1,0:T(8,128)S(1)}, u32[]{:S(2)}, u32[]{:S(2)}) collective-permute-start(f32[64,128]{1,0:T(8,128)S(1)} %get-tuple-element.380), channel_id=1, source_target_pairs={{0,24},{8,16},{16,8},{24,0},{1,25},{9,17},{17,9},{25,1},{2,26},{10... | collective-permute-start | bytes 98312 | tf_op jit(solution)/shard_map/ppermute | solution.py:270
  206.6 18.5 %collective-permute-start.47 = (f32[64,128]{1,0:T(8,128)S(1)}, f32[64,128]{1,0:T(8,128)S(1)}, u32[]{:S(2)}, u32[]{:S(2)}) collective-permute-start(f32[64,128]{1,0:T(8,128)S(1)} %get-tuple-element.381), channel_id=1, source_target_pairs={{0,16},{8,24},{16,0},{24,8},{1,17},{9,25},{17,1},{25,9},{2,18},{10... | collective-permute-start | bytes 98312 | tf_op jit(solution)/shard_map/ppermute | solution.py:270
  207.1 18.0 %collective-permute-start.46 = (f32[64,128]{1,0:T(8,128)S(1)}, f32[64,128]{1,0:T(8,128)S(1)}, u32[]{:S(2)}, u32[]{:S(2)}) collective-permute-start(f32[64,128]{1,0:T(8,128)S(1)} %get-tuple-element.382), channel_id=1, source_target_pairs={{0,8},{8,0},{16,24},{24,16},{1,9},{9,1},{17,25},{25,17},{2,10},{10... | collective-permute-start | bytes 98312 | tf_op jit(solution)/shard_map/ppermute | solution.py:270
  (25 other events, 115.4 us)

commit v3 on v2

--- a/solution.py
+++ b/solution.py
@@ -7,12 +7,13 @@
 from jax.experimental.pallas import tpu as pltpu
 from jax.sharding import PartitionSpec as P
 
-VMEM = 18 << 20
+VMEM = 26 << 20
 COST = pl.CostEstimate(flops=1000, bytes_accessed=1000, transcendentals=0)
 
 
 BLOCK = 512
-WIDE = 768
+CHUNKS = 4
+WIDE = 1536
 CUTS = (1, 1)
 STEPS = 2
 
@@ -117,14 +118,16 @@
     )(where, subspace, rho)
 
 
-def panel(weighted, rho, step, steps, outputs, adds):
+def panel(weighted, rho, step, steps, outputs, adds, before=None):
+    whole = before is not None
+    before = before or []
     rows, pairs = weighted.shape
     piece = rho.shape[1] // 2 // steps
     block = fitting(piece, WIDE)
     turns = piece // block
 
     def kernel(w_ref, rho_ref, *refs):
-        more, outs = refs[: len(adds)], refs[len(adds) :]
+        more, outs = refs[: len(adds)], refs[len(adds) + len(before) :]
         side, turn = pl.program_id(0), pl.program_id(1)
         found = jnp.dot(w_ref[...], rho_ref[...], preferred_element_type=jnp.float32)
         for s in (0, 1):
@@ -142,7 +145,7 @@
 
     def of_output(sides):
         if len(sides) == 2:
-            return lambda s, t: (0, s * turns + t)
+            return lambda s, t: (0, ((step + s * steps) if whole else s) * turns + t)
         return (lambda s, t: (0, t + s * (turns - 1 - t))) if sides[0] == 0 else (lambda s, t: (0, s * t))
 
     def of_add(side, r):
@@ -151,7 +154,8 @@
     return pl.pallas_call(
         kernel,
         out_shape=[
-            jax.ShapeDtypeStruct((b - a, piece * len(sides)), jnp.float32) for (a, b), sides in outputs
+            jax.ShapeDtypeStruct((b - a, rho.shape[1] if whole else piece * len(sides)), jnp.float32)
+            for (a, b), sides in outputs
         ],
         grid=(2, turns),
         in_specs=[
@@ -161,11 +165,13 @@
         + [
             pl.BlockSpec((outputs[at][0][1] - outputs[at][0][0], block), of_add(side, r))
             for at, side, _, r in adds
-        ],
+        ]
+        + [pl.BlockSpec(memory_space=pl.ANY)] * len(before),
+        input_output_aliases={2 + len(adds) + at: at for at in range(len(before))},
         out_specs=[pl.BlockSpec((b - a, block), of_output(sides)) for (a, b), sides in outputs],
         compiler_params=pltpu.CompilerParams(vmem_limit_bytes=VMEM),
         cost_estimate=COST,
-    )(weighted, rho, *[a for _, _, a, _ in adds])
+    )(weighted, rho, *[a for _, _, a, _ in adds], *before)
 
 
 def assemble(chi, own, step, steps, low, high):
@@ -197,22 +203,21 @@
     )(*before, own, *arrived)
 
 
-def small_product(first, count, sums, weighted, stands):
-    pairs = sums[0].shape[1]
-    total = sum(x.shape[0] for x in sums)
+def small_product(mine, weighted, stands):
+    count, pairs = mine[0].shape
+    total = sum(x.shape[0] for x in weighted)
     block = fitting(pairs, 512)
-    n = len(sums)
-
-    def kernel(first_ref, *refs):
-        out, rows, others = refs[2 * n :]
-        for group, to in ((refs[:n], rows), (refs[n : 2 * n], others)):
-            for ref, at in zip(group, stands):
-                size = ref.shape[0] // len(at)
-                for k, start in enumerate(at):
-                    to[pl.ds(start, size), :] = ref[pl.ds(k * size, size), :]
-        mine = rows[pl.ds(pl.multiple_of(first_ref[0], 8), count), :]
-        top = mine.astype(jnp.bfloat16)
-        rest = (mine - top.astype(jnp.float32)).astype(jnp.bfloat16)
+    n = len(mine)
+
+    def kernel(*refs):
+        out, others = refs[-2:]
+        for ref, at in zip(refs[n:-2], stands):
+            size = ref.shape[0] // len(at)
+            for k, start in enumerate(at):
+                others[pl.ds(start, size), :] = ref[pl.ds(k * size, size), :]
+        rows = sum((ref[...] for ref in refs[1:n]), refs[0][...])
+        top = rows.astype(jnp.bfloat16)
+        rest = (rows - top.astype(jnp.float32)).astype(jnp.bfloat16)
         dims = (((1,), (1,)), ((), ()))
         found = lax.dot_general(top, others[...], dims, preferred_element_type=jnp.float32)
         found = found + lax.dot_general(rest, others[...], dims, preferred_element_type=jnp.float32)
@@ -228,16 +233,13 @@
     return pl.pallas_call(
         kernel,
         out_shape=jax.ShapeDtypeStruct((count, total), jnp.float32),
-        grid_spec=pltpu.PrefetchScalarGridSpec(
-            num_scalar_prefetch=1,
-            grid=(pairs // block,),
-            in_specs=[pl.BlockSpec((x.shape[0], block), lambda i, at: (0, i)) for x in (*sums, *weighted)],
-            out_specs=pl.BlockSpec((count, total), lambda i, at: (0, 0)),
-            scratch_shapes=[pltpu.VMEM((total, block), jnp.float32), pltpu.VMEM((total, block), jnp.bfloat16)],
-        ),
+        grid=(pairs // block,),
+        in_specs=[pl.BlockSpec((x.shape[0], block), lambda i: (0, i)) for x in (*mine, *weighted)],
+        out_specs=pl.BlockSpec((count, total), lambda i: (0, 0)),
+        scratch_shapes=[pltpu.VMEM((total, block), jnp.bfloat16)],
         compiler_params=pltpu.CompilerParams(vmem_limit_bytes=VMEM),
         cost_estimate=COST,
-    )(first, *sums, *weighted)
+    )(*mine, *weighted)
 
 
 def body(rho, subspace, band_valence, band_conduction, occupied, energies):
@@ -393,23 +395,47 @@
         lambda *a: pair_weights(*a, pairs * q)[None, :], band_valence, band_conduction, occupied, energies
     )
 
-    def gather(group):
+    def rank(offset):
+        return offset[0] * inner + offset[1]
+
+    def place(block):
+        return (block // inner - my_outer) % outer * inner + (block % inner - my_inner) % inner
+
+    stands = [
+        [rank(o) * rows for o in mixed],
+        [rank(o) * rows for o in straight],
+        [rank(o) * rows + half for o in straight],
+        [0],
+    ]
+    slab_rows = vectors // slabs
+    first_row = slab * slab_rows
+    mine = place(first_row // rows) * rows + first_row % rows
+
+    def gather(group, stands):
         flat = [x for part in group for x in part.value]
-
-        half = flat[0].shape[0]
+        half_group = flat[0].shape[0]
+        size = 2 * half_group // len(stands)
+        starts = [a + b for a in stands for b in range(0, size, slab_rows)]
 
         def kernel(flags, weight, *flat):
             upper, lower = [], []
-            for mine, other in zip(flat[::2], flat[1::2]):
-                upper.append(jnp.where(flags[0] == 0, mine, other))
-                lower.append(jnp.where(flags[0] == 0, other, mine))
+            for one, other in zip(flat[::2], flat[1::2]):
+                upper.append(jnp.where(flags[0] == 0, one, other))
+                lower.append(jnp.where(flags[0] == 0, other, one))
             sums = jnp.concatenate([jnp.concatenate(upper, 1), jnp.concatenate(lower, 1)])
-            return (sums * weight).astype(jnp.bfloat16), sums
+            picked = jnp.zeros((slab_rows, pairs), jnp.float32)
+            for n in range(len(starts)):
+                rows_n = sums[n * slab_rows : (n + 1) * slab_rows]
+                picked = jnp.where(flags[1 + n] != 0, rows_n, picked)
+            return (sums * weight).astype(jnp.bfloat16), picked
 
         def work(*flat):
-            shape = (2 * half, pairs)
-            out = [jax.ShapeDtypeStruct(shape, jnp.bfloat16), jax.ShapeDtypeStruct(shape, jnp.float32)]
-            return small(kernel, out, core[None], weight, *flat)
+            out = [
+                jax.ShapeDtypeStruct((2 * half_group, pairs), jnp.bfloat16),
+                jax.ShapeDtypeStruct((slab_rows, pairs), jnp.float32),
+            ]
+            flags = jnp.stack([core] + [(mine == n).astype(jnp.int32) for n in starts])
+            return small(kernel, out, flags, weight, *flat)
 
         return run(work, *flat)
 
@@ -419,7 +445,7 @@
     advance(mixed_parts, low_parts)
     advance(mixed_parts, low_parts, high_parts[:1])
     finish(mixed_parts)
-    w_mixed, sum_mixed = gather(mixed_parts)
+    w_mixed, sum_mixed = gather(mixed_parts, stands[0])
 
     def send_all(values, before):
         flat = run(lambda *v: v, *[v for v, _ in values], *before)
@@ -453,72 +479,59 @@
             adds += [(at, side, x) for x in got or []]
         ends = [(at * half, (at + 1) * half) for at in range(len(straight))]
 
-        def work(w, *extra):
-            return panel(
-                w, rho, k, steps, [(e, (0, 1)) for e in ends], [(o, s, x, part) for (o, s, _), x in zip(adds, extra)]
-            )
-
-        return run(work, w, *[x for _, _, x in adds])
+        extra = [x for _, _, x in adds]
+
+        def work(w, *more):
+            given = [(o, s, x, part) for (o, s, _), x in zip(adds, more)]
+            return panel(w, rho, k, steps, [(e, (0, 1)) for e in ends], given)
+
+        return run(work, w, *extra)
 
     finish(low_parts)
-    w_low, sum_low = gather(low_parts)
+    w_low, sum_low = gather(low_parts, stands[1])
     low_arrived, high_arrived = [], []
     for k in range(steps):
         out = straight_panel(w_low, k, 0)
-        if k:
-            advance(high_parts, own_parts)
-        else:
-            advance(high_parts, own_parts)
+        advance(high_parts, own_parts)
         before = send_all(list(zip(out, straight)), before)
         low_arrived.append(before)
 
-    def rank(offset):
-        return offset[0] * inner + offset[1]
-
-    def place(block):
-        return (block // inner - my_outer) % outer * inner + (block % inner - my_inner) % inner
-
-    stands = [
-        [rank(o) * rows for o in mixed],
-        [rank(o) * rows for o in straight],
-        [rank(o) * rows + half for o in straight],
-        [0],
-    ]
-    slab_rows = vectors // slabs
-    first_row = slab * slab_rows
-
-    def local_sums(*groups):
-        mine = place(first_row // rows) * rows + first_row % rows
-        local = small_product(mine[None], slab_rows, groups[:4], groups[4:], stands)
-        return [local[:, n * rows : (n + 1) * rows] for n in range(q)]
-
     finish(high_parts)
-    w_high, sum_high = gather(high_parts)
+    w_high, sum_high = gather(high_parts, stands[2])
     own_sums = []
+
+    def own_panel(k):
+        return run(lambda w: panel(w, rho, k, steps, [((0, rows), (0, 1))], []), w_own)
+
     for k in range(steps):
         out = straight_panel(w_high, k, 1)
         if k == 0:
             advance(own_parts)
         else:
             finish(own_parts)
-            w_own, sum_own = gather(own_parts)
-            local = run(local_sums, sum_mixed, sum_low, sum_high, sum_own, w_mixed, w_low, w_high, w_own)
-            arrivals = [send_pair(local[n], (n // inner, n % inner)) for n in range(1, q)]
-            own_sums += run(lambda w: panel(w, rho, 0, steps, [((0, rows), (0, 1))], []), w_own)
+            w_own, sum_own = gather(own_parts, stands[3])
+            own_sums += own_panel(0)
         before = send_all(list(zip(out, straight)), before)
         high_arrived.append(before)
 
+    local = run(
+        lambda *x: small_product(x[:4], x[4:], stands),
+        *(sum_mixed, sum_low, sum_high, sum_own, w_mixed, w_low, w_high, w_own),
+    )
+    blocks = [local[:, n * rows : (n + 1) * rows] for n in range(q)]
+    arrivals = [send_pair(blocks[n], (n // inner, n % inner)) for n in range(1, q)]
     for k in range(1, steps):
-        own_sums += run(lambda w: panel(w, rho, k, steps, [((0, rows), (0, 1))], []), w_own)
+        own_sums += own_panel(k)
     chi = None
     for k in range(steps):
+
         def work(own, *got, chi=chi):
             n = len(low_arrived[k])
             return assemble(chi, own, k, steps, list(got[:n]), list(got[n:]))
 
         chi = run(work, own_sums[k], *low_arrived[k], *high_arrived[k])
         if k == steps - 2:
-            subspace_chi = run(lambda *x: sum(x[1:], x[0]), local[0], *arrivals)
+            subspace_chi = run(lambda *x: sum(x[1:], x[0]), blocks[0], *arrivals)
     return chi, subspace_chi
 
 

time: 228 us -> 224 us (0.982)
  other arithmetic: 4.6 us -> 13.7 us
  waiting for transfers between devices: 61.4 us -> 53.6 us
  local copies, waits for them, and re-layouts: 15.5 us -> 9.18 us
    unnamed x48 -> x42, local copies, waits for them, and re-layouts: 15.4 us -> 9.06 us
    select_n x16, other arithmetic: 0.78 us -> 6.49 us  [receive(): self.total = run(lambda a, b: jnp.where(here, a + b, a), total, got)]
    ppermute x15, waiting for transfers between devices: 27.1 us -> 22.7 us  [send_pair(): return lax.ppermute(x, 'pair', perm)]
    ppermute x16, waiting for transfers between devices: 8.1 us -> 4.73 us  [send_core(): return lax.ppermute(x, 'slab', [(s, s ^ 1) for s in range(slabs)])]
    pallas_call x4, Pallas kernels: 1.93 us -> 4.28 us  [small(): pl.pallas_call(kernel, out_shape=out_shapes, grid_spec=pltpu.PrefetchScal...]
  transfers between devices with their start and end apart: 49 -> 49, of which waited for: 21 -> 17; matrix products, arithmetic and copies ran while one was open for 3% -> 7% of each run, Pallas kernels for 39% -> 40%
where the time goes in v3:
time: 224 us; the launch traced here: 223 us
  Pallas kernels  105 us (47%)
  waiting for transfers between devices  53.6 us (24%)
  starting transfers between devices  37.8 us (17%)
  other arithmetic  13.7 us (6%)
  local copies, waits for them, and re-layouts  9.18 us (4%)
  matrix products  2.26 us (1%)
    pallas_call x8, Pallas kernels, panel(): pl.pallas_call(kernel, out_shape=[jax.ShapeDtypeStruct((b - a, rho.shape[...  64.9 us
    pallas_call x2, Pallas kernels, project(): pl.pallas_call(kernel, out_shape=[jax.ShapeDtypeStruct((h, stop - start),...  29.9 us
    ppermute x18, waiting for transfers between devices, exchange(): return lax.ppermute(x, 'slab', perm)  26.1 us
    ppermute x15, waiting for transfers between devices, send_pair(): return lax.ppermute(x, 'pair', perm)  22.7 us
    ppermute x15, starting transfers between devices, send_pair(): return lax.ppermute(x, 'pair', perm)  18 us
    ppermute x18, starting transfers between devices, exchange(): return lax.ppermute(x, 'slab', perm)  16.6 us
    unnamed x42, local copies, waits for them, and re-layouts  9.06 us
    select_n x16, other arithmetic, receive(): self.total = run(lambda a, b: jnp.where(here, a + b, a), total, got)  6.49 us
  transfers between devices with their start and end apart: 49, of which 17 were waited for; matrix products, arithmetic and copies ran while one was open for 7% of the time, Pallas kernels for 40%

profile of v3, /device:TPU:0, one launch (start us, length us, event | category | flops | bytes accessed | tf_op | source)
XLA Modules:
  0.0 223.5 jit_solution(2480590158576321938)
XLA Ops:
  0.8 2.8 %copy-done = bf16[6144,512]{1,0:T(8,128)(2,1)S(1)} copy-done((bf16[6144,512]{1,0:T(8,128)(2,1)S(1)}, bf16[6144,512]{1,0:T(8,128)(2,1)}, u32[]{:S(2)}) %copy-start) | copy-done | bytes 6291480
  3.6 14.9 %shard_map.77 = (f32[64,1536]{1,0:T(8,128)S(1)}, f32[64,1536]{1,0:T(8,128)S(1)}, f32[64,1536]{1,0:T(8,128)S(1)}, f32[64,1536]{1,0:T(8,128)S(1)}, f32[64,1536]{1,...) custom-call(s32[5]{0:T(128)S(1)} %stack.107.where_ref, ...), custom_call_target="tpu_custom_call" | custom-call | flops 1000 | bytes 1000 | tf_op jit(solution)/shard_map/pallas_call | solution.py:103
  19.0 1.3 collective-permute-done
  20.4 3.0 %collective-permute-start.2 = (f32[64,1536]{1,0:T(8,128)S(1)}, f32[64,1536]{1,0:T(8,128)}, u32[]{:S(2)}, u32[]{:S(2)}) collective-permute-start(f32[64,1536]{1,0:T(8,128)S(1)} %add.187), channel_id=1, source_target_pairs={{0,2},{1,3},{6,4},{7,5},{2,0},{3,1},{4,6},{5,7},{8,10},{9,11},{14,... | collective-permute-start | bytes 1179656 | tf_op jit(solution)/shard_map/ppermute | solution.py:308
  24.0 2.8 %copy-done.1 = bf16[6144,512]{1,0:T(8,128)(2,1)S(1)} copy-done((bf16[6144,512]{1,0:T(8,128)(2,1)S(1)}, bf16[6144,512]{1,0:T(8,128)(2,1)}, u32[]{:S(2)}) %copy-start.1) | copy-done | bytes 6291480
  26.8 14.9 %shard_map.78 = (f32[64,1536]{1,0:T(8,128)S(1)}, f32[64,1536]{1,0:T(8,128)S(1)}, f32[64,1536]{1,0:T(8,128)S(1)}, f32[64,1536]{1,0:T(8,128)S(1)}, f32[64,1536]{1,...) custom-call(s32[5]{0:T(128)S(1)} %stack.107.where_ref, ...), custom_call_target="tpu_custom_call" | custom-call | flops 1000 | bytes 1000 | tf_op jit(solution)/shard_map/pallas_call | solution.py:103
  44.2 1.1 fusion.1
  45.3 1.1 fusion
  48.2 2.9 %collective-permute-start.10 = (f32[64,1536]{1,0:T(8,128)S(1)}, f32[64,1536]{1,0:T(8,128)S(1)}, u32[]{:S(2)}, u32[]{:S(2)}) collective-permute-start(f32[64,1536]{1,0:T(8,128)S(1)} %add.189), channel_id=1, source_target_pairs={{0,2},{1,3},{6,4},{7,5},{2,0},{3,1},{4,6},{5,7},{8,10},{9,11},{14,... | collective-permute-start | bytes 1179656 | tf_op jit(solution)/shard_map/ppermute | solution.py:308
  53.0 7.4 %collective-permute-done.10 = f32[64,1536]{1,0:T(8,128)S(1)} collective-permute-done((f32[64,1536]{1,0:T(8,128)S(1)}, f32[64,1536]{1,0:T(8,128)S(1)}, u32[]{:S(2)}, u32[]{:S(2)}) %collective-permute-start.10) | collective-permute-done | bytes 393248 | tf_op jit(solution)/shard_map/ppermute | solution.py:308
  60.5 1.8 collective-permute-start.11
  62.3 8.8 %collective-permute-done.11 = f32[64,1536]{1,0:T(8,128)S(1)} collective-permute-done((f32[64,1536]{1,0:T(8,128)S(1)}, f32[64,1536]{1,0:T(8,128)S(1)}, u32[]{:S(2)}, u32[]{:S(2)}) %collective-permute-start.11) | collective-permute-done | bytes 393248 | tf_op jit(solution)/shard_map/ppermute | solution.py:308
  71.5 1.7 collective-permute-start.14
  73.2 9.9 %collective-permute-done.14 = f32[64,1536]{1,0:T(8,128)S(1)} collective-permute-done((f32[64,1536]{1,0:T(8,128)S(1)}, f32[64,1536]{1,0:T(8,128)S(1)}, u32[]{:S(2)}, u32[]{:S(2)}) %collective-permute-start.14) | collective-permute-done | bytes 393248 | tf_op jit(solution)/shard_map/ppermute | solution.py:308
  84.9 1.6 collective-permute-start.16
  88.3 9.0 %shard_map.80 = (f32[128,1536]{1,0:T(8,128)}, f32[128,1536]{1,0:T(8,128)}) custom-call(bf16[128,3072]{1,0:T(8,128)(2,1)S(1)} %get-tuple-element.361.w_ref.refs_4_, bf16[3072,6144]{1,0:T(8,128)(2,1)} %rho_ref.19), custom_call_target="tpu_custom_call" | custom-call | flops 1000 | bytes 1000 | tf_op jit(solution)/shard_map/pallas_call | solution.py:154
  99.8 1.1 add_select_fusion.7
  101.5 1.5 collective-permute-start.25
  103.0 1.5 collective-permute-start.26
  104.5 7.9 %shard_map.81 = (f32[128,1536]{1,0:T(8,128)S(1)}, f32[128,1536]{1,0:T(8,128)S(1)}) custom-call(bf16[128,3072]{1,0:T(8,128)(2,1)S(1)} %get-tuple-element.361.w_ref.refs_4_, bf16[3072,6144]{1,0:T(8,128)(2,1)} %rho_ref.19), custom_call_target="tpu_custom_call" | custom-call | flops 1000 | bytes 1000 | tf_op jit(solution)/shard_map/pallas_call | solution.py:154
  116.2 2.0 collective-permute-start.22
  118.4 3.1 %collective-permute-done.25.refs_1_ = f32[128,1536]{1,0:T(8,128)S(1)} collective-permute-done((f32[128,1536]{1,0:T(8,128)}, f32[128,1536]{1,0:T(8,128)S(1)}, u32[]{:S(2)}, u32[]{:S(2)}) %collective-permute-start.25) | collective-permute-done | bytes 786464 | tf_op jit(solution)/shard_map/ppermute | solution.py:272
  121.5 1.2 collective-permute-done.26.refs_0_
  123.2 1.5 collective-permute-start.29
  124.8 1.8 shard_map.82
  126.6 8.0 %shard_map.83 = (f32[64,3072]{1,0:T(8,128)S(1)}, f32[64,3072]{1,0:T(8,128)S(1)}) custom-call(bf16[128,3072]{1,0:T(8,128)(2,1)S(1)} %get-tuple-element.362.w_ref.refs_5_, bf16[3072,6144]{1,0:T(8,128)(2,1)} %rho_ref.19, f32[128,1536]{1,0:T(8,128)S(1)} %collective-permute-done.26.refs_0_, f32[128,1536]{1,0:T(8,128)S(1)} %collective-permute-done.25.refs_1_), custom_call_target="tpu_custom_call" | custom-call | flops 1000 | bytes 1000 | tf_op jit(solution)/shard_map/pallas_call | solution.py:154
  134.7 1.1 broadcast_select_fusion.4.refs_1_
  136.0 1.1 add_select_fusion.3
  137.8 3.8 %collective-permute-done.30.refs_1_ = f32[128,1536]{1,0:T(8,128)S(1)} collective-permute-done((f32[128,1536]{1,0:T(8,128)}, f32[128,1536]{1,0:T(8,128)S(1)}, u32[]{:S(2)}, u32[]{:S(2)}) %collective-permute-start.30) | collective-permute-done | bytes 786464 | tf_op jit(solution)/shard_map/ppermute | solution.py:272
  141.9 1.4 collective-permute-start.34
  143.4 1.5 collective-permute-start.35
  144.9 8.0 %shard_map.84 = (f32[64,3072]{1,0:T(8,128)S(1)}, f32[64,3072]{1,0:T(8,128)S(1)}) custom-call(bf16[128,3072]{1,0:T(8,128)(2,1)S(1)} %get-tuple-element.362.w_ref.refs_5_, bf16[3072,6144]{1,0:T(8,128)(2,1)} %rho_ref.19, f32[128,1536]{1,0:T(8,128)S(1)} %collective-permute-done.29.refs_0_, f32[128,1536]{1,0:T(8,128)S(1)} %collective-permute-done.30.refs_1_), custom_call_target="tpu_custom_call" | custom-call | flops 1000 | bytes 1000 | tf_op jit(solution)/shard_map/pallas_call | solution.py:154
  154.8 4.8 %collective-permute-done.34.refs_1_ = f32[64,3072]{1,0:T(8,128)S(1)} collective-permute-done((f32[64,3072]{1,0:T(8,128)S(1)}, f32[64,3072]{1,0:T(8,128)S(1)}, u32[]{:S(2)}, u32[]{:S(2)}) %collective-permute-start.34) | collective-permute-done | bytes 786464 | tf_op jit(solution)/shard_map/ppermute | solution.py:272
  159.5 1.1 collective-permute-done.35.refs_2_
  161.3 1.5 collective-permute-start.40
  163.6 7.9 %shard_map.86 = (f32[64,3072]{1,0:T(8,128)S(1)}, f32[64,3072]{1,0:T(8,128)S(1)}) custom-call(bf16[128,3072]{1,0:T(8,128)(2,1)S(1)} %get-tuple-element.363.w_ref.refs_6_, bf16[3072,6144]{1,0:T(8,128)(2,1)} %rho_ref.19, f32[128,1536]{1,0:T(8,128)S(1)} %collective-permute-done.26.refs_0_, f32[128,1536]{1,0:T(8,128)S(1)} %collective-permute-done.25.refs_1_), custom_call_target="tpu_custom_call" | custom-call | flops 1000 | bytes 1000 | tf_op jit(solution)/shard_map/pallas_call | solution.py:154
  173.4 4.3 %collective-permute-done.39.refs_2_ = f32[64,3072]{1,0:T(8,128)S(1)} collective-permute-done((f32[64,3072]{1,0:T(8,128)S(1)}, f32[64,3072]{1,0:T(8,128)S(1)}, u32[]{:S(2)}, u32[]{:S(2)}) %collective-permute-start.39) | collective-permute-done | bytes 786464 | tf_op jit(solution)/shard_map/ppermute | solution.py:272
  177.7 1.7 collective-permute-start.42
  179.4 1.8 collective-permute-start.43
  181.2 8.0 %shard_map.87 = (f32[64,3072]{1,0:T(8,128)S(1)}, f32[64,3072]{1,0:T(8,128)S(1)}) custom-call(bf16[128,3072]{1,0:T(8,128)(2,1)S(1)} %get-tuple-element.363.w_ref.refs_6_, bf16[3072,6144]{1,0:T(8,128)(2,1)} %rho_ref.19, f32[128,1536]{1,0:T(8,128)S(1)} %collective-permute-done.29.refs_0_, f32[128,1536]{1,0:T(8,128)S(1)} %collective-permute-done.30.refs_1_), custom_call_target="tpu_custom_call" | custom-call | flops 1000 | bytes 1000 | tf_op jit(solution)/shard_map/pallas_call | solution.py:154
  189.3 1.7 collective-permute-done.41.refs_4_
  191.9 8.0 %shard_map.89.refs_0_ = f32[128,3072]{1,0:T(8,128)S(1)} custom-call(bf16[128,3072]{1,0:T(8,128)(2,1)S(1)} %get-tuple-element.365.w_ref.refs_7_, bf16[3072,6144]{1,0:T(8,128)(2,1)} %rho_ref.19), custom_call_target="tpu_custom_call" | custom-call | flops 1000 | bytes 1000 | tf_op jit(solution)/shard_map/pallas_call | solution.py:154
  200.5 3.2 %shard_map.90 = f32[64,512]{1,0:T(8,128)S(1)} custom-call(f32[64,3072]{1,0:T(8,128)S(1)} %copy-done.3, f32[64,3072]{1,0:T(8,128)S(1)} %get-tuple-element.358.refs_1_, f32[64,3072]{1,0:T(8,128)S(1)} %get-tuple-element.359.refs_2_, f32[64,3072]{1,0:T(8,128)S(1)} %get-tuple-element.360.refs_3_, bf16[128,3072]{1,0:T(8,128)(2,1)S(1)} %get-tuple-element.361.w_ref.refs_4_, ...), custom_call_target="tpu_custom_call" | custom-call | flops 1000 | bytes 1000 | tf_op jit(solution)/shard_map/pallas_call | solution.py:233
  203.8 3.0 %collective-permute-start.48 = (f32[64,128]{1,0:T(8,128)S(1)}, f32[64,128]{1,0:T(8,128)S(1)}, u32[]{:S(2)}, u32[]{:S(2)}) collective-permute-start(f32[64,128]{1,0:T(8,128)S(1)} %get-tuple-element.380), channel_id=1, source_target_pairs={{0,24},{8,16},{16,8},{24,0},{1,25},{9,17},{17,9},{25,1},{2,26},{10... | collective-permute-start | bytes 98312 | tf_op jit(solution)/shard_map/ppermute | solution.py:272
  207.5 8.0 %shard_map.91.refs_1_ = f32[128,3072]{1,0:T(8,128)S(1)} custom-call(bf16[128,3072]{1,0:T(8,128)(2,1)S(1)} %get-tuple-element.365.w_ref.refs_7_, bf16[3072,6144]{1,0:T(8,128)(2,1)} %rho_ref.19), custom_call_target="tpu_custom_call" | custom-call | flops 1000 | bytes 1000 | tf_op jit(solution)/shard_map/pallas_call | solution.py:154
  215.5 1.6 shard_map.92.refs_0_
  217.1 3.3 %collective-permute-done.48 = f32[64,128]{1,0:T(8,128)S(1)} collective-permute-done((f32[64,128]{1,0:T(8,128)S(1)}, f32[64,128]{1,0:T(8,128)S(1)}, u32[]{:S(2)}, u32[]{:S(2)}) %collective-permute-start.48) | collective-permute-done | bytes 32800 | tf_op jit(solution)/shard_map/ppermute | solution.py:272
  221.9 1.6 shard_map.93
  (161 shorter events, 28.8 us)
Async XLA Ops:
  18.5 1.9 collective-permute-start
  20.4 21.9 %collective-permute-start.2 = (f32[64,1536]{1,0:T(8,128)S(1)}, f32[64,1536]{1,0:T(8,128)}, u32[]{:S(2)}, u32[]{:S(2)}) collective-permute-start(f32[64,1536]{1,0:T(8,128)S(1)} %add.187), channel_id=1, source_target_pairs={{0,2},{1,3},{6,4},{7,5},{2,0},{3,1},{4,6},{5,7},{8,10},{9,11},{14,... | collective-permute-start | bytes 1179656 | tf_op jit(solution)/shard_map/ppermute | solution.py:308
  23.5 23.0 %collective-permute-start.7 = (f32[64,1536]{1,0:T(8,128)S(1)}, f32[64,1536]{1,0:T(8,128)}, u32[]{:S(2)}, u32[]{:S(2)}) collective-permute-start(f32[64,1536]{1,0:T(8,128)S(1)} %get-tuple-element.194), channel_id=1, source_target_pairs={{0,1},{1,0},{2,3},{3,2},{4,5},{5,4},{6,7},{7,6},{8,9},{9,8},{10,11... | collective-permute-start | bytes 1179656 | tf_op jit(solution)/shard_map/ppermute | solution.py:275
  23.5 24.7 %collective-permute-start.5 = (f32[64,1536]{1,0:T(8,128)S(1)}, f32[64,1536]{1,0:T(8,128)S(1)}, u32[]{:S(2)}, u32[]{:S(2)}) collective-permute-start(f32[64,1536]{1,0:T(8,128)S(1)} %get-tuple-element.196), channel_id=1, source_target_pairs={{0,1},{1,0},{2,3},{3,2},{4,5},{5,4},{6,7},{7,6},{8,9},{9,8},{10,11... | collective-permute-start | bytes 1179656 | tf_op jit(solution)/shard_map/ppermute | solution.py:275
  24.0 27.2 %collective-permute-start.3 = (f32[64,1536]{1,0:T(8,128)S(1)}, f32[64,1536]{1,0:T(8,128)S(1)}, u32[]{:S(2)}, u32[]{:S(2)}) collective-permute-start(f32[64,1536]{1,0:T(8,128)S(1)} %get-tuple-element.198), channel_id=1, source_target_pairs={{0,1},{1,0},{2,3},{3,2},{4,5},{5,4},{6,7},{7,6},{8,9},{9,8},{10,11... | collective-permute-start | bytes 1179656 | tf_op jit(solution)/shard_map/ppermute | solution.py:275
  41.7 1.9 collective-permute-start.1
  42.3 4.3 %collective-permute-start.6 = (f32[64,1536]{1,0:T(8,128)S(1)}, f32[64,1536]{1,0:T(8,128)S(1)}, u32[]{:S(2)}, u32[]{:S(2)}) collective-permute-start(f32[64,1536]{1,0:T(8,128)S(1)} %get-tuple-element.205), channel_id=1, source_target_pairs={{0,1},{1,0},{2,3},{3,2},{4,5},{5,4},{6,7},{7,6},{8,9},{9,8},{10,11... | collective-permute-start | bytes 1179656 | tf_op jit(solution)/shard_map/ppermute | solution.py:275
  43.6 7.5 %collective-permute-start.4 = (f32[64,1536]{1,0:T(8,128)S(1)}, f32[64,1536]{1,0:T(8,128)S(1)}, u32[]{:S(2)}, u32[]{:S(2)}) collective-permute-start(f32[64,1536]{1,0:T(8,128)S(1)} %get-tuple-element.207), channel_id=1, source_target_pairs={{0,1},{1,0},{2,3},{3,2},{4,5},{5,4},{6,7},{7,6},{8,9},{9,8},{10,11... | collective-permute-start | bytes 1179656 | tf_op jit(solution)/shard_map/ppermute | solution.py:275
  46.4 5.7 %collective-permute-start.9 = (f32[64,1536]{1,0:T(8,128)S(1)}, f32[64,1536]{1,0:T(8,128)S(1)}, u32[]{:S(2)}, u32[]{:S(2)}) collective-permute-start(f32[64,1536]{1,0:T(8,128)S(1)} %get-tuple-element.209), channel_id=1, source_target_pairs={{0,1},{1,0},{2,3},{3,2},{4,5},{5,4},{6,7},{7,6},{8,9},{9,8},{10,11... | collective-permute-start | bytes 1179656 | tf_op jit(solution)/shard_map/ppermute | solution.py:275
  46.6 6.4 %collective-permute-start.8 = (f32[64,1536]{1,0:T(8,128)S(1)}, f32[64,1536]{1,0:T(8,128)S(1)}, u32[]{:S(2)}, u32[]{:S(2)}) collective-permute-start(f32[64,1536]{1,0:T(8,128)S(1)} %add_select_fusion.15), channel_id=1, source_target_pairs={{2,4},{3,5},{4,2},{5,3},{0,1},{1,0},{6,7},{7,6},{10,12},{11,13},{1... | collective-permute-start | bytes 1179656 | tf_op jit(solution)/shard_map/ppermute | solution.py:308
  48.2 12.2 %collective-permute-start.10 = (f32[64,1536]{1,0:T(8,128)S(1)}, f32[64,1536]{1,0:T(8,128)S(1)}, u32[]{:S(2)}, u32[]{:S(2)}) collective-permute-start(f32[64,1536]{1,0:T(8,128)S(1)} %add.189), channel_id=1, source_target_pairs={{0,2},{1,3},{6,4},{7,5},{2,0},{3,1},{4,6},{5,7},{8,10},{9,11},{14,... | collective-permute-start | bytes 1179656 | tf_op jit(solution)/shard_map/ppermute | solution.py:308
  60.5 10.6 %collective-permute-start.11 = (f32[64,1536]{1,0:T(8,128)S(1)}, f32[64,1536]{1,0:T(8,128)S(1)}, u32[]{:S(2)}, u32[]{:S(2)}) collective-permute-start(f32[64,1536]{1,0:T(8,128)S(1)} %broadcast_select_fusion.13), channel_id=1, source_target_pairs={{0,2},{1,3},{6,4},{7,5},{2,0},{3,1},{4,6},{5,7},{8,10},{9,11},{14,... | collective-permute-start | bytes 1179656 | tf_op jit(solution)/shard_map/ppermute | solution.py:308
  62.3 9.0 %collective-permute-start.12 = (f32[64,1536]{1,0:T(8,128)S(1)}, f32[64,1536]{1,0:T(8,128)S(1)}, u32[]{:S(2)}, u32[]{:S(2)}) collective-permute-start(f32[64,1536]{1,0:T(8,128)S(1)} %add_select_fusion.13), channel_id=1, source_target_pairs={{2,4},{3,5},{4,2},{5,3},{0,1},{1,0},{6,7},{7,6},{10,12},{11,13},{1... | collective-permute-start | bytes 1179656 | tf_op jit(solution)/shard_map/ppermute | solution.py:308
  71.2 2.0 collective-permute-start.15
  71.5 11.6 %collective-permute-start.14 = (f32[64,1536]{1,0:T(8,128)S(1)}, f32[64,1536]{1,0:T(8,128)S(1)}, u32[]{:S(2)}, u32[]{:S(2)}) collective-permute-start(f32[64,1536]{1,0:T(8,128)S(1)} %broadcast_select_fusion.11), channel_id=1, source_target_pairs={{0,2},{1,3},{6,4},{7,5},{2,0},{3,1},{4,6},{5,7},{8,10},{9,11},{14,... | collective-permute-start | bytes 1179656 | tf_op jit(solution)/shard_map/ppermute | solution.py:308
  73.2 10.0 %collective-permute-start.13 = (f32[64,1536]{1,0:T(8,128)S(1)}, f32[64,1536]{1,0:T(8,128)S(1)}, u32[]{:S(2)}, u32[]{:S(2)}) collective-permute-start(f32[64,1536]{1,0:T(8,128)S(1)} %add_select_fusion.11), channel_id=1, source_target_pairs={{2,4},{3,5},{4,2},{5,3},{0,1},{1,0},{6,7},{7,6},{10,12},{11,13},{1... | collective-permute-start | bytes 1179656 | tf_op jit(solution)/shard_map/ppermute | solution.py:308
  83.1 3.5 %collective-permute-start.18 = (f32[64,1536]{1,0:T(8,128)S(1)}, f32[64,1536]{1,0:T(8,128)S(1)}, u32[]{:S(2)}, u32[]{:S(2)}) collective-permute-start(f32[64,1536]{1,0:T(8,128)S(1)} %broadcast_select_fusion.10.refs_3_), channel_id=1, source_target_pairs={{0,1},{1,0},{2,3},{3,2},{4,5},{5,4},{6,7},{7,6},{8,9},{9,8},{10,11... | collective-permute-start | bytes 1179656 | tf_op jit(solution)/shard_map/ppermute | solution.py:275
  84.9 12.5 %collective-permute-start.16 = (f32[64,1536]{1,0:T(8,128)}, f32[64,1536]{1,0:T(8,128)S(1)}, u32[]{:S(2)}, u32[]{:S(2)}) collective-permute-start(f32[64,1536]{1,0:T(8,128)} %broadcast_select_fusion.9), channel_id=1, source_target_pairs={{0,2},{1,3},{6,4},{7,5},{2,0},{3,1},{4,6},{5,7},{8,10},{9,11},{14,... | collective-permute-start | bytes 1179656 | tf_op jit(solution)/shard_map/ppermute | solution.py:308
  86.6 12.2 %collective-permute-start.17 = (f32[64,1536]{1,0:T(8,128)}, f32[64,1536]{1,0:T(8,128)S(1)}, u32[]{:S(2)}, u32[]{:S(2)}) collective-permute-start(f32[64,1536]{1,0:T(8,128)} %add_select_fusion.9), channel_id=1, source_target_pairs={{2,4},{3,5},{4,2},{5,3},{0,1},{1,0},{6,7},{7,6},{10,12},{11,13},{1... | collective-permute-start | bytes 1179656 | tf_op jit(solution)/shard_map/ppermute | solution.py:308
  98.2 6.3 %collective-permute-start.21 = (f32[64,1536]{1,0:T(8,128)S(1)}, f32[64,1536]{1,0:T(8,128)S(1)}, u32[]{:S(2)}, u32[]{:S(2)}) collective-permute-start(f32[64,1536]{1,0:T(8,128)S(1)} %broadcast_select_fusion.8.refs_1_), channel_id=1, source_target_pairs={{0,1},{1,0},{2,3},{3,2},{4,5},{5,4},{6,7},{7,6},{8,9},{9,8},{10,11... | collective-permute-start | bytes 1179656 | tf_op jit(solution)/shard_map/ppermute | solution.py:275
  101.0 13.3 %collective-permute-start.20 = (f32[64,1536]{1,0:T(8,128)S(1)}, f32[64,1536]{1,0:T(8,128)S(1)}, u32[]{:S(2)}, u32[]{:S(2)}) collective-permute-start(f32[64,1536]{1,0:T(8,128)S(1)} %broadcast_select_fusion.7), channel_id=1, source_target_pairs={{0,2},{1,3},{6,4},{7,5},{2,0},{3,1},{4,6},{5,7},{8,10},{9,11},{14,... | collective-permute-start | bytes 1179656 | tf_op jit(solution)/shard_map/ppermute | solution.py:308
  101.3 13.1 %collective-permute-start.19 = (f32[64,1536]{1,0:T(8,128)S(1)}, f32[64,1536]{1,0:T(8,128)S(1)}, u32[]{:S(2)}, u32[]{:S(2)}) collective-permute-start(f32[64,1536]{1,0:T(8,128)S(1)} %add_select_fusion.7), channel_id=1, source_target_pairs={{2,4},{3,5},{4,2},{5,3},{0,1},{1,0},{6,7},{7,6},{10,12},{11,13},{1... | collective-permute-start | bytes 1179656 | tf_op jit(solution)/shard_map/ppermute | solution.py:308
  101.5 20.0 %collective-permute-start.25 = (f32[128,1536]{1,0:T(8,128)}, f32[128,1536]{1,0:T(8,128)S(1)}, u32[]{:S(2)}, u32[]{:S(2)}) collective-permute-start(f32[128,1536]{1,0:T(8,128)} %get-tuple-element.261), channel_id=1, source_target_pairs={{0,8},{8,0},{16,24},{24,16},{1,9},{9,1},{17,25},{25,17},{2,10},{10... | collective-permute-start | bytes 2359304 | tf_op jit(solution)/shard_map/ppermute | solution.py:272
  103.0 19.7 %collective-permute-start.26 = (f32[128,1536]{1,0:T(8,128)}, f32[128,1536]{1,0:T(8,128)S(1)}, u32[]{:S(2)}, u32[]{:S(2)}) collective-permute-start(f32[128,1536]{1,0:T(8,128)} %get-tuple-element.262), channel_id=1, source_target_pairs={{0,16},{8,24},{16,0},{24,8},{1,17},{9,25},{17,1},{25,9},{2,18},{10... | collective-permute-start | bytes 2359304 | tf_op jit(solution)/shard_map/ppermute | solution.py:272
  114.3 4.1 %collective-permute-start.24 = (f32[64,1536]{1,0:T(8,128)S(1)}, f32[64,1536]{1,0:T(8,128)}, u32[]{:S(2)}, u32[]{:S(2)}) collective-permute-start(f32[64,1536]{1,0:T(8,128)S(1)} %broadcast_select_fusion.6.refs_3_), channel_id=1, source_target_pairs={{0,1},{1,0},{2,3},{3,2},{4,5},{5,4},{6,7},{7,6},{8,9},{9,8},{10,11... | collective-permute-start | bytes 1179656 | tf_op jit(solution)/shard_map/ppermute | solution.py:275
  116.2 18.5 %collective-permute-start.22 = (f32[64,1536]{1,0:T(8,128)}, f32[64,1536]{1,0:T(8,128)}, u32[]{:S(2)}, u32[]{:S(2)}) collective-permute-start(f32[64,1536]{1,0:T(8,128)} %broadcast_select_fusion.5), channel_id=1, source_target_pairs={{0,2},{1,3},{6,4},{7,5},{2,0},{3,1},{4,6},{5,7},{8,10},{9,11},{14,... | collective-permute-start | bytes 1179656 | tf_op jit(solution)/shard_map/ppermute | solution.py:308
  118.2 17.7 %collective-permute-start.23 = (f32[64,1536]{1,0:T(8,128)}, f32[64,1536]{1,0:T(8,128)S(1)}, u32[]{:S(2)}, u32[]{:S(2)}) collective-permute-start(f32[64,1536]{1,0:T(8,128)} %add_select_fusion.5), channel_id=1, source_target_pairs={{2,4},{3,5},{4,2},{5,3},{0,1},{1,0},{6,7},{7,6},{10,12},{11,13},{1... | collective-permute-start | bytes 1179656 | tf_op jit(solution)/shard_map/ppermute | solution.py:308
  122.7 18.9 %collective-permute-start.30 = (f32[128,1536]{1,0:T(8,128)}, f32[128,1536]{1,0:T(8,128)S(1)}, u32[]{:S(2)}, u32[]{:S(2)}) collective-permute-start(f32[128,1536]{1,0:T(8,128)} %copy-done.5), channel_id=1, source_target_pairs={{0,8},{8,0},{16,24},{24,16},{1,9},{9,1},{17,25},{25,17},{2,10},{10... | collective-permute-start | bytes 2359304 | tf_op jit(solution)/shard_map/ppermute | solution.py:272
  123.2 18.7 %collective-permute-start.29 = (f32[128,1536]{1,0:T(8,128)}, f32[128,1536]{1,0:T(8,128)S(1)}, u32[]{:S(2)}, u32[]{:S(2)}) collective-permute-start(f32[128,1536]{1,0:T(8,128)} %copy-done.4), channel_id=1, source_target_pairs={{0,16},{8,24},{16,0},{24,8},{1,17},{9,25},{17,1},{25,9},{2,18},{10... | collective-permute-start | bytes 2359304 | tf_op jit(solution)/shard_map/ppermute | solution.py:272
  135.8 2.0 collective-permute-start.31
  137.1 15.8 %collective-permute-start.28 = (f32[64,1536]{1,0:T(8,128)S(1)}, f32[64,1536]{1,0:T(8,128)S(1)}, u32[]{:S(2)}, u32[]{:S(2)}) collective-permute-start(f32[64,1536]{1,0:T(8,128)S(1)} %broadcast_select_fusion.3), channel_id=1, source_target_pairs={{0,2},{1,3},{6,4},{7,5},{2,0},{3,1},{4,6},{5,7},{8,10},{9,11},{14,... | collective-permute-start | bytes 1179656 | tf_op jit(solution)/shard_map/ppermute | solution.py:308
  137.6 15.4 %collective-permute-start.27 = (f32[64,1536]{1,0:T(8,128)S(1)}, f32[64,1536]{1,0:T(8,128)S(1)}, u32[]{:S(2)}, u32[]{:S(2)}) collective-permute-start(f32[64,1536]{1,0:T(8,128)S(1)} %add_select_fusion.3), channel_id=1, source_target_pairs={{2,4},{3,5},{4,2},{5,3},{0,1},{1,0},{6,7},{7,6},{10,12},{11,13},{1... | collective-permute-start | bytes 1179656 | tf_op jit(solution)/shard_map/ppermute | solution.py:308
  141.9 17.6 %collective-permute-start.34 = (f32[64,3072]{1,0:T(8,128)S(1)}, f32[64,3072]{1,0:T(8,128)S(1)}, u32[]{:S(2)}, u32[]{:S(2)}) collective-permute-start(f32[64,3072]{1,0:T(8,128)S(1)} %get-tuple-element.306), channel_id=1, source_target_pairs={{0,8},{8,0},{16,24},{24,16},{1,9},{9,1},{17,25},{25,17},{2,10},{10... | collective-permute-start | bytes 2359304 | tf_op jit(solution)/shard_map/ppermute | solution.py:272
  143.4 17.3 %collective-permute-start.35 = (f32[64,3072]{1,0:T(8,128)S(1)}, f32[64,3072]{1,0:T(8,128)S(1)}, u32[]{:S(2)}, u32[]{:S(2)}) collective-permute-start(f32[64,3072]{1,0:T(8,128)S(1)} %get-tuple-element.307), channel_id=1, source_target_pairs={{0,16},{8,24},{16,0},{24,8},{1,17},{9,25},{17,1},{25,9},{2,18},{10... | collective-permute-start | bytes 2359304 | tf_op jit(solution)/shard_map/ppermute | solution.py:272
  153.0 1.8 collective-permute-start.33
  153.1 18.4 %collective-permute-start.32 = (f32[64,1536]{1,0:T(8,128)S(1)}, f32[64,1536]{1,0:T(8,128)S(1)}, u32[]{:S(2)}, u32[]{:S(2)}) collective-permute-start(f32[64,1536]{1,0:T(8,128)S(1)} %add_select_fusion.2), channel_id=1, source_target_pairs={{0,2},{1,3},{6,4},{7,5},{2,0},{3,1},{4,6},{5,7},{8,10},{9,11},{14,... | collective-permute-start | bytes 1179656 | tf_op jit(solution)/shard_map/ppermute | solution.py:308
  154.1 17.6 %collective-permute-start.37 = (f32[64,1536]{1,0:T(8,128)S(1)}, f32[64,1536]{1,0:T(8,128)S(1)}, u32[]{:S(2)}, u32[]{:S(2)}) collective-permute-start(f32[64,1536]{1,0:T(8,128)S(1)} %add_select_fusion.1), channel_id=1, source_target_pairs={{2,4},{3,5},{4,2},{5,3},{0,1},{1,0},{6,7},{7,6},{10,12},{11,13},{1... | collective-permute-start | bytes 1179656 | tf_op jit(solution)/shard_map/ppermute | solution.py:308
  160.6 17.0 %collective-permute-start.39 = (f32[64,3072]{1,0:T(8,128)S(1)}, f32[64,3072]{1,0:T(8,128)S(1)}, u32[]{:S(2)}, u32[]{:S(2)}) collective-permute-start(f32[64,3072]{1,0:T(8,128)S(1)} %get-tuple-element.320), channel_id=1, source_target_pairs={{0,8},{8,0},{16,24},{24,16},{1,9},{9,1},{17,25},{25,17},{2,10},{10... | collective-permute-start | bytes 2359304 | tf_op jit(solution)/shard_map/ppermute | solution.py:272
  161.3 16.4 %collective-permute-start.40 = (f32[64,3072]{1,0:T(8,128)S(1)}, f32[64,3072]{1,0:T(8,128)S(1)}, u32[]{:S(2)}, u32[]{:S(2)}) collective-permute-start(f32[64,3072]{1,0:T(8,128)S(1)} %get-tuple-element.321), channel_id=1, source_target_pairs={{0,16},{8,24},{16,0},{24,8},{1,17},{9,25},{17,1},{25,9},{2,18},{10... | collective-permute-start | bytes 2359304 | tf_op jit(solution)/shard_map/ppermute | solution.py:272
  171.6 1.8 collective-permute-start.36
  171.8 17.4 %collective-permute-start.38 = (f32[64,1536]{1,0:T(8,128)S(1)}, f32[64,1536]{1,0:T(8,128)S(1)}, u32[]{:S(2)}, u32[]{:S(2)}) collective-permute-start(f32[64,1536]{1,0:T(8,128)S(1)} %add_select_fusion), channel_id=1, source_target_pairs={{0,2},{1,3},{6,4},{7,5},{2,0},{3,1},{4,6},{5,7},{8,10},{9,11},{14,... | collective-permute-start | bytes 1179656 | tf_op jit(solution)/shard_map/ppermute | solution.py:308
  177.7 22.2 %collective-permute-start.42 = (f32[64,3072]{1,0:T(8,128)S(1)}, f32[64,3072]{1,0:T(8,128)S(1)}, u32[]{:S(2)}, u32[]{:S(2)}) collective-permute-start(f32[64,3072]{1,0:T(8,128)S(1)} %get-tuple-element.338), channel_id=1, source_target_pairs={{0,8},{8,0},{16,24},{24,16},{1,9},{9,1},{17,25},{25,17},{2,10},{10... | collective-permute-start | bytes 2359304 | tf_op jit(solution)/shard_map/ppermute | solution.py:272
  179.4 20.5 %collective-permute-start.43 = (f32[64,3072]{1,0:T(8,128)S(1)}, f32[64,3072]{1,0:T(8,128)S(1)}, u32[]{:S(2)}, u32[]{:S(2)}) collective-permute-start(f32[64,3072]{1,0:T(8,128)S(1)} %get-tuple-element.339), channel_id=1, source_target_pairs={{0,16},{8,24},{16,0},{24,8},{1,17},{9,25},{17,1},{25,9},{2,18},{10... | collective-permute-start | bytes 2359304 | tf_op jit(solution)/shard_map/ppermute | solution.py:272
  199.9 21.9 %collective-permute-start.44 = (f32[64,3072]{1,0:T(8,128)S(1)}, f32[64,3072]{1,0:T(8,128)S(1)}, u32[]{:S(2)}, u32[]{:S(2)}) collective-permute-start(f32[64,3072]{1,0:T(8,128)S(1)} %get-tuple-element.355), channel_id=1, source_target_pairs={{0,8},{8,0},{16,24},{24,16},{1,9},{9,1},{17,25},{25,17},{2,10},{10... | collective-permute-start | bytes 2359304 | tf_op jit(solution)/shard_map/ppermute | solution.py:272
  200.5 21.3 %collective-permute-start.45 = (f32[64,3072]{1,0:T(8,128)S(1)}, f32[64,3072]{1,0:T(8,128)S(1)}, u32[]{:S(2)}, u32[]{:S(2)}) collective-permute-start(f32[64,3072]{1,0:T(8,128)S(1)} %get-tuple-element.356), channel_id=1, source_target_pairs={{0,16},{8,24},{16,0},{24,8},{1,17},{9,25},{17,1},{25,9},{2,18},{10... | collective-permute-start | bytes 2359304 | tf_op jit(solution)/shard_map/ppermute | solution.py:272
  203.8 16.6 %collective-permute-start.48 = (f32[64,128]{1,0:T(8,128)S(1)}, f32[64,128]{1,0:T(8,128)S(1)}, u32[]{:S(2)}, u32[]{:S(2)}) collective-permute-start(f32[64,128]{1,0:T(8,128)S(1)} %get-tuple-element.380), channel_id=1, source_target_pairs={{0,24},{8,16},{16,8},{24,0},{1,25},{9,17},{17,9},{25,1},{2,26},{10... | collective-permute-start | bytes 98312 | tf_op jit(solution)/shard_map/ppermute | solution.py:272
  206.8 14.4 %collective-permute-start.47 = (f32[64,128]{1,0:T(8,128)S(1)}, f32[64,128]{1,0:T(8,128)S(1)}, u32[]{:S(2)}, u32[]{:S(2)}) collective-permute-start(f32[64,128]{1,0:T(8,128)S(1)} %get-tuple-element.381), channel_id=1, source_target_pairs={{0,16},{8,24},{16,0},{24,8},{1,17},{9,25},{17,1},{25,9},{2,18},{10... | collective-permute-start | bytes 98312 | tf_op jit(solution)/shard_map/ppermute | solution.py:272
  207.0 14.2 %collective-permute-start.46 = (f32[64,128]{1,0:T(8,128)S(1)}, f32[64,128]{1,0:T(8,128)S(1)}, u32[]{:S(2)}, u32[]{:S(2)}) collective-permute-start(f32[64,128]{1,0:T(8,128)S(1)} %get-tuple-element.382), channel_id=1, source_target_pairs={{0,8},{8,0},{16,24},{24,16},{1,9},{9,1},{17,25},{25,17},{2,10},{10... | collective-permute-start | bytes 98312 | tf_op jit(solution)/shard_map/ppermute | solution.py:272
  (22 other events, 214.8 us)

commit v4 on v3

--- a/solution.py
+++ b/solution.py
@@ -507,12 +507,11 @@
         out = straight_panel(w_high, k, 1)
         if k == 0:
             advance(own_parts)
-        else:
-            finish(own_parts)
-            w_own, sum_own = gather(own_parts, stands[3])
-            own_sums += own_panel(0)
-        before = send_all(list(zip(out, straight)), before)
+        before = send_all(list(zip(out, straight)), before if k == 0 else low_arrived[-1])
         high_arrived.append(before)
+    finish(own_parts)
+    w_own, sum_own = gather(own_parts, stands[3])
+    own_sums += own_panel(0)
 
     local = run(
         lambda *x: small_product(x[:4], x[4:], stands),

time: 224 us -> 219 us (0.978)
  waiting for transfers between devices: 53.6 us -> 48.7 us
    ppermute x15, waiting for transfers between devices: 22.7 us -> 18.5 us  [send_pair(): return lax.ppermute(x, 'pair', perm)]
  transfers between devices with their start and end apart: 49 -> 49, of which waited for: 17 -> 15; matrix products, arithmetic and copies ran while one was open for 7% -> 7% of each run, Pallas kernels for 40% -> 41%
where the time goes in v4:
time: 219 us
  Pallas kernels  106 us (48%)
  waiting for transfers between devices  48.7 us (22%)
  starting transfers between devices  37.8 us (17%)
  other arithmetic  13.7 us (6%)
  local copies, waits for them, and re-layouts  9.18 us (4%)
  matrix products  2.26 us (1%)
    pallas_call x8, Pallas kernels, panel(): pl.pallas_call(kernel, out_shape=[jax.ShapeDtypeStruct((b - a, rho.shape[...  65 us
    pallas_call x2, Pallas kernels, project(): pl.pallas_call(kernel, out_shape=[jax.ShapeDtypeStruct((h, stop - start),...  29.9 us
    ppermute x18, waiting for transfers between devices, exchange(): return lax.ppermute(x, 'slab', perm)  26.1 us
    ppermute x15, waiting for transfers between devices, send_pair(): return lax.ppermute(x, 'pair', perm)  18.5 us
    ppermute x15, starting transfers between devices, send_pair(): return lax.ppermute(x, 'pair', perm)  18 us
    ppermute x18, starting transfers between devices, exchange(): return lax.ppermute(x, 'slab', perm)  16.6 us
    unnamed x42, local copies, waits for them, and re-layouts  9.06 us
    select_n x16, other arithmetic, receive(): self.total = run(lambda a, b: jnp.where(here, a + b, a), total, got)  6.49 us
  transfers between devices with their start and end apart: 49, of which 15 were waited for; matrix products, arithmetic and copies ran while one was open for 7% of the time, Pallas kernels for 41%

profile of v4, /device:TPU:0, one launch (start us, length us, event | category | flops | bytes accessed | tf_op | source)
XLA Modules:
  0.0 218.6 jit_solution(2225800514356059052)
XLA Ops:
  0.8 2.8 %copy-done = bf16[6144,512]{1,0:T(8,128)(2,1)S(1)} copy-done((bf16[6144,512]{1,0:T(8,128)(2,1)S(1)}, bf16[6144,512]{1,0:T(8,128)(2,1)}, u32[]{:S(2)}) %copy-start) | copy-done | bytes 6291480
  3.6 14.9 %shard_map.77 = (f32[64,1536]{1,0:T(8,128)S(1)}, f32[64,1536]{1,0:T(8,128)S(1)}, f32[64,1536]{1,0:T(8,128)S(1)}, f32[64,1536]{1,0:T(8,128)S(1)}, f32[64,1536]{1,...) custom-call(s32[5]{0:T(128)S(1)} %stack.107.where_ref, ...), custom_call_target="tpu_custom_call" | custom-call | flops 1000 | bytes 1000 | tf_op jit(solution)/shard_map/pallas_call | solution.py:103
  19.0 1.3 collective-permute-done
  20.4 3.0 %collective-permute-start.2 = (f32[64,1536]{1,0:T(8,128)S(1)}, f32[64,1536]{1,0:T(8,128)}, u32[]{:S(2)}, u32[]{:S(2)}) collective-permute-start(f32[64,1536]{1,0:T(8,128)S(1)} %add.187), channel_id=1, source_target_pairs={{0,2},{1,3},{6,4},{7,5},{2,0},{3,1},{4,6},{5,7},{8,10},{9,11},{14,... | collective-permute-start | bytes 1179656 | tf_op jit(solution)/shard_map/ppermute | solution.py:308
  24.0 2.8 %copy-done.1 = bf16[6144,512]{1,0:T(8,128)(2,1)S(1)} copy-done((bf16[6144,512]{1,0:T(8,128)(2,1)S(1)}, bf16[6144,512]{1,0:T(8,128)(2,1)}, u32[]{:S(2)}) %copy-start.1) | copy-done | bytes 6291480
  26.8 14.9 %shard_map.78 = (f32[64,1536]{1,0:T(8,128)S(1)}, f32[64,1536]{1,0:T(8,128)S(1)}, f32[64,1536]{1,0:T(8,128)S(1)}, f32[64,1536]{1,0:T(8,128)S(1)}, f32[64,1536]{1,...) custom-call(s32[5]{0:T(128)S(1)} %stack.107.where_ref, ...), custom_call_target="tpu_custom_call" | custom-call | flops 1000 | bytes 1000 | tf_op jit(solution)/shard_map/pallas_call | solution.py:103
  44.2 1.1 fusion.1
  45.3 1.1 fusion
  48.2 2.9 %collective-permute-start.10 = (f32[64,1536]{1,0:T(8,128)S(1)}, f32[64,1536]{1,0:T(8,128)S(1)}, u32[]{:S(2)}, u32[]{:S(2)}) collective-permute-start(f32[64,1536]{1,0:T(8,128)S(1)} %add.189), channel_id=1, source_target_pairs={{0,2},{1,3},{6,4},{7,5},{2,0},{3,1},{4,6},{5,7},{8,10},{9,11},{14,... | collective-permute-start | bytes 1179656 | tf_op jit(solution)/shard_map/ppermute | solution.py:308
  53.0 7.4 %collective-permute-done.10 = f32[64,1536]{1,0:T(8,128)S(1)} collective-permute-done((f32[64,1536]{1,0:T(8,128)S(1)}, f32[64,1536]{1,0:T(8,128)S(1)}, u32[]{:S(2)}, u32[]{:S(2)}) %collective-permute-start.10) | collective-permute-done | bytes 393248 | tf_op jit(solution)/shard_map/ppermute | solution.py:308
  60.5 1.8 collective-permute-start.11
  62.3 8.8 %collective-permute-done.11 = f32[64,1536]{1,0:T(8,128)S(1)} collective-permute-done((f32[64,1536]{1,0:T(8,128)S(1)}, f32[64,1536]{1,0:T(8,128)S(1)}, u32[]{:S(2)}, u32[]{:S(2)}) %collective-permute-start.11) | collective-permute-done | bytes 393248 | tf_op jit(solution)/shard_map/ppermute | solution.py:308
  71.5 1.7 collective-permute-start.14
  73.2 9.9 %collective-permute-done.14 = f32[64,1536]{1,0:T(8,128)S(1)} collective-permute-done((f32[64,1536]{1,0:T(8,128)S(1)}, f32[64,1536]{1,0:T(8,128)S(1)}, u32[]{:S(2)}, u32[]{:S(2)}) %collective-permute-start.14) | collective-permute-done | bytes 393248 | tf_op jit(solution)/shard_map/ppermute | solution.py:308
  84.9 1.6 collective-permute-start.16
  88.3 9.0 %shard_map.80 = (f32[128,1536]{1,0:T(8,128)}, f32[128,1536]{1,0:T(8,128)}) custom-call(bf16[128,3072]{1,0:T(8,128)(2,1)S(1)} %get-tuple-element.361.w_ref.refs_4_, bf16[3072,6144]{1,0:T(8,128)(2,1)} %rho_ref.19), custom_call_target="tpu_custom_call" | custom-call | flops 1000 | bytes 1000 | tf_op jit(solution)/shard_map/pallas_call | solution.py:154
  99.8 1.1 add_select_fusion.7
  101.5 1.5 collective-permute-start.25
  103.0 1.5 collective-permute-start.26
  104.5 7.9 %shard_map.81 = (f32[128,1536]{1,0:T(8,128)S(1)}, f32[128,1536]{1,0:T(8,128)S(1)}) custom-call(bf16[128,3072]{1,0:T(8,128)(2,1)S(1)} %get-tuple-element.361.w_ref.refs_4_, bf16[3072,6144]{1,0:T(8,128)(2,1)} %rho_ref.19), custom_call_target="tpu_custom_call" | custom-call | flops 1000 | bytes 1000 | tf_op jit(solution)/shard_map/pallas_call | solution.py:154
  116.2 2.0 collective-permute-start.22
  118.4 3.1 %collective-permute-done.25.refs_1_ = f32[128,1536]{1,0:T(8,128)S(1)} collective-permute-done((f32[128,1536]{1,0:T(8,128)}, f32[128,1536]{1,0:T(8,128)S(1)}, u32[]{:S(2)}, u32[]{:S(2)}) %collective-permute-start.25) | collective-permute-done | bytes 786464 | tf_op jit(solution)/shard_map/ppermute | solution.py:272
  121.5 1.2 collective-permute-done.26.refs_0_
  123.2 1.5 collective-permute-start.29
  124.8 1.8 shard_map.82
  126.6 8.0 %shard_map.83 = (f32[64,3072]{1,0:T(8,128)S(1)}, f32[64,3072]{1,0:T(8,128)S(1)}) custom-call(bf16[128,3072]{1,0:T(8,128)(2,1)S(1)} %get-tuple-element.362.w_ref.refs_5_, bf16[3072,6144]{1,0:T(8,128)(2,1)} %rho_ref.19, f32[128,1536]{1,0:T(8,128)S(1)} %collective-permute-done.26.refs_0_, f32[128,1536]{1,0:T(8,128)S(1)} %collective-permute-done.25.refs_1_), custom_call_target="tpu_custom_call" | custom-call | flops 1000 | bytes 1000 | tf_op jit(solution)/shard_map/pallas_call | solution.py:154
  134.7 1.1 broadcast_select_fusion.4.refs_1_
  136.0 1.1 add_select_fusion.3
  137.8 3.8 %collective-permute-done.30.refs_1_ = f32[128,1536]{1,0:T(8,128)S(1)} collective-permute-done((f32[128,1536]{1,0:T(8,128)}, f32[128,1536]{1,0:T(8,128)S(1)}, u32[]{:S(2)}, u32[]{:S(2)}) %collective-permute-start.30) | collective-permute-done | bytes 786464 | tf_op jit(solution)/shard_map/ppermute | solution.py:272
  141.9 1.4 collective-permute-start.34
  143.4 1.5 collective-permute-start.35
  144.9 8.0 %shard_map.84 = (f32[64,3072]{1,0:T(8,128)S(1)}, f32[64,3072]{1,0:T(8,128)S(1)}) custom-call(bf16[128,3072]{1,0:T(8,128)(2,1)S(1)} %get-tuple-element.362.w_ref.refs_5_, bf16[3072,6144]{1,0:T(8,128)(2,1)} %rho_ref.19, f32[128,1536]{1,0:T(8,128)S(1)} %collective-permute-done.29.refs_0_, f32[128,1536]{1,0:T(8,128)S(1)} %collective-permute-done.30.refs_1_), custom_call_target="tpu_custom_call" | custom-call | flops 1000 | bytes 1000 | tf_op jit(solution)/shard_map/pallas_call | solution.py:154
  154.8 4.8 %collective-permute-done.34.refs_1_ = f32[64,3072]{1,0:T(8,128)S(1)} collective-permute-done((f32[64,3072]{1,0:T(8,128)S(1)}, f32[64,3072]{1,0:T(8,128)S(1)}, u32[]{:S(2)}, u32[]{:S(2)}) %collective-permute-start.34) | collective-permute-done | bytes 786464 | tf_op jit(solution)/shard_map/ppermute | solution.py:272
  159.5 1.1 collective-permute-done.35.refs_2_
  161.3 1.5 collective-permute-start.40
  163.6 7.9 %shard_map.86 = (f32[64,3072]{1,0:T(8,128)S(1)}, f32[64,3072]{1,0:T(8,128)S(1)}) custom-call(bf16[128,3072]{1,0:T(8,128)(2,1)S(1)} %get-tuple-element.363.w_ref.refs_6_, bf16[3072,6144]{1,0:T(8,128)(2,1)} %rho_ref.19, f32[128,1536]{1,0:T(8,128)S(1)} %collective-permute-done.26.refs_0_, f32[128,1536]{1,0:T(8,128)S(1)} %collective-permute-done.25.refs_1_), custom_call_target="tpu_custom_call" | custom-call | flops 1000 | bytes 1000 | tf_op jit(solution)/shard_map/pallas_call | solution.py:154
  173.5 4.2 %collective-permute-done.39.refs_2_ = f32[64,3072]{1,0:T(8,128)S(1)} collective-permute-done((f32[64,3072]{1,0:T(8,128)S(1)}, f32[64,3072]{1,0:T(8,128)S(1)}, u32[]{:S(2)}, u32[]{:S(2)}) %collective-permute-start.39) | collective-permute-done | bytes 786464 | tf_op jit(solution)/shard_map/ppermute | solution.py:272
  177.6 1.7 collective-permute-start.42
  179.4 1.8 collective-permute-start.43
  181.2 8.0 %shard_map.87 = (f32[64,3072]{1,0:T(8,128)S(1)}, f32[64,3072]{1,0:T(8,128)S(1)}) custom-call(bf16[128,3072]{1,0:T(8,128)(2,1)S(1)} %get-tuple-element.363.w_ref.refs_6_, bf16[3072,6144]{1,0:T(8,128)(2,1)} %rho_ref.19, f32[128,1536]{1,0:T(8,128)S(1)} %collective-permute-done.29.refs_0_, f32[128,1536]{1,0:T(8,128)S(1)} %collective-permute-done.30.refs_1_), custom_call_target="tpu_custom_call" | custom-call | flops 1000 | bytes 1000 | tf_op jit(solution)/shard_map/pallas_call | solution.py:154
  190.0 1.1 collective-permute-done.41.refs_4_
  191.9 8.0 %shard_map.89.refs_0_ = f32[128,3072]{1,0:T(8,128)S(1)} custom-call(bf16[128,3072]{1,0:T(8,128)(2,1)S(1)} %get-tuple-element.365.w_ref.refs_7_, bf16[3072,6144]{1,0:T(8,128)(2,1)} %rho_ref.19), custom_call_target="tpu_custom_call" | custom-call | flops 1000 | bytes 1000 | tf_op jit(solution)/shard_map/pallas_call | solution.py:154
  199.9 3.3 %shard_map.90 = f32[64,512]{1,0:T(8,128)S(1)} custom-call(f32[64,3072]{1,0:T(8,128)S(1)} %copy-done.3, f32[64,3072]{1,0:T(8,128)S(1)} %get-tuple-element.358.refs_1_, f32[64,3072]{1,0:T(8,128)S(1)} %get-tuple-element.359.refs_2_, f32[64,3072]{1,0:T(8,128)S(1)} %get-tuple-element.360.refs_3_, bf16[128,3072]{1,0:T(8,128)(2,1)S(1)} %get-tuple-element.361.w_ref.refs_4_, ...), custom_call_target="tpu_custom_call" | custom-call | flops 1000 | bytes 1000 | tf_op jit(solution)/shard_map/pallas_call | solution.py:233
  203.2 1.9 collective-permute-start.48
  205.3 1.5 collective-permute-start.46
  206.8 8.0 %shard_map.91.refs_1_ = f32[128,3072]{1,0:T(8,128)S(1)} custom-call(bf16[128,3072]{1,0:T(8,128)(2,1)S(1)} %get-tuple-element.365.w_ref.refs_7_, bf16[3072,6144]{1,0:T(8,128)(2,1)} %rho_ref.19), custom_call_target="tpu_custom_call" | custom-call | flops 1000 | bytes 1000 | tf_op jit(solution)/shard_map/pallas_call | solution.py:154
  214.8 1.6 shard_map.92.refs_0_
  217.0 1.6 shard_map.93
  (161 shorter events, 27.5 us)
Async XLA Ops:
  18.5 1.9 collective-permute-start
  20.4 21.9 %collective-permute-start.2 = (f32[64,1536]{1,0:T(8,128)S(1)}, f32[64,1536]{1,0:T(8,128)}, u32[]{:S(2)}, u32[]{:S(2)}) collective-permute-start(f32[64,1536]{1,0:T(8,128)S(1)} %add.187), channel_id=1, source_target_pairs={{0,2},{1,3},{6,4},{7,5},{2,0},{3,1},{4,6},{5,7},{8,10},{9,11},{14,... | collective-permute-start | bytes 1179656 | tf_op jit(solution)/shard_map/ppermute | solution.py:308
  23.5 23.0 %collective-permute-start.7 = (f32[64,1536]{1,0:T(8,128)S(1)}, f32[64,1536]{1,0:T(8,128)}, u32[]{:S(2)}, u32[]{:S(2)}) collective-permute-start(f32[64,1536]{1,0:T(8,128)S(1)} %get-tuple-element.194), channel_id=1, source_target_pairs={{0,1},{1,0},{2,3},{3,2},{4,5},{5,4},{6,7},{7,6},{8,9},{9,8},{10,11... | collective-permute-start | bytes 1179656 | tf_op jit(solution)/shard_map/ppermute | solution.py:275
  23.5 24.7 %collective-permute-start.5 = (f32[64,1536]{1,0:T(8,128)S(1)}, f32[64,1536]{1,0:T(8,128)S(1)}, u32[]{:S(2)}, u32[]{:S(2)}) collective-permute-start(f32[64,1536]{1,0:T(8,128)S(1)} %get-tuple-element.196), channel_id=1, source_target_pairs={{0,1},{1,0},{2,3},{3,2},{4,5},{5,4},{6,7},{7,6},{8,9},{9,8},{10,11... | collective-permute-start | bytes 1179656 | tf_op jit(solution)/shard_map/ppermute | solution.py:275
  24.0 27.2 %collective-permute-start.3 = (f32[64,1536]{1,0:T(8,128)S(1)}, f32[64,1536]{1,0:T(8,128)S(1)}, u32[]{:S(2)}, u32[]{:S(2)}) collective-permute-start(f32[64,1536]{1,0:T(8,128)S(1)} %get-tuple-element.198), channel_id=1, source_target_pairs={{0,1},{1,0},{2,3},{3,2},{4,5},{5,4},{6,7},{7,6},{8,9},{9,8},{10,11... | collective-permute-start | bytes 1179656 | tf_op jit(solution)/shard_map/ppermute | solution.py:275
  41.7 1.9 collective-permute-start.1
  42.3 4.3 %collective-permute-start.6 = (f32[64,1536]{1,0:T(8,128)S(1)}, f32[64,1536]{1,0:T(8,128)S(1)}, u32[]{:S(2)}, u32[]{:S(2)}) collective-permute-start(f32[64,1536]{1,0:T(8,128)S(1)} %get-tuple-element.205), channel_id=1, source_target_pairs={{0,1},{1,0},{2,3},{3,2},{4,5},{5,4},{6,7},{7,6},{8,9},{9,8},{10,11... | collective-permute-start | bytes 1179656 | tf_op jit(solution)/shard_map/ppermute | solution.py:275
  43.6 7.5 %collective-permute-start.4 = (f32[64,1536]{1,0:T(8,128)S(1)}, f32[64,1536]{1,0:T(8,128)S(1)}, u32[]{:S(2)}, u32[]{:S(2)}) collective-permute-start(f32[64,1536]{1,0:T(8,128)S(1)} %get-tuple-element.207), channel_id=1, source_target_pairs={{0,1},{1,0},{2,3},{3,2},{4,5},{5,4},{6,7},{7,6},{8,9},{9,8},{10,11... | collective-permute-start | bytes 1179656 | tf_op jit(solution)/shard_map/ppermute | solution.py:275
  46.4 5.7 %collective-permute-start.9 = (f32[64,1536]{1,0:T(8,128)S(1)}, f32[64,1536]{1,0:T(8,128)S(1)}, u32[]{:S(2)}, u32[]{:S(2)}) collective-permute-start(f32[64,1536]{1,0:T(8,128)S(1)} %get-tuple-element.209), channel_id=1, source_target_pairs={{0,1},{1,0},{2,3},{3,2},{4,5},{5,4},{6,7},{7,6},{8,9},{9,8},{10,11... | collective-permute-start | bytes 1179656 | tf_op jit(solution)/shard_map/ppermute | solution.py:275
  46.6 6.4 %collective-permute-start.8 = (f32[64,1536]{1,0:T(8,128)S(1)}, f32[64,1536]{1,0:T(8,128)S(1)}, u32[]{:S(2)}, u32[]{:S(2)}) collective-permute-start(f32[64,1536]{1,0:T(8,128)S(1)} %add_select_fusion.15), channel_id=1, source_target_pairs={{2,4},{3,5},{4,2},{5,3},{0,1},{1,0},{6,7},{7,6},{10,12},{11,13},{1... | collective-permute-start | bytes 1179656 | tf_op jit(solution)/shard_map/ppermute | solution.py:308
  48.2 12.2 %collective-permute-start.10 = (f32[64,1536]{1,0:T(8,128)S(1)}, f32[64,1536]{1,0:T(8,128)S(1)}, u32[]{:S(2)}, u32[]{:S(2)}) collective-permute-start(f32[64,1536]{1,0:T(8,128)S(1)} %add.189), channel_id=1, source_target_pairs={{0,2},{1,3},{6,4},{7,5},{2,0},{3,1},{4,6},{5,7},{8,10},{9,11},{14,... | collective-permute-start | bytes 1179656 | tf_op jit(solution)/shard_map/ppermute | solution.py:308
  60.5 10.6 %collective-permute-start.11 = (f32[64,1536]{1,0:T(8,128)S(1)}, f32[64,1536]{1,0:T(8,128)S(1)}, u32[]{:S(2)}, u32[]{:S(2)}) collective-permute-start(f32[64,1536]{1,0:T(8,128)S(1)} %broadcast_select_fusion.13), channel_id=1, source_target_pairs={{0,2},{1,3},{6,4},{7,5},{2,0},{3,1},{4,6},{5,7},{8,10},{9,11},{14,... | collective-permute-start | bytes 1179656 | tf_op jit(solution)/shard_map/ppermute | solution.py:308
  62.3 9.0 %collective-permute-start.12 = (f32[64,1536]{1,0:T(8,128)S(1)}, f32[64,1536]{1,0:T(8,128)S(1)}, u32[]{:S(2)}, u32[]{:S(2)}) collective-permute-start(f32[64,1536]{1,0:T(8,128)S(1)} %add_select_fusion.13), channel_id=1, source_target_pairs={{2,4},{3,5},{4,2},{5,3},{0,1},{1,0},{6,7},{7,6},{10,12},{11,13},{1... | collective-permute-start | bytes 1179656 | tf_op jit(solution)/shard_map/ppermute | solution.py:308
  71.2 2.0 collective-permute-start.15
  71.5 11.6 %collective-permute-start.14 = (f32[64,1536]{1,0:T(8,128)S(1)}, f32[64,1536]{1,0:T(8,128)S(1)}, u32[]{:S(2)}, u32[]{:S(2)}) collective-permute-start(f32[64,1536]{1,0:T(8,128)S(1)} %broadcast_select_fusion.11), channel_id=1, source_target_pairs={{0,2},{1,3},{6,4},{7,5},{2,0},{3,1},{4,6},{5,7},{8,10},{9,11},{14,... | collective-permute-start | bytes 1179656 | tf_op jit(solution)/shard_map/ppermute | solution.py:308
  73.2 10.0 %collective-permute-start.13 = (f32[64,1536]{1,0:T(8,128)S(1)}, f32[64,1536]{1,0:T(8,128)S(1)}, u32[]{:S(2)}, u32[]{:S(2)}) collective-permute-start(f32[64,1536]{1,0:T(8,128)S(1)} %add_select_fusion.11), channel_id=1, source_target_pairs={{2,4},{3,5},{4,2},{5,3},{0,1},{1,0},{6,7},{7,6},{10,12},{11,13},{1... | collective-permute-start | bytes 1179656 | tf_op jit(solution)/shard_map/ppermute | solution.py:308
  83.1 3.5 %collective-permute-start.18 = (f32[64,1536]{1,0:T(8,128)S(1)}, f32[64,1536]{1,0:T(8,128)S(1)}, u32[]{:S(2)}, u32[]{:S(2)}) collective-permute-start(f32[64,1536]{1,0:T(8,128)S(1)} %broadcast_select_fusion.10.refs_3_), channel_id=1, source_target_pairs={{0,1},{1,0},{2,3},{3,2},{4,5},{5,4},{6,7},{7,6},{8,9},{9,8},{10,11... | collective-permute-start | bytes 1179656 | tf_op jit(solution)/shard_map/ppermute | solution.py:275
  84.9 12.5 %collective-permute-start.16 = (f32[64,1536]{1,0:T(8,128)}, f32[64,1536]{1,0:T(8,128)S(1)}, u32[]{:S(2)}, u32[]{:S(2)}) collective-permute-start(f32[64,1536]{1,0:T(8,128)} %broadcast_select_fusion.9), channel_id=1, source_target_pairs={{0,2},{1,3},{6,4},{7,5},{2,0},{3,1},{4,6},{5,7},{8,10},{9,11},{14,... | collective-permute-start | bytes 1179656 | tf_op jit(solution)/shard_map/ppermute | solution.py:308
  86.6 12.2 %collective-permute-start.17 = (f32[64,1536]{1,0:T(8,128)}, f32[64,1536]{1,0:T(8,128)S(1)}, u32[]{:S(2)}, u32[]{:S(2)}) collective-permute-start(f32[64,1536]{1,0:T(8,128)} %add_select_fusion.9), channel_id=1, source_target_pairs={{2,4},{3,5},{4,2},{5,3},{0,1},{1,0},{6,7},{7,6},{10,12},{11,13},{1... | collective-permute-start | bytes 1179656 | tf_op jit(solution)/shard_map/ppermute | solution.py:308
  98.2 6.3 %collective-permute-start.21 = (f32[64,1536]{1,0:T(8,128)S(1)}, f32[64,1536]{1,0:T(8,128)S(1)}, u32[]{:S(2)}, u32[]{:S(2)}) collective-permute-start(f32[64,1536]{1,0:T(8,128)S(1)} %broadcast_select_fusion.8.refs_1_), channel_id=1, source_target_pairs={{0,1},{1,0},{2,3},{3,2},{4,5},{5,4},{6,7},{7,6},{8,9},{9,8},{10,11... | collective-permute-start | bytes 1179656 | tf_op jit(solution)/shard_map/ppermute | solution.py:275
  101.0 13.3 %collective-permute-start.20 = (f32[64,1536]{1,0:T(8,128)S(1)}, f32[64,1536]{1,0:T(8,128)S(1)}, u32[]{:S(2)}, u32[]{:S(2)}) collective-permute-start(f32[64,1536]{1,0:T(8,128)S(1)} %broadcast_select_fusion.7), channel_id=1, source_target_pairs={{0,2},{1,3},{6,4},{7,5},{2,0},{3,1},{4,6},{5,7},{8,10},{9,11},{14,... | collective-permute-start | bytes 1179656 | tf_op jit(solution)/shard_map/ppermute | solution.py:308
  101.3 13.1 %collective-permute-start.19 = (f32[64,1536]{1,0:T(8,128)S(1)}, f32[64,1536]{1,0:T(8,128)S(1)}, u32[]{:S(2)}, u32[]{:S(2)}) collective-permute-start(f32[64,1536]{1,0:T(8,128)S(1)} %add_select_fusion.7), channel_id=1, source_target_pairs={{2,4},{3,5},{4,2},{5,3},{0,1},{1,0},{6,7},{7,6},{10,12},{11,13},{1... | collective-permute-start | bytes 1179656 | tf_op jit(solution)/shard_map/ppermute | solution.py:308
  101.5 20.0 %collective-permute-start.25 = (f32[128,1536]{1,0:T(8,128)}, f32[128,1536]{1,0:T(8,128)S(1)}, u32[]{:S(2)}, u32[]{:S(2)}) collective-permute-start(f32[128,1536]{1,0:T(8,128)} %get-tuple-element.261), channel_id=1, source_target_pairs={{0,8},{8,0},{16,24},{24,16},{1,9},{9,1},{17,25},{25,17},{2,10},{10... | collective-permute-start | bytes 2359304 | tf_op jit(solution)/shard_map/ppermute | solution.py:272
  103.0 19.7 %collective-permute-start.26 = (f32[128,1536]{1,0:T(8,128)}, f32[128,1536]{1,0:T(8,128)S(1)}, u32[]{:S(2)}, u32[]{:S(2)}) collective-permute-start(f32[128,1536]{1,0:T(8,128)} %get-tuple-element.262), channel_id=1, source_target_pairs={{0,16},{8,24},{16,0},{24,8},{1,17},{9,25},{17,1},{25,9},{2,18},{10... | collective-permute-start | bytes 2359304 | tf_op jit(solution)/shard_map/ppermute | solution.py:272
  114.3 4.1 %collective-permute-start.24 = (f32[64,1536]{1,0:T(8,128)S(1)}, f32[64,1536]{1,0:T(8,128)}, u32[]{:S(2)}, u32[]{:S(2)}) collective-permute-start(f32[64,1536]{1,0:T(8,128)S(1)} %broadcast_select_fusion.6.refs_3_), channel_id=1, source_target_pairs={{0,1},{1,0},{2,3},{3,2},{4,5},{5,4},{6,7},{7,6},{8,9},{9,8},{10,11... | collective-permute-start | bytes 1179656 | tf_op jit(solution)/shard_map/ppermute | solution.py:275
  116.2 18.5 %collective-permute-start.22 = (f32[64,1536]{1,0:T(8,128)}, f32[64,1536]{1,0:T(8,128)}, u32[]{:S(2)}, u32[]{:S(2)}) collective-permute-start(f32[64,1536]{1,0:T(8,128)} %broadcast_select_fusion.5), channel_id=1, source_target_pairs={{0,2},{1,3},{6,4},{7,5},{2,0},{3,1},{4,6},{5,7},{8,10},{9,11},{14,... | collective-permute-start | bytes 1179656 | tf_op jit(solution)/shard_map/ppermute | solution.py:308
  118.2 17.7 %collective-permute-start.23 = (f32[64,1536]{1,0:T(8,128)}, f32[64,1536]{1,0:T(8,128)S(1)}, u32[]{:S(2)}, u32[]{:S(2)}) collective-permute-start(f32[64,1536]{1,0:T(8,128)} %add_select_fusion.5), channel_id=1, source_target_pairs={{2,4},{3,5},{4,2},{5,3},{0,1},{1,0},{6,7},{7,6},{10,12},{11,13},{1... | collective-permute-start | bytes 1179656 | tf_op jit(solution)/shard_map/ppermute | solution.py:308
  122.7 18.9 %collective-permute-start.30 = (f32[128,1536]{1,0:T(8,128)}, f32[128,1536]{1,0:T(8,128)S(1)}, u32[]{:S(2)}, u32[]{:S(2)}) collective-permute-start(f32[128,1536]{1,0:T(8,128)} %copy-done.5), channel_id=1, source_target_pairs={{0,8},{8,0},{16,24},{24,16},{1,9},{9,1},{17,25},{25,17},{2,10},{10... | collective-permute-start | bytes 2359304 | tf_op jit(solution)/shard_map/ppermute | solution.py:272
  123.2 18.7 %collective-permute-start.29 = (f32[128,1536]{1,0:T(8,128)}, f32[128,1536]{1,0:T(8,128)S(1)}, u32[]{:S(2)}, u32[]{:S(2)}) collective-permute-start(f32[128,1536]{1,0:T(8,128)} %copy-done.4), channel_id=1, source_target_pairs={{0,16},{8,24},{16,0},{24,8},{1,17},{9,25},{17,1},{25,9},{2,18},{10... | collective-permute-start | bytes 2359304 | tf_op jit(solution)/shard_map/ppermute | solution.py:272
  135.8 2.0 collective-permute-start.31
  137.1 15.8 %collective-permute-start.28 = (f32[64,1536]{1,0:T(8,128)S(1)}, f32[64,1536]{1,0:T(8,128)S(1)}, u32[]{:S(2)}, u32[]{:S(2)}) collective-permute-start(f32[64,1536]{1,0:T(8,128)S(1)} %broadcast_select_fusion.3), channel_id=1, source_target_pairs={{0,2},{1,3},{6,4},{7,5},{2,0},{3,1},{4,6},{5,7},{8,10},{9,11},{14,... | collective-permute-start | bytes 1179656 | tf_op jit(solution)/shard_map/ppermute | solution.py:308
  137.6 15.4 %collective-permute-start.27 = (f32[64,1536]{1,0:T(8,128)S(1)}, f32[64,1536]{1,0:T(8,128)S(1)}, u32[]{:S(2)}, u32[]{:S(2)}) collective-permute-start(f32[64,1536]{1,0:T(8,128)S(1)} %add_select_fusion.3), channel_id=1, source_target_pairs={{2,4},{3,5},{4,2},{5,3},{0,1},{1,0},{6,7},{7,6},{10,12},{11,13},{1... | collective-permute-start | bytes 1179656 | tf_op jit(solution)/shard_map/ppermute | solution.py:308
  141.9 17.6 %collective-permute-start.34 = (f32[64,3072]{1,0:T(8,128)S(1)}, f32[64,3072]{1,0:T(8,128)S(1)}, u32[]{:S(2)}, u32[]{:S(2)}) collective-permute-start(f32[64,3072]{1,0:T(8,128)S(1)} %get-tuple-element.306), channel_id=1, source_target_pairs={{0,8},{8,0},{16,24},{24,16},{1,9},{9,1},{17,25},{25,17},{2,10},{10... | collective-permute-start | bytes 2359304 | tf_op jit(solution)/shard_map/ppermute | solution.py:272
  143.4 17.3 %collective-permute-start.35 = (f32[64,3072]{1,0:T(8,128)S(1)}, f32[64,3072]{1,0:T(8,128)S(1)}, u32[]{:S(2)}, u32[]{:S(2)}) collective-permute-start(f32[64,3072]{1,0:T(8,128)S(1)} %get-tuple-element.307), channel_id=1, source_target_pairs={{0,16},{8,24},{16,0},{24,8},{1,17},{9,25},{17,1},{25,9},{2,18},{10... | collective-permute-start | bytes 2359304 | tf_op jit(solution)/shard_map/ppermute | solution.py:272
  153.0 1.8 collective-permute-start.33
  153.1 18.5 %collective-permute-start.32 = (f32[64,1536]{1,0:T(8,128)S(1)}, f32[64,1536]{1,0:T(8,128)S(1)}, u32[]{:S(2)}, u32[]{:S(2)}) collective-permute-start(f32[64,1536]{1,0:T(8,128)S(1)} %add_select_fusion.2), channel_id=1, source_target_pairs={{0,2},{1,3},{6,4},{7,5},{2,0},{3,1},{4,6},{5,7},{8,10},{9,11},{14,... | collective-permute-start | bytes 1179656 | tf_op jit(solution)/shard_map/ppermute | solution.py:308
  154.1 17.6 %collective-permute-start.37 = (f32[64,1536]{1,0:T(8,128)S(1)}, f32[64,1536]{1,0:T(8,128)S(1)}, u32[]{:S(2)}, u32[]{:S(2)}) collective-permute-start(f32[64,1536]{1,0:T(8,128)S(1)} %add_select_fusion.1), channel_id=1, source_target_pairs={{2,4},{3,5},{4,2},{5,3},{0,1},{1,0},{6,7},{7,6},{10,12},{11,13},{1... | collective-permute-start | bytes 1179656 | tf_op jit(solution)/shard_map/ppermute | solution.py:308
  160.6 17.0 %collective-permute-start.39 = (f32[64,3072]{1,0:T(8,128)S(1)}, f32[64,3072]{1,0:T(8,128)S(1)}, u32[]{:S(2)}, u32[]{:S(2)}) collective-permute-start(f32[64,3072]{1,0:T(8,128)S(1)} %get-tuple-element.320), channel_id=1, source_target_pairs={{0,8},{8,0},{16,24},{24,16},{1,9},{9,1},{17,25},{25,17},{2,10},{10... | collective-permute-start | bytes 2359304 | tf_op jit(solution)/shard_map/ppermute | solution.py:272
  161.3 16.3 %collective-permute-start.40 = (f32[64,3072]{1,0:T(8,128)S(1)}, f32[64,3072]{1,0:T(8,128)S(1)}, u32[]{:S(2)}, u32[]{:S(2)}) collective-permute-start(f32[64,3072]{1,0:T(8,128)S(1)} %get-tuple-element.321), channel_id=1, source_target_pairs={{0,16},{8,24},{16,0},{24,8},{1,17},{9,25},{17,1},{25,9},{2,18},{10... | collective-permute-start | bytes 2359304 | tf_op jit(solution)/shard_map/ppermute | solution.py:272
  171.7 1.8 collective-permute-start.36
  171.8 17.4 %collective-permute-start.38 = (f32[64,1536]{1,0:T(8,128)S(1)}, f32[64,1536]{1,0:T(8,128)S(1)}, u32[]{:S(2)}, u32[]{:S(2)}) collective-permute-start(f32[64,1536]{1,0:T(8,128)S(1)} %add_select_fusion), channel_id=1, source_target_pairs={{0,2},{1,3},{6,4},{7,5},{2,0},{3,1},{4,6},{5,7},{8,10},{9,11},{14,... | collective-permute-start | bytes 1179656 | tf_op jit(solution)/shard_map/ppermute | solution.py:308
  177.6 27.5 %collective-permute-start.42 = (f32[64,3072]{1,0:T(8,128)S(1)}, f32[64,3072]{1,0:T(8,128)S(1)}, u32[]{:S(2)}, u32[]{:S(2)}) collective-permute-start(f32[64,3072]{1,0:T(8,128)S(1)} %get-tuple-element.338), channel_id=1, source_target_pairs={{0,8},{8,0},{16,24},{24,16},{1,9},{9,1},{17,25},{25,17},{2,10},{10... | collective-permute-start | bytes 2359304 | tf_op jit(solution)/shard_map/ppermute | solution.py:272
  179.4 25.9 %collective-permute-start.43 = (f32[64,3072]{1,0:T(8,128)S(1)}, f32[64,3072]{1,0:T(8,128)S(1)}, u32[]{:S(2)}, u32[]{:S(2)}) collective-permute-start(f32[64,3072]{1,0:T(8,128)S(1)} %get-tuple-element.339), channel_id=1, source_target_pairs={{0,16},{8,24},{16,0},{24,8},{1,17},{9,25},{17,1},{25,9},{2,18},{10... | collective-permute-start | bytes 2359304 | tf_op jit(solution)/shard_map/ppermute | solution.py:272
  189.4 27.7 %collective-permute-start.44 = (f32[64,3072]{1,0:T(8,128)S(1)}, f32[64,3072]{1,0:T(8,128)S(1)}, u32[]{:S(2)}, u32[]{:S(2)}) collective-permute-start(f32[64,3072]{1,0:T(8,128)S(1)} %get-tuple-element.345), channel_id=1, source_target_pairs={{0,8},{8,0},{16,24},{24,16},{1,9},{9,1},{17,25},{25,17},{2,10},{10... | collective-permute-start | bytes 2359304 | tf_op jit(solution)/shard_map/ppermute | solution.py:272
  190.0 27.1 %collective-permute-start.45 = (f32[64,3072]{1,0:T(8,128)S(1)}, f32[64,3072]{1,0:T(8,128)S(1)}, u32[]{:S(2)}, u32[]{:S(2)}) collective-permute-start(f32[64,3072]{1,0:T(8,128)S(1)} %get-tuple-element.346), channel_id=1, source_target_pairs={{0,16},{8,24},{16,0},{24,8},{1,17},{9,25},{17,1},{25,9},{2,18},{10... | collective-permute-start | bytes 2359304 | tf_op jit(solution)/shard_map/ppermute | solution.py:272
  203.2 13.2 %collective-permute-start.48 = (f32[64,128]{1,0:T(8,128)S(1)}, f32[64,128]{1,0:T(8,128)S(1)}, u32[]{:S(2)}, u32[]{:S(2)}) collective-permute-start(f32[64,128]{1,0:T(8,128)S(1)} %get-tuple-element.380), channel_id=1, source_target_pairs={{0,24},{8,16},{16,8},{24,0},{1,25},{9,17},{17,9},{25,1},{2,26},{10... | collective-permute-start | bytes 98312 | tf_op jit(solution)/shard_map/ppermute | solution.py:272
  205.1 11.3 %collective-permute-start.47 = (f32[64,128]{1,0:T(8,128)S(1)}, f32[64,128]{1,0:T(8,128)S(1)}, u32[]{:S(2)}, u32[]{:S(2)}) collective-permute-start(f32[64,128]{1,0:T(8,128)S(1)} %get-tuple-element.381), channel_id=1, source_target_pairs={{0,16},{8,24},{16,0},{24,8},{1,17},{9,25},{17,1},{25,9},{2,18},{10... | collective-permute-start | bytes 98312 | tf_op jit(solution)/shard_map/ppermute | solution.py:272
  205.3 11.1 %collective-permute-start.46 = (f32[64,128]{1,0:T(8,128)S(1)}, f32[64,128]{1,0:T(8,128)S(1)}, u32[]{:S(2)}, u32[]{:S(2)}) collective-permute-start(f32[64,128]{1,0:T(8,128)S(1)} %get-tuple-element.382), channel_id=1, source_target_pairs={{0,8},{8,0},{16,24},{24,16},{1,9},{9,1},{17,25},{25,17},{2,10},{10... | collective-permute-start | bytes 98312 | tf_op jit(solution)/shard_map/ppermute | solution.py:272
  (22 other events, 214.1 us)
